TPU v7x, 32 devices: a whole 2x2x4 slice. The times are simulated.
32 devices in a mesh: row: 8 (over z, y), col: 4 (over x, core).
Axes of the slice: x: 2, y: 2, z: 4, core: 2. Of those that a mesh axis runs over, the one named last changes fastest.
Arguments:
- factor: float32 [8, 12, 1024, 4, 1024], P('row', None, None, None, 'col'), may hold values from -0.01953125 to 0.01953125
- knowns: float32 [8, 12, 1024, 256], P('row'), may hold values from -6 to 6
- inverse: float32 [4, 1024, 1024], P(None, None, 'col'), may hold values from -0.1875 to 0.1875
Outputs:
- solved: float32 [4, 1024, 256], P(None, 'col', 'row')
All inputs are finite; a program needn't handle non-finite values.
Results may differ from a plain program's by a relative error of at most 0.0001.
Values sent between devices are 32-bit elements; how exact they have to be, the bound alone decides.
No kernel may reach another device: no remote copies, remote signals or barrier semaphores. Data moves between devices by JAX's collectives and lax.ppermute only.
A program may use at most 128 MiB of HBM per device.

v0:
```python
import jax
import jax.numpy as jnp
from jax import lax
from jax.sharding import PartitionSpec as P

NBLK = 96
KW = 4


def from_behind(block, axis, distance):
    devices = range(lax.axis_size(axis))
    route = [((i - distance) % len(devices), i) for i in devices]
    return lax.ppermute(block, axis, route)


def apply_inverse(residual, inverse_block):
    full_resid = lax.all_gather(residual, "col", axis=0, tiled=True)
    return jnp.einsum(
        "cm,cs->ms",
        inverse_block,
        full_resid,
        precision=lax.Precision.HIGHEST,
        preferred_element_type=jnp.float32,
    )


def spread_block(own_factor, local_slot, solved_part):
    rows_block = own_factor[local_slot]
    return jnp.einsum(
        "ajc,as->jcs",
        rows_block,
        lax.all_gather(solved_part, "col", axis=0, tiled=True),
        precision=lax.Precision.HIGHEST,
        preferred_element_type=jnp.float32,
    )


def on_device(factor, knowns, inverse):
    row_count = lax.axis_size("row")
    row_index = lax.axis_index("row")
    col_index = lax.axis_index("col")
    slice_width = factor.shape[4]
    first_block = NBLK - KW
    own_factor = factor[0]
    own_knowns = knowns[0]
    counted = lax.iota(jnp.int32, own_knowns.shape[0]) * row_count + row_index
    keep_mask = (counted < first_block).astype(jnp.float32)
    prefix = jnp.einsum(
        "lajc,las->jcs",
        own_factor,
        own_knowns * keep_mask[:, None, None],
        precision=lax.Precision.HIGHEST,
        preferred_element_type=jnp.float32,
    )
    owned_rhs = []
    for step in range(KW):
        block_id = first_block + step
        rhs_slice = lax.dynamic_slice_in_dim(
            own_knowns[block_id // row_count], col_index * slice_width, slice_width, 0
        )
        owner_mask = (row_index == block_id % row_count).astype(jnp.float32)
        owned_rhs.append(owner_mask * rhs_slice)
    local_terms = prefix - jnp.stack(owned_rhs)
    solved_parts = []
    totals = lax.psum(local_terms, "row")
    corrections = [totals[step] for step in range(KW)]
    for step in range(KW):
        block_id = first_block + step
        residual = -corrections[step]
        solved_part = apply_inverse(residual, inverse[step])
        owner_mask = (row_index == block_id % row_count).astype(jnp.float32)
        solved_parts.append(owner_mask * solved_part)
        if step + 1 < KW:
            contrib = spread_block(own_factor, block_id // row_count, solved_part)
            for later in range(step + 1, KW):
                arrived = from_behind(contrib[later], "row", later - step)
                corrections[later] = corrections[later] + arrived
    return lax.psum_scatter(jnp.stack(solved_parts), "row", scatter_dimension=2, tiled=True)


def solution(mesh):
    return jax.shard_map(
        on_device,
        mesh=mesh,
        in_specs=(
            P("row", None, None, None, "col"),
            P("row", None, None, None),
            P(None, None, "col"),
        ),
        out_specs=P(None, "col", "row"),
        check_vma=False,
    )
```

profile of v0, /device:TPU:0, one launch (start us, length us, event | category | flops | bytes accessed | tf_op | source)
XLA Modules:
  0.0 400.9 jit_solution(3865972509091201270)
XLA Ops:
  6.5 1.3 slice.55
  7.9 0.1 copy.12
  8.0 0.1 multiply_bitcast_fusion.6
  8.1 61.7 %maximum_subtract_fusion = f32[4,256,256]{1,2,0:T(8,128)} fusion(f32[1,256,256]{1,2,0:T(8,128)S(1)} %get-tuple-element.11, f32[1,256,256]{1,2,0:T(8,128)S(1)} %get-tuple-element.12, f32[1,256,256]{1,2,0:T(8,128)S(1)} %get-tuple-element.13, f32[1,256,256]{1,2,0:T(8,128)S(1)} %get-tuple-element.10, f32[12,1024,4,256]{3,2,1,0:T(4,128)} %bitcast.128, ...), kind=kOutput, calls=%fused_computation.18 | convolution fusion | flops 38658899968 | bytes 65011760 | tf_op jit(solution)/shard_map/lajc,las->jcs/dot_general | solution.py:48
  69.8 0.0 all-gather.21.cloned.1.call-start
  69.8 80.8 %all-reduce.2.cloned.1.call-done = f32[4,256,256]{1,2,0:T(8,128)} async-done(((f32[4,256,256]{1,2,0:T(8,128)}), f32[4,256,256]{1,2,0:T(8,128)}) %all-reduce.2.cloned.1.call-update) | async-done | bytes 1048592 | tf_op jit(solution)/shard_map/psum | solution.py:65
  150.6 1.7 slice_negate_fusion
  152.3 0.0 all-gather.21.cloned.1.call-update
  152.3 0.0 all-gather.9.cloned.1.call-start
  152.4 16.4 %all-gather.21.cloned.1.call-done = f32[1,1024,256]{1,2,0:T(8,128)} async-done(((f32[1,256,256]{1,2,0:T(8,128)}), f32[1,1024,256]{1,2,0:T(8,128)}) %all-gather.21.cloned.1.call-update) | async-done | bytes 1048592 | tf_op jit(solution)/shard_map/all_gather | solution.py:17
  168.8 3.3 convolution_bitcast_fusion.2
  172.1 0.2 all-gather.11.cloned.1.call-start
  172.3 4.9 %slice.59 = f32[1,1,1024,4,256]{4,3,2,1,0:T(4,128)} slice(f32[1,12,1024,4,256]{4,3,2,1,0:T(4,128)} %param.3), slice={[0:1], [11:12], [0:1024], [0:4], [0:256]} | slice | bytes 8388608 | tf_op jit(solution)/shard_map/slice | solution.py:28
  177.2 11.8 %all-gather.9.cloned.1.call-done = f32[1024,256]{0,1:T(8,128)} async-done(((f32[256,256]{0,1:T(8,128)}), f32[1024,256]{0,1:T(8,128)}) %all-gather.9.cloned.1.call-update) | async-done | bytes 1048592 | tf_op jit(solution)/shard_map/all_gather | solution.py:32
  189.0 6.3 %fusion.7 = f32[4,256,256]{1,2,0:T(8,128)S(1)} fusion(f32[1,1,1024,4,256]{4,3,2,1,0:T(4,128)} %slice.59, f32[1024,256]{0,1:T(8,128)} %all-gather.9.cloned.1.call-done), kind=kOutput, calls=%fused_computation.9 | convolution fusion | flops 3221225472 | bytes 6291456 | tf_op jit(solution)/shard_map/ajc,as->jcs/dot_general | solution.py:29
  195.3 0.1 slice_bitcast_fusion.2
  195.3 1.5 collective-permute-start
  196.9 9.7 %collective-permute-done = f32[256,256]{0,1:T(8,128)S(1)} collective-permute-done((f32[256,256]{0,1:T(8,128)S(1)}, f32[256,256]{0,1:T(8,128)S(1)}, u32[]{:S(2)}, u32[]{:S(2)}) %collective-permute-start) | collective-permute-done | bytes 262176 | tf_op jit(solution)/shard_map/ppermute | solution.py:13
  206.5 0.7 fusion.40
  207.3 0.0 all-gather.11.cloned.1.call-update
  207.3 0.0 all-gather.13.cloned.1.call-start
  207.3 14.1 %all-gather.11.cloned.1.call-done = f32[1024,256]{0,1:T(8,128)} async-done(((f32[256,256]{0,1:T(8,128)}), f32[1024,256]{0,1:T(8,128)}) %all-gather.11.cloned.1.call-update) | async-done | bytes 1048592 | tf_op jit(solution)/shard_map/all_gather | solution.py:17
  221.5 3.3 convolution_bitcast_fusion.1
  224.8 0.0 all-gather.15.cloned.1.call-start
  224.8 1.5 collective-permute-start.1
  226.4 15.3 %all-gather.13.cloned.1.call-done = f32[1024,256]{0,1:T(8,128)} async-done(((f32[256,256]{0,1:T(8,128)}), f32[1024,256]{0,1:T(8,128)}) %all-gather.13.cloned.1.call-update) | async-done | bytes 1048592 | tf_op jit(solution)/shard_map/all_gather | solution.py:32
  241.7 6.3 %fusion.8 = f32[4,256,256]{1,2,0:T(8,128)S(1)} fusion(f32[1,1,1024,4,256]{4,3,2,1,0:T(4,128)} %slice.59, f32[1024,256]{0,1:T(8,128)} %all-gather.13.cloned.1.call-done), kind=kOutput, calls=%fused_computation.10 | convolution fusion | flops 3221225472 | bytes 6291456 | tf_op jit(solution)/shard_map/ajc,as->jcs/dot_general | solution.py:29
  248.0 1.5 collective-permute-start.2
  249.5 9.7 %collective-permute-done.2 = f32[256,256]{0,1:T(8,128)S(1)} collective-permute-done((f32[256,256]{0,1:T(8,128)S(1)}, f32[256,256]{0,1:T(8,128)S(1)}, u32[]{:S(2)}, u32[]{:S(2)}) %collective-permute-start.2) | collective-permute-done | bytes 262176 | tf_op jit(solution)/shard_map/ppermute | solution.py:13
  259.2 0.8 fusion.38
  260.0 0.0 all-gather.17.cloned.1.call-start
  260.0 14.1 %all-gather.15.cloned.1.call-done = f32[1024,256]{0,1:T(8,128)} async-done(((f32[256,256]{0,1:T(8,128)}), f32[1024,256]{0,1:T(8,128)}) %all-gather.15.cloned.1.call-update) | async-done | bytes 1048592 | tf_op jit(solution)/shard_map/all_gather | solution.py:17
  274.2 3.3 convolution_bitcast_fusion
  277.4 0.0 all-gather.17.cloned.1.call-update
  277.5 0.0 all-gather.19.cloned.1.call-start
  277.5 2.4 collective-permute-start.3
  280.0 1.5 collective-permute-start.4
  281.4 12.9 %all-gather.17.cloned.1.call-done = f32[1024,256]{0,1:T(8,128)} async-done(((f32[256,256]{0,1:T(8,128)}), f32[1024,256]{0,1:T(8,128)}) %all-gather.17.cloned.1.call-update) | async-done | bytes 1048592 | tf_op jit(solution)/shard_map/all_gather | solution.py:32
  294.3 6.3 %fusion.9 = f32[4,256,256]{1,2,0:T(8,128)S(1)} fusion(f32[1,1,1024,4,256]{4,3,2,1,0:T(4,128)} %slice.59, f32[1024,256]{0,1:T(8,128)} %all-gather.17.cloned.1.call-done), kind=kOutput, calls=%fused_computation.11 | convolution fusion | flops 3221225472 | bytes 6291456 | tf_op jit(solution)/shard_map/ajc,as->jcs/dot_general | solution.py:29
  300.6 1.5 collective-permute-start.5
  302.2 9.7 %collective-permute-done.5 = f32[256,256]{0,1:T(8,128)S(1)} collective-permute-done((f32[256,256]{0,1:T(8,128)S(1)}, f32[256,256]{0,1:T(8,128)S(1)}, u32[]{:S(2)}, u32[]{:S(2)}) %collective-permute-start.5) | collective-permute-done | bytes 262176 | tf_op jit(solution)/shard_map/ppermute | solution.py:13
  311.8 0.8 fusion.35
  312.6 0.0 reduce-scatter.2.cloned.1.call-start
  312.8 14.0 %all-gather.19.cloned.1.call-done = f32[1024,256]{0,1:T(8,128)} async-done(((f32[256,256]{0,1:T(8,128)}), f32[1024,256]{0,1:T(8,128)}) %all-gather.19.cloned.1.call-update) | async-done | bytes 1048592 | tf_op jit(solution)/shard_map/all_gather | solution.py:17
  326.8 2.6 fusion.15
  329.4 1.1 pad_maximum_fusion
  330.5 0.0 reduce-scatter.2.cloned.1.call-update
  330.5 63.9 %reduce-scatter.2.cloned.1.call-done = f32[4,256,32]{1,2,0:T(8,128)} async-done(((f32[4,256,256]{1,2,0:T(8,128)}), f32[4,256,32]{1,2,0:T(8,128)}) %reduce-scatter.2.cloned.1.call-update) | async-done | bytes 131088 | tf_op jit(solution)/shard_map/reduce_scatter | solution.py:78
  (24 shorter events, 0.3 us)
Async XLA Ops:
  6.5 144.1 %all-reduce.2.cloned.1.call-start = ((), (), s32[]{:S(2)}) async-start(), calls=%async_computation.1 | async-start | bytes 2097152 | tf_op jit(solution)/shard_map/psum | solution.py:65
  69.8 99.0 %all-gather.21.cloned.1.call-start = ((), (), s32[]{:S(2)}) async-start(), calls=%async_computation.9 | async-start | bytes 1310720 | tf_op jit(solution)/shard_map/all_gather | solution.py:17
  152.3 36.7 %all-gather.9.cloned.1.call-start = ((), (), s32[]{:S(2)}) async-start(), calls=%async_computation.2 | async-start | bytes 1310720 | tf_op jit(solution)/shard_map/all_gather | solution.py:32
  172.1 49.4 %all-gather.11.cloned.1.call-start = ((), (), s32[]{:S(2)}) async-start(), calls=%async_computation.3 | async-start | bytes 1310720 | tf_op jit(solution)/shard_map/all_gather | solution.py:17
  177.2 29.3 %copy-start.3 = (f32[4,256,256]{1,2,0:T(8,128)S(1)}, f32[4,256,256]{1,2,0:T(8,128)}, u32[]{:S(2)}) copy-start(f32[4,256,256]{1,2,0:T(8,128)} %all-reduce.2.cloned.1.call-done) | copy-start | bytes 3145732
  195.3 11.2 %collective-permute-start = (f32[256,256]{0,1:T(8,128)S(1)}, f32[256,256]{0,1:T(8,128)S(1)}, u32[]{:S(2)}, u32[]{:S(2)}) collective-permute-start(f32[256,256]{0,1:T(8,128)S(1)} %get-tuple-element.7), channel_id=1, source_target_pairs={{28,0},{0,4},{4,8},{8,12},{12,16},{16,20},{20,24},{24,28},{29,1},{... | collective-permute-start | bytes 786440 | tf_op jit(solution)/shard_map/ppermute | solution.py:13
  207.3 34.4 %all-gather.13.cloned.1.call-start = ((), (), s32[]{:S(2)}) async-start(), calls=%async_computation.4 | async-start | bytes 1310720 | tf_op jit(solution)/shard_map/all_gather | solution.py:32
  224.8 49.4 %all-gather.15.cloned.1.call-start = ((), (), s32[]{:S(2)}) async-start(), calls=%async_computation.5 | async-start | bytes 1310720 | tf_op jit(solution)/shard_map/all_gather | solution.py:17
  224.8 24.7 %collective-permute-start.1 = (f32[256,256]{0,1:T(8,128)S(1)}, f32[256,256]{0,1:T(8,128)S(1)}, u32[]{:S(2)}, u32[]{:S(2)}) collective-permute-start(f32[256,256]{0,1:T(8,128)S(1)} %get-tuple-element.6), channel_id=1, source_target_pairs={{24,0},{28,4},{0,8},{4,12},{8,16},{12,20},{16,24},{20,28},{25,1},{... | collective-permute-start | bytes 786440 | tf_op jit(solution)/shard_map/ppermute | solution.py:13
  248.0 11.2 %collective-permute-start.2 = (f32[256,256]{0,1:T(8,128)S(1)}, f32[256,256]{0,1:T(8,128)S(1)}, u32[]{:S(2)}, u32[]{:S(2)}) collective-permute-start(f32[256,256]{0,1:T(8,128)S(1)} %get-tuple-element.9), channel_id=1, source_target_pairs={{28,0},{0,4},{4,8},{8,12},{12,16},{16,20},{20,24},{24,28},{29,1},{... | collective-permute-start | bytes 786440 | tf_op jit(solution)/shard_map/ppermute | solution.py:13
  260.0 34.4 %all-gather.17.cloned.1.call-start = ((), (), s32[]{:S(2)}) async-start(), calls=%async_computation.6 | async-start | bytes 1310720 | tf_op jit(solution)/shard_map/all_gather | solution.py:32
  277.5 49.4 %all-gather.19.cloned.1.call-start = ((), (), s32[]{:S(2)}) async-start(), calls=%async_computation.7 | async-start | bytes 1310720 | tf_op jit(solution)/shard_map/all_gather | solution.py:17
  277.5 24.7 %collective-permute-start.3 = (f32[256,256]{0,1:T(8,128)S(1)}, f32[256,256]{0,1:T(8,128)S(1)}, u32[]{:S(2)}, u32[]{:S(2)}) collective-permute-start(f32[256,256]{0,1:T(8,128)S(1)} %get-tuple-element.5), channel_id=1, source_target_pairs={{20,0},{24,4},{28,8},{0,12},{4,16},{8,20},{12,24},{16,28},{21,1},{... | collective-permute-start | bytes 786440 | tf_op jit(solution)/shard_map/ppermute | solution.py:13
  280.0 32.7 %copy-start = (f32[256,256]{0,1:T(8,128)S(1)}, f32[256,256]{0,1:T(8,128)}, u32[]{:S(2)}) copy-start(f32[256,256]{0,1:T(8,128)} %convolution_bitcast_fusion.2) | copy-start | bytes 786436
  280.0 32.8 %copy-start.1 = (f32[256,256]{0,1:T(8,128)S(1)}, f32[256,256]{0,1:T(8,128)}, u32[]{:S(2)}) copy-start(f32[256,256]{0,1:T(8,128)} %convolution_bitcast_fusion.1) | copy-start | bytes 786436
  280.0 32.8 %copy-start.2 = (f32[256,256]{0,1:T(8,128)S(1)}, f32[256,256]{0,1:T(8,128)}, u32[]{:S(2)}) copy-start(f32[256,256]{0,1:T(8,128)} %convolution_bitcast_fusion) | copy-start | bytes 786436
  280.0 22.2 %collective-permute-start.4 = (f32[256,256]{0,1:T(8,128)S(1)}, f32[256,256]{0,1:T(8,128)S(1)}, u32[]{:S(2)}, u32[]{:S(2)}) collective-permute-start(f32[256,256]{0,1:T(8,128)S(1)} %get-tuple-element.8), channel_id=1, source_target_pairs={{24,0},{28,4},{0,8},{4,12},{8,16},{12,20},{16,24},{20,28},{25,1},{... | collective-permute-start | bytes 786440 | tf_op jit(solution)/shard_map/ppermute | solution.py:13
  300.6 11.2 %collective-permute-start.5 = (f32[256,256]{0,1:T(8,128)S(1)}, f32[256,256]{0,1:T(8,128)S(1)}, u32[]{:S(2)}, u32[]{:S(2)}) collective-permute-start(f32[256,256]{0,1:T(8,128)S(1)} %slice_bitcast_fusion), channel_id=1, source_target_pairs={{28,0},{0,4},{4,8},{8,12},{12,16},{16,20},{20,24},{24,28},{29,1},{... | collective-permute-start | bytes 786440 | tf_op jit(solution)/shard_map/ppermute | solution.py:13
  312.6 81.8 %reduce-scatter.2.cloned.1.call-start = ((), (), s32[]{:S(2)}) async-start(), calls=%async_computation.8 | async-start | bytes 1179648 | tf_op jit(solution)/shard_map/reduce_scatter | solution.py:78
Sparse Core Ops, SparseCore 0:
  69.9 80.6 all-reduce.1
  152.5 16.2 all-gather.20
  172.2 16.7 all-gather.8
  207.4 14.0 all-gather.10
  224.9 16.7 all-gather.12
  260.1 14.0 all-gather.14
  277.6 16.7 all-gather.16
  312.8 14.0 all-gather.18
  330.6 63.7 reduce-scatter.1
where the time goes:
time: 401 us
  waiting for transfers between devices  273 us (68%)
  matrix products  92.8 us (23%)
  between operations  13.4 us (3%)
  starting transfers between devices  10.6 us (3%)
  local copies, waits for them, and re-layouts  6.44 us (2%)
  other arithmetic  5.2 us (1%)
    psum x1, waiting for transfers between devices, on_device(): totals = lax.psum(local_terms, 'row')  80.8 us
    reduce_scatter x1, waiting for transfers between devices, on_device(): lax.psum_scatter(jnp.stack(solved_parts), 'row', scatter_dimension=2, til...  63.9 us
    dot_general x1, matrix products, on_device(): jnp.einsum('lajc,las->jcs', own_factor, own_knowns * keep_mask[:, None, N...  61.7 us
    all_gather x4, waiting for transfers between devices, apply_inverse(): full_resid = lax.all_gather(residual, 'col', axis=0, tiled=True)  58.7 us
    all_gather x3, waiting for transfers between devices, spread_block(): lax.all_gather(solved_part, 'col', axis=0, tiled=True)  40 us
    ppermute x6, waiting for transfers between devices, from_behind(): return lax.ppermute(block, axis, route)  29 us
    dot_general x3, matrix products, spread_block(): jnp.einsum('ajc,as->jcs', rows_block, lax.all_gather(solved_part, 'col',...  18.8 us
    dot_general x4, matrix products, apply_inverse(): jnp.einsum('cm,cs->ms', inverse_block, full_resid, precision=lax.Precisio...  12.4 us
  transfers between devices with their start and end apart: 15, of which 12 were waited for; matrix products, arithmetic and copies ran while one was open for 4% of the time, Pallas kernels for 0%

commit v1 on v0

v1 whole, which is shorter than its diff:
```python
import functools

import jax
import jax.numpy as jnp
from jax import lax
from jax.experimental import pallas as pl
from jax.experimental.pallas import tpu as pltpu
from jax.sharding import PartitionSpec as P

F32 = jnp.float32
BF16 = jnp.bfloat16
LANES = 128


def split(value):
    high = value.astype(BF16)
    return high, (value - high.astype(F32)).astype(BF16)


def dot3(left, right):
    product = functools.partial(jnp.dot, preferred_element_type=F32)
    return product(left[0], right[0]) + (product(left[1], right[0]) + product(left[0], right[1]))


def swap_pairs(size, mask):
    return [(i, i ^ mask) for i in range(size)]


def factor_rows(factor):
    blocks, order, window, width = factor.shape
    tiles = width // LANES
    view = factor.reshape(blocks * order, window, tiles, LANES).transpose(0, 2, 1, 3)
    return view.reshape(blocks * order * tiles * window, LANES)


def prefix_kernel(dims, knowns_ref, factor_ref, send_first, keep_first, send_rest, keep_rest, total):
    rows, window, tiles, first_block, groups, part = dims
    step = pl.program_id(0)
    row = lax.axis_index("row")
    col = lax.axis_index("col")
    order, sources = knowns_ref.shape
    width = tiles * LANES
    stride = tiles * window

    @pl.when(step == 0)
    def _():
        total[...] = jnp.zeros_like(total)

    @pl.when(step * rows + row < first_block)
    def _():
        known = split(knowns_ref[...].T)
        for j in range(window):
            pieces = [
                split(factor_ref[pl.ds(t * window + j, order, stride=stride), :]) for t in range(tiles)
            ]
            high = jnp.concatenate([p[0] for p in pieces], axis=1)
            low = jnp.concatenate([p[1] for p in pieces], axis=1)
            total[j] += dot3(known, (high, low))

    @pl.when(step == pl.num_programs(0) - 1)
    def _():
        rhs = knowns_ref[pl.ds(pl.multiple_of(col * width, width), width), :].T
        bit = lax.rem(row, 2)
        for j in range(window):
            block_id = first_block + j
            own = (row == block_id % rows).astype(F32)
            total[j] = own * rhs - total[j]
        for j in range(window):
            keep, send = (keep_first, send_first) if j == 0 else (keep_rest, send_rest)
            at = 0 if j == 0 else j - 1
            for piece in range(groups * window // 2):
                mine = pl.multiple_of((2 * piece + bit) * part, part)
                other = pl.multiple_of((2 * piece + 1 - bit) * part, part)
                keep[at, piece] = total[j, pl.ds(mine, part), :]
                send[at, piece] = total[j, pl.ds(other, part), :]


def window_kernel(window, tiles, factor_ref, *outs):
    member = lax.rem(lax.axis_index("row"), window)
    order = outs[0].shape[0]
    for ahead, out in enumerate(outs, 1):
        j = jnp.minimum(member + ahead, window - 1)
        for t in range(tiles):
            out[:, t * LANES : (t + 1) * LANES] = factor_ref[
                pl.ds(t * window + j, order, stride=tiles * window), :
            ]


def apply_kernel(negate, parts_ref, matrix_ref, *rest):
    out = rest[-1]
    chunks, sources, width = parts_ref.shape
    left = split(jnp.concatenate([parts_ref[q] for q in range(chunks)], axis=1))
    product = dot3(left, split(matrix_ref[...]))
    out[...] = rest[0][...] - product if negate else product


def apply(parts, matrix, base=None):
    chunks, sources, width = parts.shape
    args = (parts, matrix) if base is None else (parts, matrix, base)
    cost = pl.CostEstimate(
        flops=6 * matrix.size * sources, bytes_accessed=4 * (matrix.size + parts.size), transcendentals=0
    )
    return pl.pallas_call(
        functools.partial(apply_kernel, base is not None),
        out_shape=jax.ShapeDtypeStruct((sources, matrix.shape[1]), F32),
        cost_estimate=cost,
    )(*args)


def gather_col(block, col):
    held = block[None]
    size = lax.axis_size("col")
    mask = 1
    while mask < size:
        other = lax.ppermute(held, "col", swap_pairs(size, mask))
        mine_first = (col & mask) == 0
        held = jnp.concatenate(
            [jnp.where(mine_first, held, other), jnp.where(mine_first, other, held)], axis=0
        )
        mask *= 2
    return held


def on_device(factor, knowns, inverse):
    rows = lax.axis_size("row")
    row = lax.axis_index("row")
    col = lax.axis_index("col")
    _, blocks, order, window, width = factor.shape
    sources = knowns.shape[-1]
    first_block = blocks * rows - window
    tiles = width // LANES
    groups = rows // window
    part = sources // rows
    solver = (first_block % rows) // window
    member = row % window
    slot = first_block // rows
    base_row = solver * window
    row_stride = tiles * window
    flat = factor_rows(factor[0])
    own_knowns = knowns[0]

    own = pl.pallas_call(
        functools.partial(window_kernel, window, tiles),
        grid=(1,),
        in_specs=[pl.BlockSpec((order * row_stride, LANES), lambda i: (slot, 0))],
        out_specs=[pl.BlockSpec((order, width), lambda i: (0, 0))] * (window - 1),
        out_shape=[jax.ShapeDtypeStruct((order, width), F32)] * (window - 1),
        compiler_params=pltpu.CompilerParams(vmem_limit_bytes=40 << 20),
    )(flat)

    def among(pairs, payload):
        return lax.ppermute(payload, "row", [(base_row + a, base_row + b) for a, b in pairs])

    near1 = among([(0, 1), (1, 0), (2, 3)], own[0])
    far1 = among([(0, 2), (1, 3), (2, 0)], own[0])

    half = groups * window // 2
    first_shape = jax.ShapeDtypeStruct((1, half, part, width), F32)
    rest_shape = jax.ShapeDtypeStruct((window - 1, half, part, width), F32)
    whole = lambda shape: pl.BlockSpec(shape.shape, lambda i: (0,) * 4)
    send0, keep0, send1, keep1 = pl.pallas_call(
        functools.partial(prefix_kernel, (rows, window, tiles, first_block, groups, part)),
        grid=(blocks,),
        in_specs=[
            pl.BlockSpec((order, sources), lambda i: (i, 0)),
            pl.BlockSpec((order * row_stride, LANES), lambda i: (i, 0)),
        ],
        out_specs=[whole(first_shape), whole(first_shape), whole(rest_shape), whole(rest_shape)],
        out_shape=[first_shape, first_shape, rest_shape, rest_shape],
        scratch_shapes=[pltpu.VMEM((window, sources, width), F32)],
        compiler_params=pltpu.CompilerParams(vmem_limit_bytes=40 << 20),
        cost_estimate=pl.CostEstimate(
            flops=6 * flat.size * sources, bytes_accessed=4 * (flat.size + own_knowns.size), transcendentals=0
        ),
    )(own_knowns.reshape(blocks * order, sources), flat)

    def reduce_rows(send, keep):
        total = keep + lax.ppermute(send, "row", swap_pairs(rows, 1))
        mask = 2
        while mask < window:
            total = total.reshape(total.shape[0], -1, 2, part, width)
            bit = (row // mask) % 2
            keep = jnp.where(bit == 0, total[:, :, 0], total[:, :, 1])
            send = jnp.where(bit == 0, total[:, :, 1], total[:, :, 0])
            total = keep + lax.ppermute(send, "row", swap_pairs(rows, mask))
            mask *= 2
        mask = 1
        while mask < groups:
            pairs = []
            for group in range(groups):
                apart = group ^ solver
                if apart & mask and not apart & (mask - 1):
                    pairs += [(group * window + k, (group ^ mask) * window + k) for k in range(window)]
            total = total + lax.ppermute(total, "row", pairs)
            mask *= 2
        return total.reshape(total.shape[0], groups * part, width)

    residual = [reduce_rows(send0, keep0)[0]]

    near2 = among([(0, 1), (1, 0), (2, 3), (3, 2)], jnp.where(member < 2, own[1], far1))
    far2 = among([(0, 2), (1, 3), (3, 1)], jnp.where(member < 2, own[1], near1))
    residual += list(reduce_rows(send1, keep1))

    near3 = among([(0, 1), (2, 3), (3, 2)], jnp.where(member == 0, own[2], far2))
    far3 = among([(0, 2)], own[2])
    top = order // 2
    near4 = among([(2, 3)], far3[:top])
    far4 = among([(1, 3)], near3[top:])
    last = jnp.concatenate([near4, far4], axis=0)

    def choose(*options):
        out = options[-1]
        for at in range(len(options) - 2, -1, -1):
            out = jnp.where(member == at, options[at], out)
        return out

    between = {
        (0, 1): choose(own[0], near1, far1, near2),
        (1, 2): choose(near1, own[0], near2, far1),
        (2, 3): choose(far1, far2, own[0], near1),
        (0, 2): choose(own[1], near2, far2, near3),
        (1, 3): choose(near2, own[1], near3, far2),
        (0, 3): choose(own[2], near3, far3, last),
    }

    solved = []
    for j in range(window):
        x = apply(gather_col(residual[j], col), inverse[j])
        solved.append(x)
        if j + 1 < window:
            full = gather_col(x, col)
            for k in range(j + 1, window):
                residual[k] = apply(full, between[j, k], residual[k])

    stacked = jnp.stack(solved).reshape(window, groups, part, width)
    result = stacked[:, solver]
    for group in range(groups):
        if group != solver:
            pairs = [(base_row + k, group * window + k) for k in range(window)]
            moved = lax.ppermute(stacked[:, group], "row", pairs)
            result = jnp.where(row // window == group, moved, result)
    return result.transpose(0, 2, 1)


def solution(mesh):
    return jax.shard_map(
        on_device,
        mesh=mesh,
        in_specs=(
            P("row", None, None, None, "col"),
            P("row", None, None, None),
            P(None, None, "col"),
        ),
        out_specs=P(None, "col", "row"),
        check_vma=False,
    )
```

time: 401 us -> 209 us (0.52)
  the two profiles are of different devices: /device:TPU:0 before, /device:TPU:12 now
where the time goes in v1:
time: 209 us; the launch traced here: 207 us
  waiting for transfers between devices  65.9 us (32%)
  Pallas kernels  55.3 us (26%)
  starting transfers between devices  48.3 us (23%)
  other arithmetic  29.2 us (14%)
  local copies, waits for them, and re-layouts  8.47 us (4%)
    ppermute x1, waiting for transfers between devices, on_device(): moved = lax.ppermute(stacked[:, group], 'row', pairs)  31.7 us
    pallas_call x1, Pallas kernels, on_device(): pl.pallas_call(functools.partial(prefix_kernel, (rows, window, tiles, fir...  29.2 us
    pallas_call x10, Pallas kernels, apply(): pl.pallas_call(functools.partial(apply_kernel, base is not None), out_sha...  23 us
    ppermute x14, waiting for transfers between devices, gather_col(): other = lax.ppermute(held, 'col', swap_pairs(size, mask))  21.8 us
    ppermute x2, starting transfers between devices, reduce_rows(): total = total + lax.ppermute(total, 'row', pairs)  20.7 us
    ppermute x8, starting transfers between devices, among(): lax.ppermute(payload, 'row', [(base_row + a, base_row + b) for a, b in pa...  10.7 us
    ppermute x14, starting transfers between devices, gather_col(): other = lax.ppermute(held, 'col', swap_pairs(size, mask))  9.8 us
    select_n x14, other arithmetic, gather_col(): jnp.where(mine_first, held, other)  6.13 us
  transfers between devices with their start and end apart: 29, of which 14 were waited for; matrix products, arithmetic and copies ran while one was open for 10% of the time, Pallas kernels for 18%

profile of v1, /device:TPU:12, one launch (start us, length us, event | category | flops | bytes accessed | tf_op | source)
XLA Modules:
  0.0 207.4 jit_solution(17148428709880285166)
XLA Ops:
  0.0 3.1 %shard_map.39 = (f32[1024,256]{1,0:T(8,128)S(1)}, f32[1024,256]{1,0:T(8,128)S(1)}, f32[1024,256]{1,0:T(8,128)S(1)}) custom-call(f32[98304,128]{1,0:T(8,128)} %bitcast.95), custom_call_target="tpu_custom_call" | custom-call | tf_op jit(solution)/shard_map/pallas_call | solution.py:142
  3.1 1.8 collective-permute-start.7
  4.9 1.8 collective-permute-start.8
  6.7 29.2 %shard_map.37 = (f32[1,4,32,256]{3,2,1,0:T(8,128)}, f32[1,4,32,256]{3,2,1,0:T(8,128)S(1)}, f32[3,4,32,256]{3,2,1,0:T(8,128)S(1)}, f32[3,4,32,256]{3,2,1,0:T(8,128)S(1)}) custom-call(f32[12288,256]{1,0:T(8,128)S(1)} %bitcast.94, f32[98304,128]{1,0:T(8,128)} %bitcast.96), custom_call_target="tpu_custom_call" | custom-call | flops 19327352832 | bytes 62914560 | tf_op jit(solution)/shard_map/pallas_call | solution.py:161
  37.7 5.0 %collective-permute-done = f32[1,4,32,256]{3,2,1,0:T(8,128)} collective-permute-done((f32[1,4,32,256]{3,2,1,0:T(8,128)}, f32[1,4,32,256]{3,2,1,0:T(8,128)}, u32[]{:S(2)}, u32[]{:S(2)}) %collective-permute-start) | collective-permute-done | bytes 131104 | tf_op jit(solution)/shard_map/ppermute | solution.py:178
  44.3 3.1 %broadcast_select_fusion = (f32[1024,256]{1,0:T(8,128)}, f32[1024,256]{1,0:T(8,128)}) fusion(f32[1024,256]{1,0:T(8,128)S(1)} %get-tuple-element.15, f32[1024,256]{1,0:T(8,128)} %collective-permute-done.7, pred[]{:T(512)S(6)} %lt.18, f32[1024,256]{1,0:T(8,128)} %collective-permute-done.8), kind=kLoop, calls=%fused_computation.12 | loop fusion | flops 524288 | bytes 5242881 | tf_op jit(solution)/shard_map/jit(_where)/select_n | solution.py:201
  47.4 1.6 collective-permute-start.17
  49.0 5.5 %collective-permute-start.2 = (f32[1,2,32,256]{3,2,1,0:T(8,128)S(1)}, f32[1,2,32,256]{3,2,1,0:T(8,128)S(1)}, u32[]{:S(2)}, u32[]{:S(2)}) collective-permute-start(f32[1,2,32,256]{3,2,1,0:T(8,128)S(1)} %bitcast_add_fusion.1), channel_id=1, source_target_pairs={{0,16},{4,20},{8,24},{12,28},{1,17},{5,21},{9,25},{13,29},{2,18},{... | collective-permute-start | bytes 196616 | tf_op jit(solution)/shard_map/ppermute | solution.py:194
  54.6 1.7 collective-permute-start.23
  56.3 1.4 collective-permute-start.10
  58.3 4.2 %slice_bitcast_fusion = (f32[1024,256]{1,0:T(8,128)}, f32[1024,256]{1,0:T(8,128)}, f32[1024,256]{1,0:T(8,128)}, f32[1024,256]{1,0:T(8,128)}) fusion(f32[4,1024,256]{2,1,0:T(8,128)} %param.5), kind=kLoop, calls=%fused_computation.3 | loop fusion | bytes 8388608 | tf_op jit(solution)/shard_map/squeeze | solution.py:228
  63.4 1.6 collective-permute-start.4
  65.5 1.8 add.33
  67.2 2.3 %broadcast_select_fusion.2 = f32[1024,256]{1,0:T(8,128)} fusion(f32[1024,256]{1,0:T(8,128)S(1)} %get-tuple-element.18, f32[1024,256]{1,0:T(8,128)} %collective-permute-done.17, pred[]{:T(512)S(6)} %eq.22), kind=kLoop, calls=%fused_computation.14 | loop fusion | flops 262144 | bytes 3145729 | tf_op jit(solution)/shard_map/jit(_where)/select_n | solution.py:204
  69.6 1.7 collective-permute-start.18
  72.0 2.3 %shard_map.38 = f32[64,256]{1,0:T(8,128)} custom-call(f32[4,64,256]{2,1,0:T(8,128)} %pad_maximum_fusion.parts_ref, f32[1024,256]{1,0:T(8,128)} %get-tuple-element.21.matrix_ref), custom_call_target="tpu_custom_call" | custom-call | flops 100663296 | bytes 1310720 | tf_op jit(solution)/shard_map/pallas_call | solution.py:103
  75.4 3.4 %collective-permute-start.11 = (f32[3,2,32,256]{3,2,1,0:T(8,128)S(1)}, f32[3,2,32,256]{3,2,1,0:T(8,128)S(1)}, u32[]{:S(2)}, u32[]{:S(2)}) collective-permute-start(f32[3,2,32,256]{3,2,1,0:T(8,128)S(1)} %select_bitcast_fusion), channel_id=1, source_target_pairs={{0,8},{4,12},{8,0},{12,4},{16,24},{20,28},{24,16},{28,20},{1,9},{5... | collective-permute-start | bytes 589832 | tf_op jit(solution)/shard_map/ppermute | solution.py:185
  81.3 2.9 %collective-permute-done.11 = f32[3,2,32,256]{3,2,1,0:T(8,128)S(1)} collective-permute-done((f32[3,2,32,256]{3,2,1,0:T(8,128)S(1)}, f32[3,2,32,256]{3,2,1,0:T(8,128)S(1)}, u32[]{:S(2)}, u32[]{:S(2)}) %collective-permute-start.11) | collective-permute-done | bytes 196640 | tf_op jit(solution)/shard_map/ppermute | solution.py:185
  84.2 1.1 bitcast_add_fusion
  85.2 15.2 %collective-permute-start.12 = (f32[3,2,32,256]{3,2,1,0:T(8,128)S(1)}, f32[3,2,32,256]{3,2,1,0:T(8,128)S(1)}, u32[]{:S(2)}, u32[]{:S(2)}) collective-permute-start(f32[3,2,32,256]{3,2,1,0:T(8,128)S(1)} %bitcast_add_fusion), channel_id=1, source_target_pairs={{0,16},{4,20},{8,24},{12,28},{1,17},{5,21},{9,25},{13,29},{2,18},{... | collective-permute-start | bytes 589832 | tf_op jit(solution)/shard_map/ppermute | solution.py:194
  100.5 1.1 slice.59
  102.3 1.1 slice.60
  104.8 3.9 %collective-permute-done.12 = f32[3,2,32,256]{3,2,1,0:T(8,128)S(1)} collective-permute-done((f32[3,2,32,256]{3,2,1,0:T(8,128)S(1)}, f32[3,2,32,256]{3,2,1,0:T(8,128)S(1)}, u32[]{:S(2)}, u32[]{:S(2)}) %collective-permute-start.12) | collective-permute-done | bytes 196640 | tf_op jit(solution)/shard_map/ppermute | solution.py:194
  109.5 5.4 %select_select_fusion.3 = (f32[1024,256]{1,0:T(8,128)}, f32[1024,256]{1,0:T(8,128)}, f32[1024,256]{1,0:T(8,128)}, f32[1024,256]{1,0:T(8,128)}, f32[1024,256]{1,0:T(8,128)}, /*index=5*/f32[1024,256]{1,0:T(8,128)}) fusion(f32[1024,256]{1,0:T(8,128)} %collective-permute-done.7, f32[1024,256]{1,0:T(8,128)S(1)} %get-tuple-element.14, ...), kind=kLoop, calls=%fused_computation.8 | loop fusion | flops 4980736 | bytes 16777220 | tf_op jit(solution)/shard_map/jit(_where)/select_n | solution.py:214
  114.9 2.3 %shard_map.40 = f32[64,256]{1,0:T(8,128)} custom-call(f32[4,64,256]{2,1,0:T(8,128)} %pad_maximum_fusion.1.parts_ref, f32[1024,256]{1,0:T(8,128)} %get-tuple-element.26.matrix_ref, f32[64,256]{1,0:T(8,128)} %bitcast.109), custom_call_target="tpu_custom_call" | custom-call | flops 100663296 | bytes 1310720 | tf_op jit(solution)/shard_map/pallas_call | solution.py:103
  117.2 1.4 collective-permute-done.13
  119.6 1.6 collective-permute-start.14
  121.1 4.1 %collective-permute-done.14 = f32[2,64,256]{2,1,0:T(8,128)S(1)} collective-permute-done((f32[2,64,256]{2,1,0:T(8,128)S(1)}, f32[2,64,256]{2,1,0:T(8,128)S(1)}, u32[]{:S(2)}, u32[]{:S(2)}) %collective-permute-start.14) | collective-permute-done | bytes 131104 | tf_op jit(solution)/shard_map/ppermute | solution.py:115
  125.9 2.3 %shard_map.41 = f32[64,256]{1,0:T(8,128)} custom-call(f32[4,64,256]{2,1,0:T(8,128)} %pad_maximum_fusion.2.parts_ref, f32[1024,256]{1,0:T(8,128)} %get-tuple-element.20.matrix_ref), custom_call_target="tpu_custom_call" | custom-call | flops 100663296 | bytes 1310720 | tf_op jit(solution)/shard_map/pallas_call | solution.py:103
  128.3 1.5 collective-permute-done.15
  130.6 1.6 collective-permute-start.16
  132.2 2.3 %shard_map.42.rest_0_ = f32[64,256]{1,0:T(8,128)} custom-call(f32[4,64,256]{2,1,0:T(8,128)} %pad_maximum_fusion.1.parts_ref, f32[1024,256]{1,0:T(8,128)} %get-tuple-element.28.matrix_ref, f32[64,256]{1,0:T(8,128)} %bitcast.108), custom_call_target="tpu_custom_call" | custom-call | flops 100663296 | bytes 1310720 | tf_op jit(solution)/shard_map/pallas_call | solution.py:103
  134.4 1.8 collective-permute-done.16
  137.0 2.3 %shard_map.43 = f32[64,256]{1,0:T(8,128)} custom-call(f32[4,64,256]{2,1,0:T(8,128)} %pad_maximum_fusion.3.parts_ref, f32[1024,256]{1,0:T(8,128)} %get-tuple-element.25.matrix_ref, f32[64,256]{1,0:T(8,128)} %shard_map.42.rest_0_), custom_call_target="tpu_custom_call" | custom-call | flops 100663296 | bytes 1310720 | tf_op jit(solution)/shard_map/pallas_call | solution.py:103
  139.3 1.5 collective-permute-done.19
  141.6 1.6 collective-permute-start.20
  143.2 4.1 %collective-permute-done.20 = f32[2,64,256]{2,1,0:T(8,128)S(1)} collective-permute-done((f32[2,64,256]{2,1,0:T(8,128)S(1)}, f32[2,64,256]{2,1,0:T(8,128)S(1)}, u32[]{:S(2)}, u32[]{:S(2)}) %collective-permute-start.20) | collective-permute-done | bytes 131104 | tf_op jit(solution)/shard_map/ppermute | solution.py:115
  148.0 2.3 %shard_map.44 = f32[64,256]{1,0:T(8,128)} custom-call(f32[4,64,256]{2,1,0:T(8,128)} %pad_maximum_fusion.4.parts_ref, f32[1024,256]{1,0:T(8,128)} %get-tuple-element.22.matrix_ref), custom_call_target="tpu_custom_call" | custom-call | flops 100663296 | bytes 1310720 | tf_op jit(solution)/shard_map/pallas_call | solution.py:103
  150.3 1.5 collective-permute-done.21
  152.6 1.6 collective-permute-start.22
  154.2 2.3 %shard_map.45.rest_0_ = f32[64,256]{1,0:T(8,128)} custom-call(f32[4,64,256]{2,1,0:T(8,128)} %pad_maximum_fusion.1.parts_ref, f32[1024,256]{1,0:T(8,128)} %get-tuple-element.30.matrix_ref, f32[64,256]{1,0:T(8,128)} %bitcast.107), custom_call_target="tpu_custom_call" | custom-call | flops 100663296 | bytes 1310720 | tf_op jit(solution)/shard_map/pallas_call | solution.py:103
  156.5 2.3 %shard_map.46.rest_0_ = f32[64,256]{1,0:T(8,128)} custom-call(f32[4,64,256]{2,1,0:T(8,128)} %pad_maximum_fusion.3.parts_ref, f32[1024,256]{1,0:T(8,128)} %get-tuple-element.29.matrix_ref, f32[64,256]{1,0:T(8,128)} %shard_map.45.rest_0_), custom_call_target="tpu_custom_call" | custom-call | flops 100663296 | bytes 1310720 | tf_op jit(solution)/shard_map/pallas_call | solution.py:103
  159.5 2.3 %shard_map.47 = f32[64,256]{1,0:T(8,128)} custom-call(f32[4,64,256]{2,1,0:T(8,128)} %pad_maximum_fusion.5.parts_ref, f32[1024,256]{1,0:T(8,128)} %get-tuple-element.27.matrix_ref, f32[64,256]{1,0:T(8,128)} %shard_map.46.rest_0_), custom_call_target="tpu_custom_call" | custom-call | flops 100663296 | bytes 1310720 | tf_op jit(solution)/shard_map/pallas_call | solution.py:103
  161.8 1.5 collective-permute-done.26
  165.2 4.6 %collective-permute-done.27 = f32[2,64,256]{2,1,0:T(8,128)S(1)} collective-permute-done((f32[2,64,256]{2,1,0:T(8,128)S(1)}, f32[2,64,256]{2,1,0:T(8,128)S(1)}, u32[]{:S(2)}, u32[]{:S(2)}) %collective-permute-start.27) | collective-permute-done | bytes 131104 | tf_op jit(solution)/shard_map/ppermute | solution.py:115
  170.5 2.3 %shard_map.48 = f32[64,256]{1,0:T(8,128)} custom-call(f32[4,64,256]{2,1,0:T(8,128)} %pad_maximum_fusion.6.parts_ref, f32[1024,256]{1,0:T(8,128)} %get-tuple-element.19.matrix_ref), custom_call_target="tpu_custom_call" | custom-call | flops 100663296 | bytes 1310720 | tf_op jit(solution)/shard_map/pallas_call | solution.py:103
  173.7 1.3 collective-permute-start.28
  175.0 31.7 %collective-permute-done.28 = f32[4,32,256]{2,1,0:T(8,128)S(1)} collective-permute-done((f32[4,32,256]{2,1,0:T(8,128)S(1)}, f32[4,32,256]{2,1,0:T(8,128)S(1)}, u32[]{:S(2)}, u32[]{:S(2)}) %collective-permute-start.28) | collective-permute-done | bytes 131104 | tf_op jit(solution)/shard_map/ppermute | solution.py:240
  (78 shorter events, 23.3 us)
Async XLA Ops:
  0.0 6.7 %copy-start.1 = (f32[1,12,1024,256]{3,2,1,0:T(8,128)S(1)}, f32[1,12,1024,256]{3,2,1,0:T(8,128)}, u32[]{:S(2)}) copy-start(f32[1,12,1024,256]{3,2,1,0:T(8,128)} %param.4) | copy-start | bytes 37748740
  3.1 41.2 %collective-permute-start.7 = (f32[1024,256]{1,0:T(8,128)S(1)}, f32[1024,256]{1,0:T(8,128)}, u32[]{:S(2)}, u32[]{:S(2)}) collective-permute-start(f32[1024,256]{1,0:T(8,128)S(1)} %get-tuple-element.14), channel_id=1, source_target_pairs={{16,20},{20,16},{24,28},{17,21},{21,17},{25,29},{18,22},{22,18},{2... | collective-permute-start | bytes 3145736 | tf_op jit(solution)/shard_map/ppermute | solution.py:152
  4.9 39.4 %collective-permute-start.8 = (f32[1024,256]{1,0:T(8,128)S(1)}, f32[1024,256]{1,0:T(8,128)}, u32[]{:S(2)}, u32[]{:S(2)}) collective-permute-start(f32[1024,256]{1,0:T(8,128)S(1)} %get-tuple-element.14), channel_id=1, source_target_pairs={{16,24},{20,28},{24,16},{17,25},{21,29},{25,17},{18,26},{22,30},{2... | collective-permute-start | bytes 3145736 | tf_op jit(solution)/shard_map/ppermute | solution.py:152
  35.8 0.7 copy-start
  36.5 0.7 copy-start.2
  37.2 5.5 %collective-permute-start = (f32[1,4,32,256]{3,2,1,0:T(8,128)}, f32[1,4,32,256]{3,2,1,0:T(8,128)}, u32[]{:S(2)}, u32[]{:S(2)}) collective-permute-start(f32[1,4,32,256]{3,2,1,0:T(8,128)} %get-tuple-element.13), channel_id=1, source_target_pairs={{0,4},{4,0},{8,12},{12,8},{16,20},{20,16},{24,28},{28,24},{1,5},{5... | collective-permute-start | bytes 393224 | tf_op jit(solution)/shard_map/ppermute | solution.py:178
  43.8 5.2 %collective-permute-start.1 = (f32[1,2,32,256]{3,2,1,0:T(8,128)S(1)}, f32[1,2,32,256]{3,2,1,0:T(8,128)S(1)}, u32[]{:S(2)}, u32[]{:S(2)}) collective-permute-start(f32[1,2,32,256]{3,2,1,0:T(8,128)S(1)} %select_bitcast_fusion.1), channel_id=1, source_target_pairs={{0,8},{4,12},{8,0},{12,4},{16,24},{20,28},{24,16},{28,20},{1,9},{5... | collective-permute-start | bytes 196616 | tf_op jit(solution)/shard_map/ppermute | solution.py:185
  47.4 19.9 %collective-permute-start.17 = (f32[1024,256]{1,0:T(8,128)}, f32[1024,256]{1,0:T(8,128)}, u32[]{:S(2)}, u32[]{:S(2)}) collective-permute-start(f32[1024,256]{1,0:T(8,128)} %get-tuple-element.31), channel_id=1, source_target_pairs={{16,24},{20,28},{28,20},{17,25},{21,29},{29,21},{18,26},{22,30},{3... | collective-permute-start | bytes 3145736 | tf_op jit(solution)/shard_map/ppermute | solution.py:152
  49.0 8.6 %collective-permute-start.2 = (f32[1,2,32,256]{3,2,1,0:T(8,128)S(1)}, f32[1,2,32,256]{3,2,1,0:T(8,128)S(1)}, u32[]{:S(2)}, u32[]{:S(2)}) collective-permute-start(f32[1,2,32,256]{3,2,1,0:T(8,128)S(1)} %bitcast_add_fusion.1), channel_id=1, source_target_pairs={{0,16},{4,20},{8,24},{12,28},{1,17},{5,21},{9,25},{13,29},{2,18},{... | collective-permute-start | bytes 196616 | tf_op jit(solution)/shard_map/ppermute | solution.py:194
  54.6 45.9 %collective-permute-start.23 = (f32[1024,256]{1,0:T(8,128)S(1)}, f32[1024,256]{1,0:T(8,128)}, u32[]{:S(2)}, u32[]{:S(2)}) collective-permute-start(f32[1024,256]{1,0:T(8,128)S(1)} %get-tuple-element.18), channel_id=1, source_target_pairs={{16,24},{17,25},{18,26},{19,27}} | collective-permute-start | bytes 3145736 | tf_op jit(solution)/shard_map/ppermute | solution.py:152
  56.3 9.2 %collective-permute-start.10 = (f32[3,4,32,256]{3,2,1,0:T(8,128)}, f32[3,4,32,256]{3,2,1,0:T(8,128)}, u32[]{:S(2)}, u32[]{:S(2)}) collective-permute-start(f32[3,4,32,256]{3,2,1,0:T(8,128)} %copy-done.2), channel_id=1, source_target_pairs={{0,4},{4,0},{8,12},{12,8},{16,20},{20,16},{24,28},{28,24},{1,5},{5... | collective-permute-start | bytes 1179656 | tf_op jit(solution)/shard_map/ppermute | solution.py:178
  58.3 4.2 %collective-permute-start.3 = (f32[1,64,256]{2,1,0:T(8,128)}, f32[1,64,256]{2,1,0:T(8,128)}, u32[]{:S(2)}, u32[]{:S(2)}) collective-permute-start(f32[1,64,256]{2,1,0:T(8,128)} %bitcast.7), channel_id=1, source_target_pairs={{0,1},{1,0},{2,3},{3,2},{4,5},{5,4},{6,7},{7,6},{8,9},{9,8},{10,11... | collective-permute-start | bytes 196616 | tf_op jit(solution)/shard_map/ppermute | solution.py:115
  63.4 7.9 %collective-permute-start.4 = (f32[2,64,256]{2,1,0:T(8,128)S(1)}, f32[2,64,256]{2,1,0:T(8,128)S(1)}, u32[]{:S(2)}, u32[]{:S(2)}) collective-permute-start(f32[2,64,256]{2,1,0:T(8,128)S(1)} %pad_maximum_fusion.8), channel_id=1, source_target_pairs={{0,2},{1,3},{2,0},{3,1},{4,6},{5,7},{6,4},{7,5},{8,10},{9,11},{10,... | collective-permute-start | bytes 393224 | tf_op jit(solution)/shard_map/ppermute | solution.py:115
  69.6 32.7 %collective-permute-start.18 = (f32[1024,256]{1,0:T(8,128)}, f32[1024,256]{1,0:T(8,128)}, u32[]{:S(2)}, u32[]{:S(2)}) collective-permute-start(f32[1024,256]{1,0:T(8,128)} %broadcast_select_fusion.2), channel_id=1, source_target_pairs={{16,20},{24,28},{28,24},{17,21},{25,29},{29,25},{18,22},{26,30},{3... | collective-permute-start | bytes 3145736 | tf_op jit(solution)/shard_map/ppermute | solution.py:152
  74.3 5.2 %collective-permute-start.5 = (f32[1,64,256]{2,1,0:T(8,128)}, f32[1,64,256]{2,1,0:T(8,128)S(1)}, u32[]{:S(2)}, u32[]{:S(2)}) collective-permute-start(f32[1,64,256]{2,1,0:T(8,128)} %bitcast.101), channel_id=1, source_target_pairs={{0,1},{1,0},{2,3},{3,2},{4,5},{5,4},{6,7},{7,6},{8,9},{9,8},{10,11... | collective-permute-start | bytes 196616 | tf_op jit(solution)/shard_map/ppermute | solution.py:115
  75.4 8.8 %collective-permute-start.11 = (f32[3,2,32,256]{3,2,1,0:T(8,128)S(1)}, f32[3,2,32,256]{3,2,1,0:T(8,128)S(1)}, u32[]{:S(2)}, u32[]{:S(2)}) collective-permute-start(f32[3,2,32,256]{3,2,1,0:T(8,128)S(1)} %select_bitcast_fusion), channel_id=1, source_target_pairs={{0,8},{4,12},{8,0},{12,4},{16,24},{20,28},{24,16},{28,20},{1,9},{5... | collective-permute-start | bytes 589832 | tf_op jit(solution)/shard_map/ppermute | solution.py:185
  78.8 30.7 %collective-permute-start.9 = (f32[1024,256]{1,0:T(8,128)}, f32[1024,256]{1,0:T(8,128)S(1)}, u32[]{:S(2)}, u32[]{:S(2)}) collective-permute-start(f32[1024,256]{1,0:T(8,128)} %get-tuple-element.32), channel_id=1, source_target_pairs={{16,20},{20,16},{24,28},{28,24},{17,21},{21,17},{25,29},{29,25},{1... | collective-permute-start | bytes 3145736 | tf_op jit(solution)/shard_map/ppermute | solution.py:152
  80.4 23.6 %collective-permute-start.6 = (f32[2,64,256]{2,1,0:T(8,128)S(1)}, f32[2,64,256]{2,1,0:T(8,128)S(1)}, u32[]{:S(2)}, u32[]{:S(2)}) collective-permute-start(f32[2,64,256]{2,1,0:T(8,128)S(1)} %pad_maximum_fusion.9), channel_id=1, source_target_pairs={{0,2},{1,3},{2,0},{3,1},{4,6},{5,7},{6,4},{7,5},{8,10},{9,11},{10,... | collective-permute-start | bytes 393224 | tf_op jit(solution)/shard_map/ppermute | solution.py:115
  85.2 23.5 %collective-permute-start.12 = (f32[3,2,32,256]{3,2,1,0:T(8,128)S(1)}, f32[3,2,32,256]{3,2,1,0:T(8,128)S(1)}, u32[]{:S(2)}, u32[]{:S(2)}) collective-permute-start(f32[3,2,32,256]{3,2,1,0:T(8,128)S(1)} %bitcast_add_fusion), channel_id=1, source_target_pairs={{0,16},{4,20},{8,24},{12,28},{1,17},{5,21},{9,25},{13,29},{2,18},{... | collective-permute-start | bytes 589832 | tf_op jit(solution)/shard_map/ppermute | solution.py:194
  101.6 7.9 %collective-permute-start.24 = (f32[512,256]{1,0:T(8,128)S(1)}, f32[512,256]{1,0:T(8,128)S(1)}, u32[]{:S(2)}, u32[]{:S(2)}) collective-permute-start(f32[512,256]{1,0:T(8,128)S(1)} %slice.59), channel_id=1, source_target_pairs={{24,28},{25,29},{26,30},{27,31}} | collective-permute-start | bytes 1572872 | tf_op jit(solution)/shard_map/ppermute | solution.py:152
  103.3 6.2 %collective-permute-start.25 = (f32[512,256]{1,0:T(8,128)S(1)}, f32[512,256]{1,0:T(8,128)S(1)}, u32[]{:S(2)}, u32[]{:S(2)}) collective-permute-start(f32[512,256]{1,0:T(8,128)S(1)} %slice.60), channel_id=1, source_target_pairs={{20,28},{21,29},{22,30},{23,31}} | collective-permute-start | bytes 1572872 | tf_op jit(solution)/shard_map/ppermute | solution.py:152
  114.9 57.9 %copy-start.3 = (f32[64,256]{1,0:T(8,128)S(1)}, f32[64,256]{1,0:T(8,128)}, u32[]{:S(2)}) copy-start(f32[64,256]{1,0:T(8,128)} %shard_map.38) | copy-start | bytes 196612
  117.2 1.5 collective-permute-start.13
  119.6 5.6 %collective-permute-start.14 = (f32[2,64,256]{2,1,0:T(8,128)S(1)}, f32[2,64,256]{2,1,0:T(8,128)S(1)}, u32[]{:S(2)}, u32[]{:S(2)}) collective-permute-start(f32[2,64,256]{2,1,0:T(8,128)S(1)} %pad_maximum_fusion.10), channel_id=1, source_target_pairs={{0,2},{1,3},{2,0},{3,1},{4,6},{5,7},{6,4},{7,5},{8,10},{9,11},{10,... | collective-permute-start | bytes 393224 | tf_op jit(solution)/shard_map/ppermute | solution.py:115
  128.3 44.5 %copy-start.4 = (f32[64,256]{1,0:T(8,128)S(1)}, f32[64,256]{1,0:T(8,128)}, u32[]{:S(2)}) copy-start(f32[64,256]{1,0:T(8,128)} %shard_map.41) | copy-start | bytes 196612
  128.3 1.5 collective-permute-start.15
  130.6 5.6 %collective-permute-start.16 = (f32[2,64,256]{2,1,0:T(8,128)S(1)}, f32[2,64,256]{2,1,0:T(8,128)S(1)}, u32[]{:S(2)}, u32[]{:S(2)}) collective-permute-start(f32[2,64,256]{2,1,0:T(8,128)S(1)} %pad_maximum_fusion.11), channel_id=1, source_target_pairs={{0,2},{1,3},{2,0},{3,1},{4,6},{5,7},{6,4},{7,5},{8,10},{9,11},{10,... | collective-permute-start | bytes 393224 | tf_op jit(solution)/shard_map/ppermute | solution.py:115
  139.3 1.5 collective-permute-start.19
  141.6 5.6 %collective-permute-start.20 = (f32[2,64,256]{2,1,0:T(8,128)S(1)}, f32[2,64,256]{2,1,0:T(8,128)S(1)}, u32[]{:S(2)}, u32[]{:S(2)}) collective-permute-start(f32[2,64,256]{2,1,0:T(8,128)S(1)} %pad_maximum_fusion.12), channel_id=1, source_target_pairs={{0,2},{1,3},{2,0},{3,1},{4,6},{5,7},{6,4},{7,5},{8,10},{9,11},{10,... | collective-permute-start | bytes 393224 | tf_op jit(solution)/shard_map/ppermute | solution.py:115
  150.3 1.5 collective-permute-start.21
  152.6 6.1 %collective-permute-start.22 = (f32[2,64,256]{2,1,0:T(8,128)S(1)}, f32[2,64,256]{2,1,0:T(8,128)S(1)}, u32[]{:S(2)}, u32[]{:S(2)}) collective-permute-start(f32[2,64,256]{2,1,0:T(8,128)S(1)} %pad_maximum_fusion.13), channel_id=1, source_target_pairs={{0,2},{1,3},{2,0},{3,1},{4,6},{5,7},{6,4},{7,5},{8,10},{9,11},{10,... | collective-permute-start | bytes 393224 | tf_op jit(solution)/shard_map/ppermute | solution.py:115
  161.8 1.5 collective-permute-start.26
  164.1 5.6 %collective-permute-start.27 = (f32[2,64,256]{2,1,0:T(8,128)S(1)}, f32[2,64,256]{2,1,0:T(8,128)S(1)}, u32[]{:S(2)}, u32[]{:S(2)}) collective-permute-start(f32[2,64,256]{2,1,0:T(8,128)S(1)} %pad_maximum_fusion.14), channel_id=1, source_target_pairs={{0,2},{1,3},{2,0},{3,1},{4,6},{5,7},{6,4},{7,5},{8,10},{9,11},{10,... | collective-permute-start | bytes 393224 | tf_op jit(solution)/shard_map/ppermute | solution.py:115
  173.7 33.1 %collective-permute-start.28 = (f32[4,32,256]{2,1,0:T(8,128)S(1)}, f32[4,32,256]{2,1,0:T(8,128)S(1)}, u32[]{:S(2)}, u32[]{:S(2)}) collective-permute-start(f32[4,32,256]{2,1,0:T(8,128)S(1)} %slice_bitcast_fusion.7), channel_id=1, source_target_pairs={{16,0},{20,4},{24,8},{28,12},{17,1},{21,5},{25,9},{29,13},{18,2},{... | collective-permute-start | bytes 393224 | tf_op jit(solution)/shard_map/ppermute | solution.py:240

commit v2 on v1

v2 whole, which is shorter than its diff:
```python
import functools

import jax
import jax.numpy as jnp
from jax import lax
from jax.experimental import pallas as pl
from jax.experimental.pallas import tpu as pltpu
from jax.sharding import PartitionSpec as P

F32 = jnp.float32
BF16 = jnp.bfloat16
LANES = 128


def split(value):
    high = value.astype(BF16)
    return high, (value - high.astype(F32)).astype(BF16)


def dot3(left, right):
    product = functools.partial(jnp.dot, preferred_element_type=F32)
    return product(left[0], right[0]) + (product(left[1], right[0]) + product(left[0], right[1]))


def swap_pairs(size, mask):
    return [(i, i ^ mask) for i in range(size)]


def factor_rows(factor):
    blocks, order, window, width = factor.shape
    tiles = width // LANES
    view = factor.reshape(blocks * order, window, tiles, LANES).transpose(0, 2, 1, 3)
    return view.reshape(blocks * order * tiles * window, LANES)


def accumulate(dims, block, knowns_ref, factor_ref, total):
    rows, window, tiles, first_block = dims
    order = knowns_ref.shape[0]
    stride = tiles * window

    @pl.when(block * rows + lax.axis_index("row") < first_block)
    def _():
        known = split(knowns_ref[...].T)
        for j in range(window):
            pieces = [
                split(factor_ref[pl.ds(t * window + j, order, stride=stride), :]) for t in range(tiles)
            ]
            high = jnp.concatenate([p[0] for p in pieces], axis=1)
            low = jnp.concatenate([p[1] for p in pieces], axis=1)
            total[j] += dot3(known, (high, low))


def prefix_kernel(dims, groups, part, knowns_ref, factor_ref, send_first, keep_first, send_rest, keep_rest, total):
    rows, window, tiles, first_block = dims
    step = pl.program_id(0)
    row = lax.axis_index("row")
    col = lax.axis_index("col")
    width = tiles * LANES

    @pl.when(step == 0)
    def _():
        total[...] = jnp.zeros_like(total)

    accumulate(dims, step, knowns_ref, factor_ref, total)

    @pl.when(step == pl.num_programs(0) - 1)
    def _():
        rhs = knowns_ref[pl.ds(pl.multiple_of(col * width, width), width), :].T
        bit = lax.rem(row, 2)
        for j in range(window):
            own = (row == (first_block + j) % rows).astype(F32)
            total[j] = own * rhs - total[j]
        for j in range(window):
            early = keep_first.shape[0]
            keep, send = (keep_first, send_first) if j < early else (keep_rest, send_rest)
            at = j if j < early else j - early
            for piece in range(groups * window // 2):
                mine = pl.multiple_of((2 * piece + bit) * part, part)
                other = pl.multiple_of((2 * piece + 1 - bit) * part, part)
                keep[at, piece] = total[j, pl.ds(mine, part), :]
                send[at, piece] = total[j, pl.ds(other, part), :]


def window_kernel(window, tiles, least, factor_ref, *outs):
    member = lax.rem(lax.axis_index("row"), window)
    order = outs[0].shape[0]
    for ahead, out in enumerate(outs, least):
        j = jnp.minimum(member + ahead, window - 1)
        for t in range(tiles):
            out[:, t * LANES : (t + 1) * LANES] = factor_ref[
                pl.ds(t * window + j, order, stride=tiles * window), :
            ]


def dot(left, right):
    return jnp.dot(left, right, precision=lax.Precision.HIGH, preferred_element_type=F32)


def gather_col(block):
    size = lax.axis_size("col")
    col = lax.axis_index("col")
    held, mask = block, 1
    while mask < size:
        other = lax.ppermute(held, "col", swap_pairs(size, mask))
        first = (col & mask) == 0
        held = jnp.concatenate([jnp.where(first, held, other), jnp.where(first, other, held)], axis=1)
        mask *= 2
    return held


def on_device(factor, knowns, inverse):
    rows = lax.axis_size("row")
    row = lax.axis_index("row")
    col = lax.axis_index("col")
    _, blocks, order, window, width = factor.shape
    sources = knowns.shape[-1]
    first_block = blocks * rows - window
    tiles = width // LANES
    groups = rows // window
    part = sources // rows
    solver = (first_block % rows) // window
    member = row % window
    slot = first_block // rows
    base_row = solver * window
    row_stride = tiles * window
    flat = factor_rows(factor[0])
    own_knowns = knowns[0]

    cuts = 4

    def window_blocks(count):
        return pl.pallas_call(
            functools.partial(window_kernel, window, tiles, 1),
            grid=(cuts,),
            in_specs=[pl.BlockSpec((order // cuts * row_stride, LANES), lambda i: (slot * cuts + i, 0))],
            out_specs=[pl.BlockSpec((order // cuts, width), lambda i: (i, 0))] * count,
            out_shape=[jax.ShapeDtypeStruct((order, width), F32)] * count,
            compiler_params=pltpu.CompilerParams(vmem_limit_bytes=40 << 20),
        )(flat)

    def among(pairs, payload):
        return lax.ppermute(payload, "row", [(base_row + a, base_row + b) for a, b in pairs])

    early = 1
    top = order // 2
    next_block, *far_blocks = window_blocks(window - 1)
    with jax.named_scope("next_blocks"):
        near = among([(0, 1), (1, 0), (2, 3)], next_block)
        far = among([(0, 2), (1, 3), (2, 0)], next_block)

    half = groups * window // 2
    first_shape = jax.ShapeDtypeStruct((early, half, part, width), F32)
    rest_shape = jax.ShapeDtypeStruct((window - early, half, part, width), F32)
    whole = lambda shape: pl.BlockSpec(shape.shape, lambda i: (0,) * len(shape.shape))
    send0, keep0, send1, keep1 = pl.pallas_call(
        functools.partial(prefix_kernel, (rows, window, tiles, first_block), groups, part),
        grid=(blocks,),
        in_specs=[
            pl.BlockSpec((order, sources), lambda i: (i, 0)),
            pl.BlockSpec((order * row_stride, LANES), lambda i: (i, 0)),
        ],
        out_specs=[whole(first_shape), whole(first_shape), whole(rest_shape), whole(rest_shape)],
        out_shape=[first_shape, first_shape, rest_shape, rest_shape],
        scratch_shapes=[pltpu.VMEM((window, sources, width), F32)],
        compiler_params=pltpu.CompilerParams(vmem_limit_bytes=48 << 20),
        cost_estimate=pl.CostEstimate(
            flops=6 * flat.size * sources, bytes_accessed=4 * (flat.size + own_knowns.size), transcendentals=0
        ),
    )(own_knowns.reshape(blocks * order, sources), flat)

    send0, keep0, send1, keep1, near, far = lax.optimization_barrier((send0, keep0, send1, keep1, near, far))
    with jax.named_scope("next_blocks_relay"):
        near2 = among([(0, 1), (2, 3), (3, 2)], far[:top])
        far2 = among([(0, 2), (1, 3), (3, 1)], near[top:])
    def reduce_rows(send, keep, beside=()):
        total = keep + lax.ppermute(send, "row", swap_pairs(rows, 1))
        mask = 2
        while mask < window:
            total = total.reshape(total.shape[0], -1, 2, part, width)
            bit = (row // mask) % 2
            keep = jnp.where(bit == 0, total[:, :, 0], total[:, :, 1])
            send = jnp.where(bit == 0, total[:, :, 1], total[:, :, 0])
            total = keep + lax.ppermute(send, "row", swap_pairs(rows, mask))
            mask *= 2
        mask = 1
        while mask < groups:
            pairs = []
            for group in range(groups):
                apart = group ^ solver
                if apart & mask and not apart & (mask - 1):
                    pairs += [(group * window + k, (group ^ mask) * window + k) for k in range(window)]
            moved, *beside = lax.optimization_barrier((lax.ppermute(total, "row", pairs), *beside))
            total = total + moved
            mask *= 2
        return total.reshape(total.shape[0], groups * part, width), beside

    with jax.named_scope("reduce_first"):
        first, (near2, far2) = reduce_rows(send0, keep0, (near2, far2))
    with jax.named_scope("reduce_rest"):
        rest, _ = reduce_rows(send1, keep1)
    residual = [*first, *rest]

    with jax.named_scope("pick"):
        third = jnp.concatenate([near2, far2])

        def pick(*options):
            out = options[-1]
            for place in range(window - 1):
                out = jnp.where(member == place, options[place], out)
            return out

        above = [
            pick(next_block, near, far, third),
            pick(near, next_block, third, far),
            pick(far, third, next_block, near),
        ]
    def far_terms(owner, x):
        others = [k for k in range(window) if k != owner]
        shares = jnp.concatenate([x] + [among([(k, owner)], x) for k in others])
        blocks_here = far_blocks[: window - 2 - owner]
        terms = dot(shares, jnp.concatenate(blocks_here, axis=1)).reshape(window, x.shape[0], -1)
        total = jnp.where(member == owner, terms[0], 0.0)
        for at, k in enumerate(others, 1):
            total = total + among([(owner, k)], terms[at])
        return [total[:, at * width : (at + 1) * width] for at in range(len(blocks_here))]

    solved = []
    for j in range(window):
        with jax.named_scope(f"solve{j}"):
            solved.append(dot(gather_col(residual[j]), inverse[j]))
            if j + 1 == window:
                break
            x = gather_col(solved[j])
        if j + 2 < window:
            with jax.named_scope(f"far{j}"):
                for k, term in enumerate(far_terms(j, x), j + 2):
                    residual[k] = residual[k] - term
        with jax.named_scope(f"next{j}"):
            residual[j + 1] = residual[j + 1] - dot(x, above[j])

    stacked = jnp.stack(solved).reshape(window, groups, part, width)
    result = stacked[:, solver]
    for group in range(groups):
        if group != solver:
            pairs = [(base_row + k, group * window + k) for k in range(window)]
            moved = lax.ppermute(stacked[:, group], "row", pairs)
            result = jnp.where(row // window == group, moved, result)
    return result.transpose(0, 2, 1)


def solution(mesh):
    return jax.shard_map(
        on_device,
        mesh=mesh,
        in_specs=(
            P("row", None, None, None, "col"),
            P("row", None, None, None),
            P(None, None, "col"),
        ),
        out_specs=P(None, "col", "row"),
        check_vma=False,
    )
```

time: 209 us -> 159 us (0.76)
  the two profiles are of different devices: /device:TPU:12 before, /device:TPU:0 now
where the time goes in v2:
time: 159 us; the launch traced here: 156 us
  waiting for transfers between devices  64.8 us (41%)
  starting transfers between devices  41.8 us (26%)
  Pallas kernels  33.9 us (21%)
  local copies, waits for them, and re-layouts  7.03 us (4%)
  matrix products  5.48 us (3%)
  other arithmetic  2.22 us (1%)
    pallas_call x1, Pallas kernels, on_device(): pl.pallas_call(functools.partial(prefix_kernel, (rows, window, tiles, fir...  30.7 us
    ppermute x14, waiting for transfers between devices, gather_col(): other = lax.ppermute(held, 'col', swap_pairs(size, mask))  28.1 us
    ppermute x1, waiting for transfers between devices, on_device(): moved = lax.ppermute(stacked[:, group], 'row', pairs)  27.9 us
    ppermute x2, starting transfers between devices, reduce_rows(): lax.ppermute(total, 'row', pairs)  15.9 us
    ppermute x16, starting transfers between devices, among(): lax.ppermute(payload, 'row', [(base_row + a, base_row + b) for a, b in pa...  12.5 us
    ppermute x14, starting transfers between devices, gather_col(): other = lax.ppermute(held, 'col', swap_pairs(size, mask))  5.66 us
    dot_general x9, matrix products, dot(): jnp.dot(left, right, precision=lax.Precision.HIGH, preferred_element_type...  5.48 us
    ppermute x2, waiting for transfers between devices, reduce_rows(): lax.ppermute(total, 'row', pairs)  4.43 us
  transfers between devices with their start and end apart: 37, of which 16 were waited for; matrix products, arithmetic and copies ran while one was open for 7% of the time, Pallas kernels for 20%

profile of v2, /device:TPU:0, one launch (start us, length us, event | category | flops | bytes accessed | tf_op | source)
XLA Modules:
  0.0 155.9 jit_solution(12929739718485676354)
XLA Ops:
  0.0 3.2 %shard_map.38 = (f32[1024,256]{1,0:T(8,128)S(1)}, f32[1024,256]{1,0:T(8,128)S(1)}, f32[1024,256]{1,0:T(8,128)S(1)}) custom-call(f32[98304,128]{1,0:T(8,128)} %bitcast.86), custom_call_target="tpu_custom_call" | custom-call | tf_op jit(solution)/shard_map/pallas_call | solution.py:132
  3.2 1.0 copy-done
  4.2 0.7 collective-permute-start.1
  4.9 0.7 collective-permute-start
  5.7 30.7 %shard_map.37 = (f32[1,4,32,256]{3,2,1,0:T(8,128)S(1)}, f32[1,4,32,256]{3,2,1,0:T(8,128)S(1)}, f32[3,4,32,256]{3,2,1,0:T(8,128)S(1)}, f32[3,4,32,256]{3,2,1,0:T(8,128)S(1)}) custom-call(f32[12288,256]{1,0:T(8,128)} %bitcast.97, f32[98304,128]{1,0:T(8,128)} %bitcast.87), custom_call_target="tpu_custom_call" | custom-call | flops 19327352832 | bytes 62914560 | tf_op jit(solution)/shard_map/pallas_call | solution.py:155
  36.4 3.0 %collective-permute-start.2 = (f32[1,4,32,256]{3,2,1,0:T(8,128)S(1)}, f32[1,4,32,256]{3,2,1,0:T(8,128)}, u32[]{:S(2)}, u32[]{:S(2)}) collective-permute-start(f32[1,4,32,256]{3,2,1,0:T(8,128)S(1)} %get-tuple-element.27), channel_id=1, source_target_pairs={{0,4},{4,0},{8,12},{12,8},{16,20},{20,16},{24,28},{28,24},{1,5},{5... | collective-permute-start | bytes 393224 | tf_op jit(solution)/shard_map/reduce_first/ppermute | solution.py:176
  39.5 1.2 collective-permute-start.9
  40.7 3.2 %collective-permute-done.2 = f32[1,4,32,256]{3,2,1,0:T(8,128)} collective-permute-done((f32[1,4,32,256]{3,2,1,0:T(8,128)S(1)}, f32[1,4,32,256]{3,2,1,0:T(8,128)}, u32[]{:S(2)}, u32[]{:S(2)}) %collective-permute-start.2) | collective-permute-done | bytes 131104 | tf_op jit(solution)/shard_map/reduce_first/ppermute | solution.py:176
  43.9 0.9 add.47
  44.9 2.2 %collective-permute-start.3 = (f32[1,2,32,256]{3,2,1,0:T(8,128)S(1)}, f32[1,2,32,256]{3,2,1,0:T(8,128)S(1)}, u32[]{:S(2)}, u32[]{:S(2)}) collective-permute-start(f32[1,2,32,256]{3,2,1,0:T(8,128)S(1)} %select_bitcast_fusion.1), channel_id=1, source_target_pairs={{0,8},{4,12},{8,0},{12,4},{16,24},{20,28},{24,16},{28,20},{1,9},{5... | collective-permute-start | bytes 196616 | tf_op jit(solution)/shard_map/reduce_first/ppermute | solution.py:183
  47.0 1.9 %slice.83 = f32[512,256]{1,0:T(8,128)} slice(f32[1024,256]{1,0:T(8,128)} %copy-done.2), slice={[0:512], [0:256]} | slice | bytes 1048576 | tf_op jit(solution)/shard_map/next_blocks_relay/slice | solution.py:173
  48.9 1.9 %slice.84 = f32[512,256]{1,0:T(8,128)} slice(f32[1024,256]{1,0:T(8,128)} %copy-done.4), slice={[512:1024], [0:256]} | slice | bytes 1048576 | tf_op jit(solution)/shard_map/next_blocks_relay/slice | solution.py:174
  50.8 1.5 collective-permute-start.6
  52.3 1.5 collective-permute-start.5
  53.8 10.8 %collective-permute-start.4 = (f32[1,2,32,256]{3,2,1,0:T(8,128)S(1)}, f32[1,2,32,256]{3,2,1,0:T(8,128)S(1)}, u32[]{:S(2)}, u32[]{:S(2)}) collective-permute-start(f32[1,2,32,256]{3,2,1,0:T(8,128)S(1)} %fusion.81), channel_id=1, source_target_pairs={{0,16},{4,20},{8,24},{12,28},{1,17},{5,21},{9,25},{13,29},{2,18},{... | collective-permute-start | bytes 196616 | tf_op jit(solution)/shard_map/reduce_first/ppermute | solution.py:192
  64.8 1.7 %collective-permute-done.4 = f32[1,2,32,256]{3,2,1,0:T(8,128)S(1)} collective-permute-done((f32[1,2,32,256]{3,2,1,0:T(8,128)S(1)}, f32[1,2,32,256]{3,2,1,0:T(8,128)S(1)}, u32[]{:S(2)}, u32[]{:S(2)}) %collective-permute-start.4) | collective-permute-done | bytes 65568 | tf_op jit(solution)/shard_map/reduce_first/ppermute | solution.py:192
  66.5 1.1 constant_dynamic-update-slice_fusion.1
  67.8 1.6 collective-permute-start.8
  69.4 1.1 collective-permute-done.10
  70.5 5.1 %collective-permute-start.11 = (f32[3,2,32,256]{3,2,1,0:T(8,128)S(1)}, f32[3,2,32,256]{3,2,1,0:T(8,128)S(1)}, u32[]{:S(2)}, u32[]{:S(2)}) collective-permute-start(f32[3,2,32,256]{3,2,1,0:T(8,128)S(1)} %fusion.68), channel_id=1, source_target_pairs={{0,16},{4,20},{8,24},{12,28},{1,17},{5,21},{9,25},{13,29},{2,18},{... | collective-permute-start | bytes 589832 | tf_op jit(solution)/shard_map/reduce_rest/ppermute | solution.py:192
  76.2 1.1 constant_dynamic-update-slice_fusion
  77.3 2.8 %collective-permute-done.11 = f32[3,2,32,256]{3,2,1,0:T(8,128)S(1)} collective-permute-done((f32[3,2,32,256]{3,2,1,0:T(8,128)S(1)}, f32[3,2,32,256]{3,2,1,0:T(8,128)S(1)}, u32[]{:S(2)}, u32[]{:S(2)}) %collective-permute-start.11) | collective-permute-done | bytes 196640 | tf_op jit(solution)/shard_map/reduce_rest/ppermute | solution.py:192
  80.7 4.4 %collective-permute-done.13 = f32[64,512]{1,0:T(8,128)S(1)} collective-permute-done((f32[64,512]{1,0:T(8,128)S(1)}, f32[64,512]{1,0:T(8,128)S(1)}, u32[]{:S(2)}, u32[]{:S(2)}) %collective-permute-start.13) | collective-permute-done | bytes 131104 | tf_op jit(solution)/shard_map/solve0/ppermute | solution.py:104
  85.9 1.2 collective-permute-done.14
  87.8 0.7 collective-permute-start.17
  88.5 0.7 collective-permute-start.16
  89.2 0.7 collective-permute-start.18
  89.9 2.9 %collective-permute-done.15 = f32[64,512]{1,0:T(8,128)S(1)} collective-permute-done((f32[64,512]{1,0:T(8,128)S(1)}, f32[64,512]{1,0:T(8,128)S(1)}, u32[]{:S(2)}, u32[]{:S(2)}) %collective-permute-start.15) | collective-permute-done | bytes 131104 | tf_op jit(solution)/shard_map/solve1/ppermute | solution.py:104
  93.4 1.2 fusion
  94.6 0.7 collective-permute-start.19
  95.3 0.7 collective-permute-start.21
  96.0 0.7 collective-permute-start.20
  97.4 5.3 %collective-permute-done.23 = f32[64,512]{1,0:T(8,128)S(1)} collective-permute-done((f32[64,512]{1,0:T(8,128)S(1)}, f32[64,512]{1,0:T(8,128)S(1)}, u32[]{:S(2)}, u32[]{:S(2)}) %collective-permute-start.23) | collective-permute-done | bytes 131104 | tf_op jit(solution)/shard_map/solve1/ppermute | solution.py:104
  102.7 0.7 fusion.79
  103.4 1.2 collective-permute-done.24
  105.3 0.7 collective-permute-start.27
  106.0 0.7 collective-permute-start.26
  106.7 0.7 collective-permute-start.28
  107.4 2.9 %collective-permute-done.25 = f32[64,512]{1,0:T(8,128)S(1)} collective-permute-done((f32[64,512]{1,0:T(8,128)S(1)}, f32[64,512]{1,0:T(8,128)S(1)}, u32[]{:S(2)}, u32[]{:S(2)}) %collective-permute-start.25) | collective-permute-done | bytes 131104 | tf_op jit(solution)/shard_map/solve2/ppermute | solution.py:104
  112.8 0.7 collective-permute-start.29
  113.4 0.7 collective-permute-start.31
  114.1 0.7 collective-permute-start.30
  114.8 3.0 %collective-permute-done.33 = f32[64,512]{1,0:T(8,128)S(1)} collective-permute-done((f32[64,512]{1,0:T(8,128)S(1)}, f32[64,512]{1,0:T(8,128)S(1)}, u32[]{:S(2)}, u32[]{:S(2)}) %collective-permute-start.33) | collective-permute-done | bytes 131104 | tf_op jit(solution)/shard_map/solve2/ppermute | solution.py:104
  118.6 1.2 collective-permute-done.34
  120.4 5.0 %collective-permute-done.35 = f32[64,512]{1,0:T(8,128)S(1)} collective-permute-done((f32[64,512]{1,0:T(8,128)S(1)}, f32[64,512]{1,0:T(8,128)S(1)}, u32[]{:S(2)}, u32[]{:S(2)}) %collective-permute-start.35) | collective-permute-done | bytes 131104 | tf_op jit(solution)/shard_map/solve3/ppermute | solution.py:104
  126.0 1.3 collective-permute-start.36
  127.3 27.9 %collective-permute-done.36 = f32[4,32,256]{2,1,0:T(8,128)S(1)} collective-permute-done((f32[4,32,256]{2,1,0:T(8,128)S(1)}, f32[4,32,256]{2,1,0:T(8,128)S(1)}, u32[]{:S(2)}, u32[]{:S(2)}) %collective-permute-start.36) | collective-permute-done | bytes 131104 | tf_op jit(solution)/shard_map/ppermute | solution.py:246
  155.2 0.7 fusion.70
  (94 shorter events, 9.4 us)
Async XLA Ops:
  3.2 1.0 copy-start
  4.2 32.2 %collective-permute-start.1 = (f32[1024,256]{1,0:T(8,128)S(1)}, f32[1024,256]{1,0:T(8,128)S(1)}, u32[]{:S(2)}, u32[]{:S(2)}) collective-permute-start(f32[1024,256]{1,0:T(8,128)S(1)} %get-tuple-element.25), channel_id=1, source_target_pairs={{16,24},{20,28},{24,16},{17,25},{21,29},{25,17},{18,26},{22,30},{2... | collective-permute-start | bytes 3145736 | tf_op jit(solution)/shard_map/next_blocks/ppermute | solution.py:142
  4.9 31.5 %collective-permute-start = (f32[1024,256]{1,0:T(8,128)S(1)}, f32[1024,256]{1,0:T(8,128)S(1)}, u32[]{:S(2)}, u32[]{:S(2)}) collective-permute-start(f32[1024,256]{1,0:T(8,128)S(1)} %get-tuple-element.25), channel_id=1, source_target_pairs={{16,20},{20,16},{24,28},{17,21},{21,17},{25,29},{18,22},{22,18},{2... | collective-permute-start | bytes 3145736 | tf_op jit(solution)/shard_map/next_blocks/ppermute | solution.py:142
  36.4 3.1 %copy-start.2 = (f32[1024,256]{1,0:T(8,128)}, f32[1024,256]{1,0:T(8,128)S(1)}, u32[]{:S(2)}) copy-start(f32[1024,256]{1,0:T(8,128)S(1)} %collective-permute-done.1) | copy-start | bytes 3145732
  36.4 3.0 %copy-start.4 = (f32[1024,256]{1,0:T(8,128)}, f32[1024,256]{1,0:T(8,128)S(1)}, u32[]{:S(2)}) copy-start(f32[1024,256]{1,0:T(8,128)S(1)} %collective-permute-done) | copy-start | bytes 3145732
  36.4 7.5 %collective-permute-start.2 = (f32[1,4,32,256]{3,2,1,0:T(8,128)S(1)}, f32[1,4,32,256]{3,2,1,0:T(8,128)}, u32[]{:S(2)}, u32[]{:S(2)}) collective-permute-start(f32[1,4,32,256]{3,2,1,0:T(8,128)S(1)} %get-tuple-element.27), channel_id=1, source_target_pairs={{0,4},{4,0},{8,12},{12,8},{16,20},{20,16},{24,28},{28,24},{1,5},{5... | collective-permute-start | bytes 393224 | tf_op jit(solution)/shard_map/reduce_first/ppermute | solution.py:176
  39.5 25.1 %collective-permute-start.9 = (f32[3,4,32,256]{3,2,1,0:T(8,128)S(1)}, f32[3,4,32,256]{3,2,1,0:T(8,128)S(1)}, u32[]{:S(2)}, u32[]{:S(2)}) collective-permute-start(f32[3,4,32,256]{3,2,1,0:T(8,128)S(1)} %get-tuple-element.32), channel_id=1, source_target_pairs={{0,4},{4,0},{8,12},{12,8},{16,20},{20,16},{24,28},{28,24},{1,5},{5... | collective-permute-start | bytes 1179656 | tf_op jit(solution)/shard_map/reduce_rest/ppermute | solution.py:176
  44.9 8.9 %collective-permute-start.3 = (f32[1,2,32,256]{3,2,1,0:T(8,128)S(1)}, f32[1,2,32,256]{3,2,1,0:T(8,128)S(1)}, u32[]{:S(2)}, u32[]{:S(2)}) collective-permute-start(f32[1,2,32,256]{3,2,1,0:T(8,128)S(1)} %select_bitcast_fusion.1), channel_id=1, source_target_pairs={{0,8},{4,12},{8,0},{12,4},{16,24},{20,28},{24,16},{28,20},{1,9},{5... | collective-permute-start | bytes 196616 | tf_op jit(solution)/shard_map/reduce_first/ppermute | solution.py:183
  50.8 15.7 %collective-permute-start.6 = (f32[512,256]{1,0:T(8,128)}, f32[512,256]{1,0:T(8,128)}, u32[]{:S(2)}, u32[]{:S(2)}) collective-permute-start(f32[512,256]{1,0:T(8,128)} %slice.84), channel_id=1, source_target_pairs={{16,24},{20,28},{28,20},{17,25},{21,29},{29,21},{18,26},{22,30},{3... | collective-permute-start | bytes 1572872 | tf_op jit(solution)/shard_map/next_blocks_relay/ppermute | solution.py:142
  52.3 14.2 %collective-permute-start.5 = (f32[512,256]{1,0:T(8,128)}, f32[512,256]{1,0:T(8,128)}, u32[]{:S(2)}, u32[]{:S(2)}) collective-permute-start(f32[512,256]{1,0:T(8,128)} %slice.83), channel_id=1, source_target_pairs={{16,20},{24,28},{28,24},{17,21},{25,29},{29,25},{18,22},{26,30},{3... | collective-permute-start | bytes 1572872 | tf_op jit(solution)/shard_map/next_blocks_relay/ppermute | solution.py:142
  53.7 21.9 %copy-start.6 = (f32[4,1024,256]{2,1,0:T(8,128)S(1)}, f32[4,1024,256]{2,1,0:T(8,128)}, u32[]{:S(2)}) copy-start(f32[4,1024,256]{2,1,0:T(8,128)} %param.5) | copy-start | bytes 12582916
  53.8 12.7 %collective-permute-start.4 = (f32[1,2,32,256]{3,2,1,0:T(8,128)S(1)}, f32[1,2,32,256]{3,2,1,0:T(8,128)S(1)}, u32[]{:S(2)}, u32[]{:S(2)}) collective-permute-start(f32[1,2,32,256]{3,2,1,0:T(8,128)S(1)} %fusion.81), channel_id=1, source_target_pairs={{0,16},{4,20},{8,24},{12,28},{1,17},{5,21},{9,25},{13,29},{2,18},{... | collective-permute-start | bytes 196616 | tf_op jit(solution)/shard_map/reduce_first/ppermute | solution.py:192
  64.6 20.5 %copy-start.3 = (f32[1024,256]{1,0:T(8,128)S(1)}, f32[1024,256]{1,0:T(8,128)}, u32[]{:S(2)}) copy-start(f32[1024,256]{1,0:T(8,128)} %copy-done.2) | copy-start | bytes 3145732
  64.6 20.5 %copy-start.5 = (f32[1024,256]{1,0:T(8,128)S(1)}, f32[1024,256]{1,0:T(8,128)}, u32[]{:S(2)}) copy-start(f32[1024,256]{1,0:T(8,128)} %copy-done.4) | copy-start | bytes 3145732
  64.7 5.7 %collective-permute-start.10 = (f32[3,2,32,256]{3,2,1,0:T(8,128)S(1)}, f32[3,2,32,256]{3,2,1,0:T(8,128)S(1)}, u32[]{:S(2)}, u32[]{:S(2)}) collective-permute-start(f32[3,2,32,256]{3,2,1,0:T(8,128)S(1)} %select_bitcast_fusion), channel_id=1, source_target_pairs={{0,8},{4,12},{8,0},{12,4},{16,24},{20,28},{24,16},{28,20},{1,9},{5... | collective-permute-start | bytes 589832 | tf_op jit(solution)/shard_map/reduce_rest/ppermute | solution.py:183
  66.5 1.3 collective-permute-start.7
  67.8 7.8 %collective-permute-start.8 = (f32[64,512]{1,0:T(8,128)S(1)}, f32[64,512]{1,0:T(8,128)S(1)}, u32[]{:S(2)}, u32[]{:S(2)}) collective-permute-start(f32[64,512]{1,0:T(8,128)S(1)} %pad_maximum_fusion.4), channel_id=1, source_target_pairs={{0,2},{1,3},{2,0},{3,1},{4,6},{5,7},{6,4},{7,5},{8,10},{9,11},{10,... | collective-permute-start | bytes 393224 | tf_op jit(solution)/shard_map/solve0/ppermute | solution.py:104
  70.5 9.6 %collective-permute-start.11 = (f32[3,2,32,256]{3,2,1,0:T(8,128)S(1)}, f32[3,2,32,256]{3,2,1,0:T(8,128)S(1)}, u32[]{:S(2)}, u32[]{:S(2)}) collective-permute-start(f32[3,2,32,256]{3,2,1,0:T(8,128)S(1)} %fusion.68), channel_id=1, source_target_pairs={{0,16},{4,20},{8,24},{12,28},{1,17},{5,21},{9,25},{13,29},{2,18},{... | collective-permute-start | bytes 589832 | tf_op jit(solution)/shard_map/reduce_rest/ppermute | solution.py:192
  76.1 3.9 %collective-permute-start.12 = (f32[64,256]{1,0:T(8,128)S(1)}, f32[64,256]{1,0:T(8,128)S(1)}, u32[]{:S(2)}, u32[]{:S(2)}) collective-permute-start(f32[64,256]{1,0:T(8,128)S(1)} %fusion.28), channel_id=1, source_target_pairs={{0,1},{1,0},{2,3},{3,2},{4,5},{5,4},{6,7},{7,6},{8,9},{9,8},{10,11... | collective-permute-start | bytes 196616 | tf_op jit(solution)/shard_map/solve0/ppermute | solution.py:104
  80.1 13.3 %copy-start.1 = (f32[1024,256]{1,0:T(8,128)S(1)}, f32[1024,256]{1,0:T(8,128)}, u32[]{:S(2)}) copy-start(f32[1024,256]{1,0:T(8,128)} %copy-done) | copy-start | bytes 3145732
  80.1 5.0 %collective-permute-start.13 = (f32[64,512]{1,0:T(8,128)S(1)}, f32[64,512]{1,0:T(8,128)S(1)}, u32[]{:S(2)}, u32[]{:S(2)}) collective-permute-start(f32[64,512]{1,0:T(8,128)S(1)} %pad_maximum_fusion.5), channel_id=1, source_target_pairs={{0,2},{1,3},{2,0},{3,1},{4,6},{5,7},{6,4},{7,5},{8,10},{9,11},{10,... | collective-permute-start | bytes 393224 | tf_op jit(solution)/shard_map/solve0/ppermute | solution.py:104
  85.8 1.3 collective-permute-start.14
  87.2 5.6 %collective-permute-start.15 = (f32[64,512]{1,0:T(8,128)S(1)}, f32[64,512]{1,0:T(8,128)S(1)}, u32[]{:S(2)}, u32[]{:S(2)}) collective-permute-start(f32[64,512]{1,0:T(8,128)S(1)} %pad_maximum_fusion.6), channel_id=1, source_target_pairs={{0,2},{1,3},{2,0},{3,1},{4,6},{5,7},{6,4},{7,5},{8,10},{9,11},{10,... | collective-permute-start | bytes 393224 | tf_op jit(solution)/shard_map/solve1/ppermute | solution.py:104
  87.8 5.6 %collective-permute-start.17 = (f32[64,1024]{1,0:T(8,128)S(1)}, f32[64,1024]{1,0:T(8,128)S(1)}, u32[]{:S(2)}, u32[]{:S(2)}) collective-permute-start(f32[64,1024]{1,0:T(8,128)S(1)} %pad_maximum_fusion), channel_id=1, source_target_pairs={{24,16},{25,17},{26,18},{27,19}} | collective-permute-start | bytes 786440 | tf_op jit(solution)/shard_map/far0/ppermute | solution.py:142
  88.5 4.9 %collective-permute-start.16 = (f32[64,1024]{1,0:T(8,128)S(1)}, f32[64,1024]{1,0:T(8,128)S(1)}, u32[]{:S(2)}, u32[]{:S(2)}) collective-permute-start(f32[64,1024]{1,0:T(8,128)S(1)} %pad_maximum_fusion), channel_id=1, source_target_pairs={{20,16},{21,17},{22,18},{23,19}} | collective-permute-start | bytes 786440 | tf_op jit(solution)/shard_map/far0/ppermute | solution.py:142
  89.2 4.2 %collective-permute-start.18 = (f32[64,1024]{1,0:T(8,128)S(1)}, f32[64,1024]{1,0:T(8,128)S(1)}, u32[]{:S(2)}, u32[]{:S(2)}) collective-permute-start(f32[64,1024]{1,0:T(8,128)S(1)} %pad_maximum_fusion), channel_id=1, source_target_pairs={{28,16},{29,17},{30,18},{31,19}} | collective-permute-start | bytes 786440 | tf_op jit(solution)/shard_map/far0/ppermute | solution.py:142
  93.3 3.4 %collective-permute-start.22 = (f32[64,256]{1,0:T(8,128)S(1)}, f32[64,256]{1,0:T(8,128)S(1)}, u32[]{:S(2)}, u32[]{:S(2)}) collective-permute-start(f32[64,256]{1,0:T(8,128)S(1)} %fusion.26), channel_id=1, source_target_pairs={{0,1},{1,0},{2,3},{3,2},{4,5},{5,4},{6,7},{7,6},{8,9},{9,8},{10,11... | collective-permute-start | bytes 196616 | tf_op jit(solution)/shard_map/solve1/ppermute | solution.py:104
  94.6 2.7 %collective-permute-start.19 = (f32[64,512]{1,0:T(8,128)S(1)}, f32[64,512]{1,0:T(8,128)S(1)}, u32[]{:S(2)}, u32[]{:S(2)}) collective-permute-start(f32[64,512]{1,0:T(8,128)S(1)} %get-tuple-element.37), channel_id=1, source_target_pairs={{16,20},{17,21},{18,22},{19,23}} | collective-permute-start | bytes 393224 | tf_op jit(solution)/shard_map/far0/ppermute | solution.py:142
  95.3 2.0 %collective-permute-start.21 = (f32[64,512]{1,0:T(8,128)S(1)}, f32[64,512]{1,0:T(8,128)S(1)}, u32[]{:S(2)}, u32[]{:S(2)}) collective-permute-start(f32[64,512]{1,0:T(8,128)S(1)} %get-tuple-element.38), channel_id=1, source_target_pairs={{16,28},{17,29},{18,30},{19,31}} | collective-permute-start | bytes 393224 | tf_op jit(solution)/shard_map/far0/ppermute | solution.py:142
  96.0 1.3 collective-permute-start.20
  96.7 5.9 %collective-permute-start.23 = (f32[64,512]{1,0:T(8,128)S(1)}, f32[64,512]{1,0:T(8,128)S(1)}, u32[]{:S(2)}, u32[]{:S(2)}) collective-permute-start(f32[64,512]{1,0:T(8,128)S(1)} %pad_maximum_fusion.7), channel_id=1, source_target_pairs={{0,2},{1,3},{2,0},{3,1},{4,6},{5,7},{6,4},{7,5},{8,10},{9,11},{10,... | collective-permute-start | bytes 393224 | tf_op jit(solution)/shard_map/solve1/ppermute | solution.py:104
  103.3 1.3 collective-permute-start.24
  104.7 5.6 %collective-permute-start.25 = (f32[64,512]{1,0:T(8,128)S(1)}, f32[64,512]{1,0:T(8,128)S(1)}, u32[]{:S(2)}, u32[]{:S(2)}) collective-permute-start(f32[64,512]{1,0:T(8,128)S(1)} %pad_maximum_fusion.8), channel_id=1, source_target_pairs={{0,2},{1,3},{2,0},{3,1},{4,6},{5,7},{6,4},{7,5},{8,10},{9,11},{10,... | collective-permute-start | bytes 393224 | tf_op jit(solution)/shard_map/solve2/ppermute | solution.py:104
  105.3 5.6 %collective-permute-start.27 = (f32[64,1024]{1,0:T(8,128)S(1)}, f32[64,1024]{1,0:T(8,128)S(1)}, u32[]{:S(2)}, u32[]{:S(2)}) collective-permute-start(f32[64,1024]{1,0:T(8,128)S(1)} %pad_maximum_fusion.1), channel_id=1, source_target_pairs={{24,20},{25,21},{26,22},{27,23}} | collective-permute-start | bytes 786440 | tf_op jit(solution)/shard_map/far1/ppermute | solution.py:142
  106.0 4.9 %collective-permute-start.26 = (f32[64,1024]{1,0:T(8,128)S(1)}, f32[64,1024]{1,0:T(8,128)S(1)}, u32[]{:S(2)}, u32[]{:S(2)}) collective-permute-start(f32[64,1024]{1,0:T(8,128)S(1)} %pad_maximum_fusion.1), channel_id=1, source_target_pairs={{16,20},{17,21},{18,22},{19,23}} | collective-permute-start | bytes 786440 | tf_op jit(solution)/shard_map/far1/ppermute | solution.py:142
  106.7 4.2 %collective-permute-start.28 = (f32[64,1024]{1,0:T(8,128)S(1)}, f32[64,1024]{1,0:T(8,128)S(1)}, u32[]{:S(2)}, u32[]{:S(2)}) collective-permute-start(f32[64,1024]{1,0:T(8,128)S(1)} %pad_maximum_fusion.1), channel_id=1, source_target_pairs={{28,20},{29,21},{30,22},{31,23}} | collective-permute-start | bytes 786440 | tf_op jit(solution)/shard_map/far1/ppermute | solution.py:142
  110.8 1.3 collective-permute-start.32
  112.1 5.6 %collective-permute-start.33 = (f32[64,512]{1,0:T(8,128)S(1)}, f32[64,512]{1,0:T(8,128)S(1)}, u32[]{:S(2)}, u32[]{:S(2)}) collective-permute-start(f32[64,512]{1,0:T(8,128)S(1)} %pad_maximum_fusion.9), channel_id=1, source_target_pairs={{0,2},{1,3},{2,0},{3,1},{4,6},{5,7},{6,4},{7,5},{8,10},{9,11},{10,... | collective-permute-start | bytes 393224 | tf_op jit(solution)/shard_map/solve2/ppermute | solution.py:104
  112.8 5.0 %collective-permute-start.29 = (f32[64,256]{1,0:T(8,128)S(1)}, f32[64,256]{1,0:T(8,128)S(1)}, u32[]{:S(2)}, u32[]{:S(2)}) collective-permute-start(f32[64,256]{1,0:T(8,128)S(1)} %get-tuple-element.46), channel_id=1, source_target_pairs={{20,16},{21,17},{22,18},{23,19}} | collective-permute-start | bytes 196616 | tf_op jit(solution)/shard_map/far1/ppermute | solution.py:142
  113.4 4.4 %collective-permute-start.31 = (f32[64,256]{1,0:T(8,128)S(1)}, f32[64,256]{1,0:T(8,128)S(1)}, u32[]{:S(2)}, u32[]{:S(2)}) collective-permute-start(f32[64,256]{1,0:T(8,128)S(1)} %get-tuple-element.47), channel_id=1, source_target_pairs={{20,28},{21,29},{22,30},{23,31}} | collective-permute-start | bytes 196616 | tf_op jit(solution)/shard_map/far1/ppermute | solution.py:142
  114.1 3.7 %collective-permute-start.30 = (f32[64,256]{1,0:T(8,128)S(1)}, f32[64,256]{1,0:T(8,128)S(1)}, u32[]{:S(2)}, u32[]{:S(2)}) collective-permute-start(f32[64,256]{1,0:T(8,128)S(1)} %get-tuple-element.48), channel_id=1, source_target_pairs={{20,24},{21,25},{22,26},{23,27}} | collective-permute-start | bytes 196616 | tf_op jit(solution)/shard_map/far1/ppermute | solution.py:142
  118.5 1.3 collective-permute-start.34
  119.8 5.6 %collective-permute-start.35 = (f32[64,512]{1,0:T(8,128)S(1)}, f32[64,512]{1,0:T(8,128)S(1)}, u32[]{:S(2)}, u32[]{:S(2)}) collective-permute-start(f32[64,512]{1,0:T(8,128)S(1)} %pad_maximum_fusion.10), channel_id=1, source_target_pairs={{0,2},{1,3},{2,0},{3,1},{4,6},{5,7},{6,4},{7,5},{8,10},{9,11},{10,... | collective-permute-start | bytes 393224 | tf_op jit(solution)/shard_map/solve3/ppermute | solution.py:104
  126.0 29.2 %collective-permute-start.36 = (f32[4,32,256]{2,1,0:T(8,128)S(1)}, f32[4,32,256]{2,1,0:T(8,128)S(1)}, u32[]{:S(2)}, u32[]{:S(2)}) collective-permute-start(f32[4,32,256]{2,1,0:T(8,128)S(1)} %slice_bitcast_fusion.1), channel_id=1, source_target_pairs={{16,0},{20,4},{24,8},{28,12},{17,1},{21,5},{25,9},{29,13},{18,2},{... | collective-permute-start | bytes 393224 | tf_op jit(solution)/shard_map/ppermute | solution.py:246

commit v3 on v2

v3 whole, which is shorter than its diff:
```python
import functools

import jax
import jax.numpy as jnp
from jax import lax
from jax.experimental import pallas as pl
from jax.experimental.pallas import tpu as pltpu
from jax.sharding import PartitionSpec as P

F32 = jnp.float32
BF16 = jnp.bfloat16
LANES = 128


def split(value):
    high = value.astype(BF16)
    return high, (value - high.astype(F32)).astype(BF16)


def dot3(left, right):
    product = functools.partial(jnp.dot, preferred_element_type=F32)
    return product(left[0], right[0]) + (product(left[1], right[0]) + product(left[0], right[1]))


def swap_pairs(size, mask):
    return [(i, i ^ mask) for i in range(size)]


def factor_rows(factor):
    blocks, order, window, width = factor.shape
    tiles = width // LANES
    view = factor.reshape(blocks * order, window, tiles, LANES).transpose(0, 2, 1, 3)
    return view.reshape(blocks * order * tiles * window, LANES)


def accumulate(dims, block, knowns_ref, factor_ref, total):
    rows, window, tiles, first_block = dims
    order = knowns_ref.shape[0]
    stride = tiles * window

    @pl.when(block * rows + lax.axis_index("row") < first_block)
    def _():
        known = split(knowns_ref[...].T)
        for j in range(window):
            pieces = [
                split(factor_ref[pl.ds(t * window + j, order, stride=stride), :]) for t in range(tiles)
            ]
            high = jnp.concatenate([p[0] for p in pieces], axis=1)
            low = jnp.concatenate([p[1] for p in pieces], axis=1)
            total[j] += dot3(known, (high, low))


def prefix_kernel(dims, part, sizes, knowns_ref, factor_ref, *refs):
    keeps, sends, total = refs[: len(sizes)], refs[len(sizes) : -1], refs[-1]
    rows, window, tiles, first_block = dims
    step = pl.program_id(0)
    row = lax.axis_index("row")
    col = lax.axis_index("col")
    width = tiles * LANES

    @pl.when(step == 0)
    def _():
        total[...] = jnp.zeros_like(total)

    accumulate(dims, step, knowns_ref, factor_ref, total)

    @pl.when(step == pl.num_programs(0) - 1)
    def _():
        rhs = knowns_ref[pl.ds(pl.multiple_of(col * width, width), width), :].T
        bit = lax.rem(row, 2)
        j = 0
        for keep, send, size in zip(keeps, sends, sizes):
            for at in range(size):
                own = (row == (first_block + j) % rows).astype(F32)
                total[j] = own * rhs - total[j]
                for piece in range(rows // 2):
                    mine = pl.multiple_of((2 * piece + bit) * part, part)
                    other = pl.multiple_of((2 * piece + 1 - bit) * part, part)
                    keep[at, piece] = total[j, pl.ds(mine, part), :]
                    send[at, piece] = total[j, pl.ds(other, part), :]
                j += 1


def window_kernel(window, tiles, least, factor_ref, *outs):
    member = lax.rem(lax.axis_index("row"), window)
    order = outs[0].shape[0]
    for ahead, out in enumerate(outs, least):
        j = jnp.minimum(member + ahead, window - 1)
        for t in range(tiles):
            out[:, t * LANES : (t + 1) * LANES] = factor_ref[
                pl.ds(t * window + j, order, stride=tiles * window), :
            ]


def dot(left, right):
    return jnp.dot(left, right, precision=lax.Precision.HIGH, preferred_element_type=F32)


def wait(event, arrays):
    return lax.optimization_barrier((event, *arrays))[1:]


def line_steps(count, target):
    below, above, steps = list(range(target)), list(range(count - 1, target, -1)), []
    while below or above:
        moves, taken = [], False
        for side in (below, above):
            pairs = [(side[at], side[at + 1]) for at in range(0, len(side) - 1, 2)]
            left = [to for _, to in pairs]
            if len(side) % 2:
                if taken:
                    left.append(side[-1])
                else:
                    pairs.append((side[-1], target))
                    taken = True
            moves += pairs
            side[:] = left
        steps.append(moves)
    return steps


def gather_col(block):
    return lax.all_gather(block, "col", axis=1, tiled=True)


def on_device(factor, knowns, inverse):
    rows = lax.axis_size("row")
    row = lax.axis_index("row")
    _, blocks, order, window, width = factor.shape
    sources = knowns.shape[-1]
    first_block = blocks * rows - window
    tiles = width // LANES
    part = sources // rows
    pieces = rows // 2
    slot = first_block // rows
    base_row = first_block % rows
    leader = row % 2 == 0
    row_stride = tiles * window
    flat = pltpu.with_memory_space_constraint(factor_rows(factor[0]), pltpu.HBM)
    own_knowns = knowns[0]
    cuts = 4

    ahead = pl.pallas_call(
        functools.partial(window_kernel, window, tiles, 1),
        grid=(cuts,),
        in_specs=[pl.BlockSpec((order // cuts * row_stride, LANES), lambda i: (slot * cuts + i, 0))],
        out_specs=[pl.BlockSpec((order // cuts, width), lambda i: (i, 0))] * (window - 1),
        out_shape=[jax.ShapeDtypeStruct((order, width), F32)] * (window - 1),
        compiler_params=pltpu.CompilerParams(vmem_limit_bytes=40 << 20),
    )(flat)

    def among(pairs, payload):
        return lax.ppermute(payload, "row", [(base_row + a, base_row + b) for a, b in pairs])

    with jax.named_scope("near1"):
        near = [among([(0, 1), (1, 0), (2, 3)], ahead[0])]
    with jax.named_scope("far"):
        far = among([(2, 0)], ahead[0])

    sizes = (1, 1, window - 2)
    shapes = [jax.ShapeDtypeStruct((size, pieces, part, width), F32) for size in sizes] * 2
    keeps_sends = pl.pallas_call(
        functools.partial(prefix_kernel, (rows, window, tiles, first_block), part, sizes),
        grid=(blocks,),
        in_specs=[
            pl.BlockSpec((order, sources), lambda i: (i, 0)),
            pl.BlockSpec((order * row_stride, LANES), lambda i: (i, 0)),
        ],
        out_specs=[pl.BlockSpec(shape.shape, lambda i: (0, 0, 0, 0)) for shape in shapes],
        out_shape=shapes,
        scratch_shapes=[pltpu.VMEM((window, sources, width), F32)],
        compiler_params=pltpu.CompilerParams(vmem_limit_bytes=48 << 20),
        cost_estimate=pl.CostEstimate(
            flops=6 * flat.size * sources, bytes_accessed=4 * (flat.size + own_knowns.size), transcendentals=0
        ),
    )(pltpu.with_memory_space_constraint(own_knowns.reshape(blocks * order, sources), pltpu.HBM), flat)
    keeps, sends = list(keeps_sends[: len(sizes)]), list(keeps_sends[len(sizes) :])
    sends[0], sends[1], near[0], far = lax.optimization_barrier((sends[0], sends[1], near[0], far))

    def reduce_rows(send, keep):
        total = keep + (yield lax.ppermute(send, "row", swap_pairs(rows, 1)))
        for moves in line_steps(pieces, base_row // 2):
            pairs = [(2 * a + k, 2 * b + k) for a, b in moves for k in (0, 1)]
            total = total + (yield lax.ppermute(total, "row", pairs))
        yield total.reshape(total.shape[0], pieces * part, width)

    with jax.named_scope("reduce0"):
        leading = reduce_rows(sends[0], keeps[0])
        lead = next(leading)
    with jax.named_scope("reduce1"):
        trailing = reduce_rows(*wait(lead, (sends[1],)), keeps[1])
        trail = next(trailing)
    with jax.named_scope("reduce2"):
        last = reduce_rows(*wait(trail, (sends[2],)), keeps[2])
        held = next(last)
    for step in range(len(line_steps(pieces, base_row // 2))):
        with jax.named_scope("reduce0"):
            lead = leading.send(lead)
        if step == 0:
            lead, trail = lax.optimization_barrier((lead, trail))
        else:
            lead, trail, held = lax.optimization_barrier((lead, trail, held))
        with jax.named_scope("reduce1"):
            trail = trailing.send(trail)
    after_first = wait(held, (near[0], *ahead[1:]))
    for _ in line_steps(pieces, base_row // 2):
        with jax.named_scope("reduce2"):
            held = last.send(held)
    residual = [one for gen, value in ((leading, lead), (trailing, trail), (last, held)) for one in gen.send(value)]

    def between(i, j):
        if i < 2:
            mine, other = ahead[j - i - 1], near[j - i - 1]
            return jnp.where(leader, mine, other) if i == 0 else jnp.where(leader, other, mine)
        return jnp.where(leader, far, across)

    with jax.named_scope("near2"):
        near.append(among([(0, 1), (1, 0)], after_first[1]))
    with jax.named_scope("near3"):
        near.append(among([(0, 1)], after_first[2]))
    with jax.named_scope("across"):
        across = among([(3, 1)], after_first[0])

    solved = []
    for j in range(window):
        with jax.named_scope(f"solve{j}"):
            full = gather_col(residual[j])
            solved.append(dot(full, inverse[j]))
            if j + 1 == window:
                break
            x = gather_col(solved[j])
        if j == 0:
            corner = x
        for k in range(j + 1, window):
            with jax.named_scope(f"term{j}{k}"):
                if (j, k) != (0, window - 1):
                    residual[k] = residual[k] - dot(x, between(j, k))
        if j == 2:
            with jax.named_scope("corner"):
                residual[window - 1] = residual[window - 1] - dot(corner, between(0, window - 1))

    def hand_out(values):
        parts = values.reshape(-1, pieces, part, width)
        home = base_row // 2
        result = jnp.where(row // 2 == home, parts[:, home], 0.0)
        for piece in range(pieces):
            if piece != home:
                pairs = [(base_row + k, 2 * piece + k) for k in (0, 1)]
                result = result + lax.ppermute(parts[:, piece], "row", pairs)
        return result

    with jax.named_scope("out"):
        result = hand_out(jnp.stack(solved))
    return result.transpose(0, 2, 1)


def solution(mesh):
    return jax.shard_map(
        on_device,
        mesh=mesh,
        in_specs=(
            P("row", None, None, None, "col"),
            P("row", None, None, None),
            P(None, None, "col"),
        ),
        out_specs=P(None, "col", "row"),
        check_vma=False,
    )
```

time: 159 us -> 141 us (0.89); the launches traced: 156 us -> 140 us
  waiting for transfers between devices: 64.8 us -> 12.1 us
  blocking collectives: 0 us -> 50.9 us
  starting transfers between devices: 41.8 us -> 31.9 us
  local copies, waits for them, and re-layouts: 7.03 us -> 0.07 us
  other arithmetic: 2.22 us -> 4.58 us
    ppermute x21 -> x12, waiting for transfers between devices: 64.7 us -> 12.1 us  [the longest x3 6.67 us: hand_out(): result = result + lax.ppermute(parts[:, piece], 'row', pairs)]
    all_gather x0 -> x7, blocking collectives: none -> 50.9 us  [gather_col(): return lax.all_gather(block, 'col', axis=1, tiled=True)]
    ppermute x16 -> x5, starting transfers between devices: 12.5 us -> 3.63 us  [among(): lax.ppermute(payload, 'row', [(base_row + a, base_row + b) for a, b in pa...]
    slice x4 -> x0, local copies, waits for them, and re-layouts: 3.79 us -> none  [the longest x1 1.88 us: on_device(): near2 = among([(0, 1), (2, 3), (3, 2)], far[:top])]
    add x7 -> x9, other arithmetic: 1.11 us -> 3.85 us  [the longest x6 2.02 us: reduce_rows(): total = total + (yield lax.ppermute(total, 'row', pairs))]
    unnamed x15 -> x10, local copies, waits for them, and re-layouts: 2.13 us -> 0.02 us
    ppermute x21 -> x12, starting transfers between devices: 29.3 us -> 28.3 us  [the longest x6 19.4 us: reduce_rows(): total = total + (yield lax.ppermute(total, 'row', pairs))]
    dot_general x9 -> x10, matrix products: 5.48 us -> 5.45 us  [dot(): jnp.dot(left, right, precision=lax.Precision.HIGH, preferred_element_type...]
  transfers between devices with their start and end apart: 37 -> 17, of which waited for: 16 -> 4; matrix products, arithmetic and copies ran while one was open for 7% -> 4% of each run, Pallas kernels for 20% -> 22%
where the time goes in v3:
time: 141 us; the launch traced here: 140 us
  blocking collectives  50.9 us (36%)
  Pallas kernels  34.6 us (25%)
  starting transfers between devices  31.9 us (23%)
  waiting for transfers between devices  12.1 us (9%)
  matrix products  5.45 us (4%)
  other arithmetic  4.58 us (3%)
    all_gather x7, blocking collectives, gather_col(): return lax.all_gather(block, 'col', axis=1, tiled=True)  50.9 us
    pallas_call x1, Pallas kernels, on_device(): pl.pallas_call(functools.partial(prefix_kernel, (rows, window, tiles, fir...  31.4 us
    ppermute x6, starting transfers between devices, reduce_rows(): total = total + (yield lax.ppermute(total, 'row', pairs))  19.4 us
    ppermute x3, waiting for transfers between devices, hand_out(): result = result + lax.ppermute(parts[:, piece], 'row', pairs)  6.67 us
    ppermute x3, starting transfers between devices, reduce_rows(): total = keep + (yield lax.ppermute(send, 'row', swap_pairs(rows, 1)))  6.22 us
    dot_general x10, matrix products, dot(): jnp.dot(left, right, precision=lax.Precision.HIGH, preferred_element_type...  5.45 us
    ppermute x5, starting transfers between devices, among(): lax.ppermute(payload, 'row', [(base_row + a, base_row + b) for a, b in pa...  3.63 us
    ppermute x3, waiting for transfers between devices, reduce_rows(): total = keep + (yield lax.ppermute(send, 'row', swap_pairs(rows, 1)))  3.51 us
  transfers between devices with their start and end apart: 17, of which 4 were waited for; matrix products, arithmetic and copies ran while one was open for 4% of the time, Pallas kernels for 22%

profile of v3, /device:TPU:0, one launch (start us, length us, event | category | flops | bytes accessed | tf_op | source)
XLA Modules:
  0.0 140.0 jit_solution(10630847077652004378)
XLA Ops:
  0.0 3.2 %shard_map.38 = (f32[1024,256]{1,0:T(8,128)S(1)}, f32[1024,256]{1,0:T(8,128)S(1)}, f32[1024,256]{1,0:T(8,128)S(1)}) custom-call(f32[98304,128]{1,0:T(8,128)} %bitcast.84), custom_call_target="tpu_custom_call" | custom-call | tf_op jit(solution)/shard_map/pallas_call | solution.py:143
  3.2 0.7 collective-permute-start.1
  3.9 0.7 collective-permute-start
  4.6 31.4 %shard_map.37 = (f32[1,4,32,256]{3,2,1,0:T(8,128)S(1)}, f32[1,4,32,256]{3,2,1,0:T(8,128)S(1)}, f32[2,4,32,256]{3,2,1,0:T(8,128)S(1)}, f32[1,4,32,256]{3,2,1,0:T(...) custom-call(f32[12288,256]{1,0:T(8,128)} %bitcast.91, f32[98304,128]{1,0:T(8,128)} %bitcast.85), custom_call_target="tpu_custom_call" | custom-call | flops 19327352832 | bytes 62914560 | tf_op jit(solution)/shard_map/pallas_call | solution.py:162
  36.1 0.0 collective-permute-done
  36.1 3.0 %collective-permute-start.2 = (f32[1,4,32,256]{3,2,1,0:T(8,128)S(1)}, f32[1,4,32,256]{3,2,1,0:T(8,128)S(1)}, u32[]{:S(2)}, u32[]{:S(2)}) collective-permute-start(f32[1,4,32,256]{3,2,1,0:T(8,128)S(1)} %get-tuple-element.32), channel_id=1, source_target_pairs={{0,4},{4,0},{8,12},{12,8},{16,20},{20,16},{24,28},{28,24},{1,5},{5... | collective-permute-start | bytes 393224 | tf_op jit(solution)/shard_map/reduce0/ppermute | solution.py:181
  39.1 3.5 %collective-permute-done.2 = f32[1,4,32,256]{3,2,1,0:T(8,128)S(1)} collective-permute-done((f32[1,4,32,256]{3,2,1,0:T(8,128)S(1)}, f32[1,4,32,256]{3,2,1,0:T(8,128)S(1)}, u32[]{:S(2)}, u32[]{:S(2)}) %collective-permute-start.2) | collective-permute-done | bytes 131104 | tf_op jit(solution)/shard_map/reduce0/ppermute | solution.py:181
  42.6 1.7 %collective-permute-start.4 = (f32[1,4,32,256]{3,2,1,0:T(8,128)S(1)}, f32[1,4,32,256]{3,2,1,0:T(8,128)S(1)}, u32[]{:S(2)}, u32[]{:S(2)}) collective-permute-start(f32[1,4,32,256]{3,2,1,0:T(8,128)S(1)} %get-tuple-element.34), channel_id=1, source_target_pairs={{0,4},{4,0},{8,12},{12,8},{16,20},{20,16},{24,28},{28,24},{1,5},{5... | collective-permute-start | bytes 393224 | tf_op jit(solution)/shard_map/reduce1/ppermute | solution.py:181
  44.4 3.5 %collective-permute-start.3 = (f32[1,4,32,256]{3,2,1,0:T(8,128)S(1)}, f32[1,4,32,256]{3,2,1,0:T(8,128)S(1)}, u32[]{:S(2)}, u32[]{:S(2)}) collective-permute-start(f32[1,4,32,256]{3,2,1,0:T(8,128)S(1)} %add.41), channel_id=1, source_target_pairs={{0,8},{4,12},{24,16},{28,20},{1,9},{5,13},{25,17},{29,21},{2,10},{... | collective-permute-start | bytes 393224 | tf_op jit(solution)/shard_map/reduce0/ppermute | solution.py:184
  47.9 0.0 collective-permute-done.4
  47.9 1.4 %collective-permute-start.7 = (f32[2,4,32,256]{3,2,1,0:T(8,128)}, f32[2,4,32,256]{3,2,1,0:T(8,128)}, u32[]{:S(2)}, u32[]{:S(2)}) collective-permute-start(f32[2,4,32,256]{3,2,1,0:T(8,128)} %get-tuple-element.39), channel_id=1, source_target_pairs={{0,4},{4,0},{8,12},{12,8},{16,20},{20,16},{24,28},{28,24},{1,5},{5... | collective-permute-start | bytes 786440 | tf_op jit(solution)/shard_map/reduce2/ppermute | solution.py:181
  49.3 1.0 collective-permute-done.3
  50.4 0.7 add.43
  51.1 5.0 %collective-permute-start.6 = (f32[1,4,32,256]{3,2,1,0:T(8,128)}, f32[1,4,32,256]{3,2,1,0:T(8,128)}, u32[]{:S(2)}, u32[]{:S(2)}) collective-permute-start(f32[1,4,32,256]{3,2,1,0:T(8,128)} %add.43), channel_id=1, source_target_pairs={{0,8},{4,12},{24,16},{28,20},{1,9},{5,13},{25,17},{29,21},{2,10},{... | collective-permute-start | bytes 393224 | tf_op jit(solution)/shard_map/reduce1/ppermute | solution.py:184
  56.1 1.3 collective-permute-start.5
  57.4 0.9 collective-permute-done.6
  58.3 0.9 add.44
  59.2 1.0 add.45
  60.2 0.0 copy-start.2
  60.2 1.1 add.48
  61.3 0.8 collective-permute-start.8
  62.1 8.1 %collective-permute-start.9 = (f32[2,4,32,256]{3,2,1,0:T(8,128)S(1)}, f32[2,4,32,256]{3,2,1,0:T(8,128)S(1)}, u32[]{:S(2)}, u32[]{:S(2)}) collective-permute-start(f32[2,4,32,256]{3,2,1,0:T(8,128)S(1)} %add.48), channel_id=1, source_target_pairs={{0,8},{4,12},{24,16},{28,20},{1,9},{5,13},{25,17},{29,21},{2,10},{... | collective-permute-start | bytes 786440 | tf_op jit(solution)/shard_map/reduce2/ppermute | solution.py:184
  70.3 7.2 %all_gather.21 = f32[128,1024]{1,0:T(8,128)S(1)} all-gather(f32[128,256]{1,0:T(8,128)S(1)} %bitcast.90), channel_id=1, replica_groups=mesh['row'=8,'col'=4] {'col'}, dimensions={1}, use_global_device_ids=true | all-gather | bytes 655360 | tf_op jit(solution)/shard_map/solve0/all_gather | solution.py:123
  77.5 0.7 collective-permute-start.11
  78.2 0.7 collective-permute-start.12
  78.9 0.7 collective-permute-start.13
  79.7 1.6 %fusion.5 = f32[128,256]{1,0:T(8,128)S(1)} fusion(f32[128,1024]{1,0:T(8,128)S(1)} %all_gather.21, f32[4,1024,256]{2,1,0:T(8,128)} %param.5), kind=kOutput, calls=%fused_computation.6 | convolution fusion | flops 201326592 | bytes 1703936 | tf_op jit(solution)/shard_map/solve0/dot_general | solution.py:96
  81.3 7.3 %all_gather.22 = f32[128,1024]{1,0:T(8,128)S(1)} all-gather(f32[128,256]{1,0:T(8,128)S(1)} %fusion.5), channel_id=1, replica_groups=mesh['row'=8,'col'=4] {'col'}, dimensions={1}, use_global_device_ids=true | all-gather | bytes 655360 | tf_op jit(solution)/shard_map/solve0/all_gather | solution.py:123
  88.6 0.4 bitcast_subtract_fusion.2
  89.1 7.3 %all_gather.23 = f32[128,1024]{1,0:T(8,128)S(1)} all-gather(f32[128,256]{1,0:T(8,128)S(1)} %bitcast_subtract_fusion.2), channel_id=1, replica_groups=mesh['row'=8,'col'=4] {'col'}, dimensions={1}, use_global_device_ids=true | all-gather | bytes 655360 | tf_op jit(solution)/shard_map/solve1/all_gather | solution.py:123
  96.4 0.7 collective-permute-start.10
  97.1 0.4 fusion.3
  97.5 7.3 %all_gather.24 = f32[128,1024]{1,0:T(8,128)S(1)} all-gather(f32[128,256]{1,0:T(8,128)S(1)} %fusion.3), channel_id=1, replica_groups=mesh['row'=8,'col'=4] {'col'}, dimensions={1}, use_global_device_ids=true | all-gather | bytes 655360 | tf_op jit(solution)/shard_map/solve1/all_gather | solution.py:123
  104.9 0.4 fusion.17
  105.3 0.4 fusion.37
  105.8 7.3 %all_gather.25 = f32[128,1024]{1,0:T(8,128)S(1)} all-gather(f32[128,256]{1,0:T(8,128)S(1)} %fusion.37), channel_id=1, replica_groups=mesh['row'=8,'col'=4] {'col'}, dimensions={1}, use_global_device_ids=true | all-gather | bytes 655360 | tf_op jit(solution)/shard_map/solve2/all_gather | solution.py:123
  113.1 0.4 fusion.1
  113.5 7.3 %all_gather.26 = f32[128,1024]{1,0:T(8,128)S(1)} all-gather(f32[128,256]{1,0:T(8,128)S(1)} %fusion.1), channel_id=1, replica_groups=mesh['row'=8,'col'=4] {'col'}, dimensions={1}, use_global_device_ids=true | all-gather | bytes 655360 | tf_op jit(solution)/shard_map/solve2/all_gather | solution.py:123
  120.8 0.4 fusion.12
  121.2 0.4 fusion.10
  121.7 0.4 fusion.36
  122.1 7.3 %all_gather.27 = f32[128,1024]{1,0:T(8,128)S(1)} all-gather(f32[128,256]{1,0:T(8,128)S(1)} %fusion.36), channel_id=1, replica_groups=mesh['row'=8,'col'=4] {'col'}, dimensions={1}, use_global_device_ids=true | all-gather | bytes 655360 | tf_op jit(solution)/shard_map/solve3/all_gather | solution.py:123
  129.4 0.4 convolution_bitcast_fusion
  129.9 1.3 collective-permute-start.14
  131.2 0.7 collective-permute-start.16
  131.9 0.7 collective-permute-start.15
  132.6 6.7 %collective-permute-done.14 = f32[4,32,256]{2,1,0:T(8,128)S(1)} collective-permute-done((f32[4,32,256]{2,1,0:T(8,128)S(1)}, f32[4,32,256]{2,1,0:T(8,128)S(1)}, u32[]{:S(2)}, u32[]{:S(2)}) %collective-permute-start.14) | collective-permute-done | bytes 131104 | tf_op jit(solution)/shard_map/out/ppermute | solution.py:249
  139.3 0.7 fusion.34
  (28 shorter events, 0.3 us)
Async XLA Ops:
  3.2 32.9 %collective-permute-start.1 = (f32[1024,256]{1,0:T(8,128)S(1)}, f32[1024,256]{1,0:T(8,128)S(1)}, u32[]{:S(2)}, u32[]{:S(2)}) collective-permute-start(f32[1024,256]{1,0:T(8,128)S(1)} %get-tuple-element.31), channel_id=1, source_target_pairs={{24,16},{25,17},{26,18},{27,19}} | collective-permute-start | bytes 3145736 | tf_op jit(solution)/shard_map/far/ppermute | solution.py:153
  3.9 32.2 %collective-permute-start = (f32[1024,256]{1,0:T(8,128)S(1)}, f32[1024,256]{1,0:T(8,128)S(1)}, u32[]{:S(2)}, u32[]{:S(2)}) collective-permute-start(f32[1024,256]{1,0:T(8,128)S(1)} %get-tuple-element.31), channel_id=1, source_target_pairs={{16,20},{20,16},{24,28},{17,21},{21,17},{25,29},{18,22},{22,18},{2... | collective-permute-start | bytes 3145736 | tf_op jit(solution)/shard_map/near1/ppermute | solution.py:153
  36.1 20.0 %copy-start.3 = (f32[1024,256]{1,0:T(8,128)}, f32[1024,256]{1,0:T(8,128)S(1)}, u32[]{:S(2)}) copy-start(f32[1024,256]{1,0:T(8,128)S(1)} %collective-permute-done.1) | copy-start | bytes 3145732
  36.1 15.0 %copy-start = (f32[1024,256]{1,0:T(8,128)}, f32[1024,256]{1,0:T(8,128)S(1)}, u32[]{:S(2)}) copy-start(f32[1024,256]{1,0:T(8,128)S(1)} %collective-permute-done) | copy-start | bytes 3145732
  36.1 6.5 %collective-permute-start.2 = (f32[1,4,32,256]{3,2,1,0:T(8,128)S(1)}, f32[1,4,32,256]{3,2,1,0:T(8,128)S(1)}, u32[]{:S(2)}, u32[]{:S(2)}) collective-permute-start(f32[1,4,32,256]{3,2,1,0:T(8,128)S(1)} %get-tuple-element.32), channel_id=1, source_target_pairs={{0,4},{4,0},{8,12},{12,8},{16,20},{20,16},{24,28},{28,24},{1,5},{5... | collective-permute-start | bytes 393224 | tf_op jit(solution)/shard_map/reduce0/ppermute | solution.py:181
  42.6 5.3 %collective-permute-start.4 = (f32[1,4,32,256]{3,2,1,0:T(8,128)S(1)}, f32[1,4,32,256]{3,2,1,0:T(8,128)S(1)}, u32[]{:S(2)}, u32[]{:S(2)}) collective-permute-start(f32[1,4,32,256]{3,2,1,0:T(8,128)S(1)} %get-tuple-element.34), channel_id=1, source_target_pairs={{0,4},{4,0},{8,12},{12,8},{16,20},{20,16},{24,28},{28,24},{1,5},{5... | collective-permute-start | bytes 393224 | tf_op jit(solution)/shard_map/reduce1/ppermute | solution.py:181
  44.4 6.0 %collective-permute-start.3 = (f32[1,4,32,256]{3,2,1,0:T(8,128)S(1)}, f32[1,4,32,256]{3,2,1,0:T(8,128)S(1)}, u32[]{:S(2)}, u32[]{:S(2)}) collective-permute-start(f32[1,4,32,256]{3,2,1,0:T(8,128)S(1)} %add.41), channel_id=1, source_target_pairs={{0,8},{4,12},{24,16},{28,20},{1,9},{5,13},{25,17},{29,21},{2,10},{... | collective-permute-start | bytes 393224 | tf_op jit(solution)/shard_map/reduce0/ppermute | solution.py:184
  47.9 10.4 %collective-permute-start.7 = (f32[2,4,32,256]{3,2,1,0:T(8,128)}, f32[2,4,32,256]{3,2,1,0:T(8,128)}, u32[]{:S(2)}, u32[]{:S(2)}) collective-permute-start(f32[2,4,32,256]{3,2,1,0:T(8,128)} %get-tuple-element.39), channel_id=1, source_target_pairs={{0,4},{4,0},{8,12},{12,8},{16,20},{20,16},{24,28},{28,24},{1,5},{5... | collective-permute-start | bytes 786440 | tf_op jit(solution)/shard_map/reduce2/ppermute | solution.py:181
  51.1 7.2 %collective-permute-start.6 = (f32[1,4,32,256]{3,2,1,0:T(8,128)}, f32[1,4,32,256]{3,2,1,0:T(8,128)}, u32[]{:S(2)}, u32[]{:S(2)}) collective-permute-start(f32[1,4,32,256]{3,2,1,0:T(8,128)} %add.43), channel_id=1, source_target_pairs={{0,8},{4,12},{24,16},{28,20},{1,9},{5,13},{25,17},{29,21},{2,10},{... | collective-permute-start | bytes 393224 | tf_op jit(solution)/shard_map/reduce1/ppermute | solution.py:184
  56.1 2.2 %collective-permute-start.5 = (f32[1,4,32,256]{3,2,1,0:T(8,128)S(1)}, f32[1,4,32,256]{3,2,1,0:T(8,128)}, u32[]{:S(2)}, u32[]{:S(2)}) collective-permute-start(f32[1,4,32,256]{3,2,1,0:T(8,128)S(1)} %add.42), channel_id=1, source_target_pairs={{8,16},{12,20},{9,17},{13,21},{10,18},{14,22},{11,19},{15,23}} | collective-permute-start | bytes 393224 | tf_op jit(solution)/shard_map/reduce0/ppermute | solution.py:184
  57.4 31.2 %copy-start.1 = (f32[1024,256]{1,0:T(8,128)S(1)}, f32[1024,256]{1,0:T(8,128)}, u32[]{:S(2)}) copy-start(f32[1024,256]{1,0:T(8,128)} %copy-done) | copy-start | bytes 3145732
  60.2 36.9 %copy-start.2 = (f32[4,1024,256]{2,1,0:T(8,128)S(1)}, f32[4,1024,256]{2,1,0:T(8,128)}, u32[]{:S(2)}) copy-start(f32[4,1024,256]{2,1,0:T(8,128)} %param.5) | copy-start | bytes 12582916
  61.3 27.3 %collective-permute-start.8 = (f32[1,4,32,256]{3,2,1,0:T(8,128)S(1)}, f32[1,4,32,256]{3,2,1,0:T(8,128)S(1)}, u32[]{:S(2)}, u32[]{:S(2)}) collective-permute-start(f32[1,4,32,256]{3,2,1,0:T(8,128)S(1)} %add.45), channel_id=1, source_target_pairs={{8,16},{12,20},{9,17},{13,21},{10,18},{14,22},{11,19},{15,23}} | collective-permute-start | bytes 393224 | tf_op jit(solution)/shard_map/reduce1/ppermute | solution.py:184
  62.1 34.2 %collective-permute-start.9 = (f32[2,4,32,256]{3,2,1,0:T(8,128)S(1)}, f32[2,4,32,256]{3,2,1,0:T(8,128)S(1)}, u32[]{:S(2)}, u32[]{:S(2)}) collective-permute-start(f32[2,4,32,256]{3,2,1,0:T(8,128)S(1)} %add.48), channel_id=1, source_target_pairs={{0,8},{4,12},{24,16},{28,20},{1,9},{5,13},{25,17},{29,21},{2,10},{... | collective-permute-start | bytes 786440 | tf_op jit(solution)/shard_map/reduce2/ppermute | solution.py:184
  77.5 27.4 %collective-permute-start.11 = (f32[1024,256]{1,0:T(8,128)S(1)}, f32[1024,256]{1,0:T(8,128)S(1)}, u32[]{:S(2)}, u32[]{:S(2)}) collective-permute-start(f32[1024,256]{1,0:T(8,128)S(1)} %get-tuple-element.47), channel_id=1, source_target_pairs={{16,20},{20,16},{17,21},{21,17},{18,22},{22,18},{19,23},{23,19}} | collective-permute-start | bytes 3145736 | tf_op jit(solution)/shard_map/near2/ppermute | solution.py:153
  78.2 43.0 %collective-permute-start.12 = (f32[1024,256]{1,0:T(8,128)}, f32[1024,256]{1,0:T(8,128)S(1)}, u32[]{:S(2)}, u32[]{:S(2)}) collective-permute-start(f32[1024,256]{1,0:T(8,128)} %copy-done), channel_id=1, source_target_pairs={{28,20},{29,21},{30,22},{31,23}} | collective-permute-start | bytes 3145736 | tf_op jit(solution)/shard_map/across/ppermute | solution.py:153
  78.9 42.8 %collective-permute-start.13 = (f32[1024,256]{1,0:T(8,128)S(1)}, f32[1024,256]{1,0:T(8,128)S(1)}, u32[]{:S(2)}, u32[]{:S(2)}) collective-permute-start(f32[1024,256]{1,0:T(8,128)S(1)} %get-tuple-element.50), channel_id=1, source_target_pairs={{16,20},{17,21},{18,22},{19,23}} | collective-permute-start | bytes 3145736 | tf_op jit(solution)/shard_map/near3/ppermute | solution.py:153
  96.4 8.4 %collective-permute-start.10 = (f32[2,4,32,256]{3,2,1,0:T(8,128)S(1)}, f32[2,4,32,256]{3,2,1,0:T(8,128)S(1)}, u32[]{:S(2)}, u32[]{:S(2)}) collective-permute-start(f32[2,4,32,256]{3,2,1,0:T(8,128)S(1)} %add.49), channel_id=1, source_target_pairs={{8,16},{12,20},{9,17},{13,21},{10,18},{14,22},{11,19},{15,23}} | collective-permute-start | bytes 786440 | tf_op jit(solution)/shard_map/reduce2/ppermute | solution.py:184
  105.3 15.9 %copy-start.4 = (f32[1024,256]{1,0:T(8,128)S(1)}, f32[1024,256]{1,0:T(8,128)}, u32[]{:S(2)}) copy-start(f32[1024,256]{1,0:T(8,128)} %copy-done.3) | copy-start | bytes 3145732
  129.9 9.3 %collective-permute-start.14 = (f32[4,32,256]{2,1,0:T(8,128)S(1)}, f32[4,32,256]{2,1,0:T(8,128)S(1)}, u32[]{:S(2)}, u32[]{:S(2)}) collective-permute-start(f32[4,32,256]{2,1,0:T(8,128)S(1)} %get-tuple-element.51), channel_id=1, source_target_pairs={{16,0},{20,4},{17,1},{21,5},{18,2},{22,6},{19,3},{23,7}} | collective-permute-start | bytes 393224 | tf_op jit(solution)/shard_map/out/ppermute | solution.py:249
  131.2 8.0 %collective-permute-start.16 = (f32[4,32,256]{2,1,0:T(8,128)S(1)}, f32[4,32,256]{2,1,0:T(8,128)S(1)}, u32[]{:S(2)}, u32[]{:S(2)}) collective-permute-start(f32[4,32,256]{2,1,0:T(8,128)S(1)} %get-tuple-element.52), channel_id=1, source_target_pairs={{16,24},{20,28},{17,25},{21,29},{18,26},{22,30},{19,27},{23,31}} | collective-permute-start | bytes 393224 | tf_op jit(solution)/shard_map/out/ppermute | solution.py:249
  131.9 7.4 %collective-permute-start.15 = (f32[4,32,256]{2,1,0:T(8,128)S(1)}, f32[4,32,256]{2,1,0:T(8,128)S(1)}, u32[]{:S(2)}, u32[]{:S(2)}) collective-permute-start(f32[4,32,256]{2,1,0:T(8,128)S(1)} %get-tuple-element.53), channel_id=1, source_target_pairs={{16,8},{20,12},{17,9},{21,13},{18,10},{22,14},{19,11},{23,15}} | collective-permute-start | bytes 393224 | tf_op jit(solution)/shard_map/out/ppermute | solution.py:249

commit v4 on v3

v4 whole, which is shorter than its diff:
```python
import functools

import jax
import jax.numpy as jnp
from jax import lax
from jax.experimental import pallas as pl
from jax.experimental.pallas import tpu as pltpu
from jax.sharding import PartitionSpec as P

F32 = jnp.float32
BF16 = jnp.bfloat16
LANES = 128


def split(value):
    high = value.astype(BF16)
    return high, (value - high.astype(F32)).astype(BF16)


def dot3(left, right):
    product = functools.partial(jnp.dot, preferred_element_type=F32)
    return product(left[0], right[0]) + (product(left[1], right[0]) + product(left[0], right[1]))


def swap_pairs(size, mask):
    return [(i, i ^ mask) for i in range(size)]


def factor_rows(factor):
    blocks, order, window, width = factor.shape
    tiles = width // LANES
    view = factor.reshape(blocks * order, window, tiles, LANES).transpose(0, 2, 1, 3)
    return view.reshape(blocks * order, tiles * window, 1, LANES)


def prefix_kernel(dims, part, sizes, knowns_ref, *refs):
    rows, window, tiles, first_block, order = dims
    columns, refs = refs[: tiles * window], refs[tiles * window :]
    keeps, sends, total = refs[: len(sizes)], refs[len(sizes) : -1], refs[-1]
    step = pl.program_id(0)
    row = lax.axis_index("row")
    col = lax.axis_index("col")
    width = tiles * LANES
    depth = knowns_ref.shape[0]
    per_step = depth // order

    @pl.when(step == 0)
    def _():
        total[...] = jnp.zeros_like(total)

    counted = [
        knowns_ref[at * order : (at + 1) * order, :]
        * (((step * per_step + at) * rows + row) < first_block).astype(F32)
        for at in range(per_step)
    ]
    known = split(jnp.concatenate(counted, axis=0).T)
    for j in range(window):
        pieces = [split(columns[t * window + j].reshape(depth, LANES)[...]) for t in range(tiles)]
        high = jnp.concatenate([p[0] for p in pieces], axis=1)
        low = jnp.concatenate([p[1] for p in pieces], axis=1)
        total[j] += dot3(known, (high, low))

    @pl.when(step == pl.num_programs(0) - 1)
    def _():
        first_row = depth - order + col * width
        rhs = knowns_ref[pl.ds(pl.multiple_of(first_row, width), width), :].T
        bit = lax.rem(row, 2)
        j = 0
        for keep, send, size in zip(keeps, sends, sizes):
            for at in range(size):
                own = (row == (first_block + j) % rows).astype(F32)
                total[j] = own * rhs - total[j]
                for piece in range(rows // 2):
                    mine = pl.multiple_of((2 * piece + bit) * part, part)
                    other = pl.multiple_of((2 * piece + 1 - bit) * part, part)
                    keep[at, piece] = total[j, pl.ds(mine, part), :]
                    send[at, piece] = total[j, pl.ds(other, part), :]
                j += 1


def window_kernel(window, tiles, factor_ref, *outs):
    member = lax.rem(lax.axis_index("row"), window)
    order = outs[0].shape[0]
    for ahead, out in enumerate(outs, 1):
        j = jnp.minimum(member + ahead, window - 1)
        for t in range(tiles):
            out[:, t * LANES : (t + 1) * LANES] = factor_ref[
                pl.ds(t * window + j, order, stride=tiles * window), :
            ]


def dot(left, right):
    return jnp.dot(left, right, precision=lax.Precision.HIGH, preferred_element_type=F32)


def wait(event, arrays):
    return lax.optimization_barrier((event, *arrays))[1:]


def line_steps(count, target):
    below, above, steps = list(range(target)), list(range(count - 1, target, -1)), []
    while below or above:
        moves, taken = [], False
        for side in (below, above):
            pairs = [(side[at], side[at + 1]) for at in range(0, len(side) - 1, 2)]
            left = [to for _, to in pairs]
            if len(side) % 2:
                if taken:
                    left.append(side[-1])
                else:
                    pairs.append((side[-1], target))
                    taken = True
            moves += pairs
            side[:] = left
        steps.append(moves)
    return steps


def gather_col(block):
    return lax.all_gather(block, "col", axis=1, tiled=True)


def on_device(factor, knowns, inverse):
    rows = lax.axis_size("row")
    row = lax.axis_index("row")
    _, blocks, order, window, width = factor.shape
    sources = knowns.shape[-1]
    first_block = blocks * rows - window
    tiles = width // LANES
    part = sources // rows
    pieces = rows // 2
    slot = first_block // rows
    base_row = first_block % rows
    leader = row % 2 == 0
    columns = tiles * window
    view = factor_rows(factor[0])
    flat = pltpu.with_memory_space_constraint(view.reshape(-1, LANES), pltpu.HBM)
    view = pltpu.with_memory_space_constraint(view, pltpu.HBM)
    own_knowns = knowns[0]
    cuts = 4

    ahead = pl.pallas_call(
        functools.partial(window_kernel, window, tiles),
        grid=(cuts,),
        in_specs=[pl.BlockSpec((order // cuts * columns, LANES), lambda i: (slot * cuts + i, 0))],
        out_specs=[pl.BlockSpec((order // cuts, width), lambda i: (i, 0))] * (window - 1),
        out_shape=[jax.ShapeDtypeStruct((order, width), F32)] * (window - 1),
        compiler_params=pltpu.CompilerParams(vmem_limit_bytes=40 << 20),
    )(flat)

    def among(pairs, payload):
        return lax.ppermute(payload, "row", [(base_row + a, base_row + b) for a, b in pairs])

    with jax.named_scope("near1"):
        near = [among([(0, 1), (1, 0), (2, 3)], ahead[0])]
    with jax.named_scope("far"):
        far = among([(2, 0)], ahead[0])

    sizes = (1, window - 1)
    shapes = [(size, pieces, part, width) for size in sizes] * 2
    per_step = 2 if blocks % 2 == 0 else 1
    depth = per_step * order
    keeps_sends = pl.pallas_call(
        functools.partial(prefix_kernel, (rows, window, tiles, first_block, order), part, sizes),
        grid=(blocks // per_step,),
        in_specs=[pl.BlockSpec((depth, sources), lambda i: (i, 0))]
        + [
            pl.BlockSpec((depth, 1, 1, LANES), functools.partial(lambda at, i: (i, at, 0, 0), at))
            for at in range(columns)
        ],
        out_specs=[pl.BlockSpec(shape, lambda i: (0, 0, 0, 0)) for shape in shapes],
        out_shape=[pltpu.VMEM(shape, F32) for shape in shapes[: len(sizes)]]
        + [jax.ShapeDtypeStruct(shape, F32) for shape in shapes[len(sizes) :]],
        scratch_shapes=[pltpu.VMEM((window, sources, width), F32)],
        compiler_params=pltpu.CompilerParams(vmem_limit_bytes=52 << 20),
        cost_estimate=pl.CostEstimate(
            flops=6 * flat.size * sources, bytes_accessed=4 * (flat.size + own_knowns.size), transcendentals=0
        ),
    )(
        pltpu.with_memory_space_constraint(own_knowns.reshape(blocks * order, sources), pltpu.HBM),
        *[view] * columns,
    )
    keeps, sends = list(keeps_sends[: len(sizes)]), list(keeps_sends[len(sizes) :])
    sends[0], sends[1], near[0], far = lax.optimization_barrier((sends[0], sends[1], near[0], far))


    home = base_row // 2

    def moves_to(moves):
        return [(2 * a + k, 2 * b + k) for a, b in moves for k in (0, 1)]

    with jax.named_scope("reduce0"):
        arrived = lax.ppermute(sends[0], "row", swap_pairs(rows, 1))
        lead = keeps[0] + arrived
        places = [place for place in range(pieces) if place != home]
        straight = [lax.ppermute(lead, "row", moves_to([(place, home)])) for place in places]
    with jax.named_scope("reduce1"):
        trail_arrived = lax.ppermute(*wait(arrived, (sends[1],)), "row", swap_pairs(rows, 1))
    after_trail = wait(trail_arrived, (near[0], *ahead[1:]))
    with jax.named_scope("near2"):
        near.append(among([(0, 1), (1, 0)], after_trail[1]))
    *straight, trail_arrived = lax.optimization_barrier((*straight, trail_arrived))
    with jax.named_scope("reduce0"):
        for one in straight:
            lead = lead + one
    with jax.named_scope("reduce1"):
        trail = keeps[1] + trail_arrived
        for moves in line_steps(pieces, home):
            trail = trail + lax.ppermute(trail, "row", moves_to(moves))
    with jax.named_scope("across"):
        across = among([(3, 1)], *wait(trail, (near[0],)))
    with jax.named_scope("near3"):
        near.append(among([(0, 1)], after_trail[2]))
    residual = [one.reshape(pieces * part, width) for one in (*lead, *trail)]

    def between(i, j):
        if i < 2:
            mine, other = ahead[j - i - 1], near[j - i - 1]
            return jnp.where(leader, mine, other) if i == 0 else jnp.where(leader, other, mine)
        return jnp.where(leader, far, across)

    def hand_out(values):
        parts = values.reshape(-1, pieces, part, width)
        result = jnp.where(row // 2 == home, parts[:, home], 0.0)
        for piece in range(pieces):
            if piece != home:
                pairs = [(base_row + k, 2 * piece + k) for k in (0, 1)]
                result = result + lax.ppermute(parts[:, piece], "row", pairs)
        return result

    solved = []
    for j in range(window - 1):
        with jax.named_scope(f"solve{j}"):
            solved.append(dot(gather_col(residual[j]), inverse[j]))
            x = gather_col(solved[j])
        if j == 0:
            corner = x
        for k in range(j + 1, window):
            with jax.named_scope(f"term{j}{k}"):
                if (j, k) != (0, window - 1):
                    residual[k] = residual[k] - dot(x, between(j, k))
        if j == 2:
            with jax.named_scope("corner"):
                residual[window - 1] = residual[window - 1] - dot(corner, between(0, window - 1))
    with jax.named_scope("out_last"):
        own = hand_out(residual[-1])[0]
        own_solved = dot(gather_col(own), inverse[window - 1])
    with jax.named_scope("out"):
        result = jnp.concatenate([hand_out(jnp.stack(solved)), own_solved[None]])
    return result.transpose(0, 2, 1)


def solution(mesh):
    return jax.shard_map(
        on_device,
        mesh=mesh,
        in_specs=(
            P("row", None, None, None, "col"),
            P("row", None, None, None),
            P(None, None, "col"),
        ),
        out_specs=P(None, "col", "row"),
        check_vma=False,
    )
```

time: 141 us -> 133 us (0.943)
  Pallas kernels: 34.6 us -> 31 us
  starting transfers between devices: 31.9 us -> 28.7 us
  blocking collectives: 50.9 us -> 49.2 us
  waiting for transfers between devices: 12.1 us -> 13.6 us
    ppermute x9 -> x7, starting transfers between devices: 25.6 us -> 19.8 us  [the longest x3 9.49 us: on_device(): lax.ppermute(lead, 'row', moves_to([(place, home)]))]
    pallas_call x1, Pallas kernels: 31.4 us -> 27.8 us  [on_device(): pl.pallas_call(functools.partial(prefix_kernel, (rows, window, tiles, fir...]
    ppermute x3 -> x6, waiting for transfers between devices: 6.67 us -> 10 us  [hand_out(): result = result + lax.ppermute(parts[:, piece], 'row', pairs)]
    ppermute x3 -> x6, starting transfers between devices: 2.63 us -> 5.24 us  [hand_out(): result = result + lax.ppermute(parts[:, piece], 'row', pairs)]
    ppermute x9 -> x7, waiting for transfers between devices: 5.42 us -> 3.51 us  [the longest x1 3.5 us: on_device(): arrived = lax.ppermute(sends[0], 'row', swap_pairs(rows, 1))]
    all_gather x7, blocking collectives: 50.9 us -> 49.2 us  [gather_col(): return lax.all_gather(block, 'col', axis=1, tiled=True)]
    add x9 -> x7, other arithmetic: 3.85 us -> 3.08 us  [the longest x1 1.13 us: on_device(): trail = keeps[1] + trail_arrived]
  transfers between devices with their start and end apart: 17 -> 18, of which waited for: 4 -> 2; matrix products, arithmetic and copies ran while one was open for 4% -> 6% of each run, Pallas kernels for 22% -> 21%
where the time goes in v4:
time: 133 us
  blocking collectives  49.2 us (37%)
  Pallas kernels  31 us (23%)
  starting transfers between devices  28.7 us (22%)
  waiting for transfers between devices  13.6 us (10%)
  matrix products  5.84 us (4%)
  other arithmetic  3.78 us (3%)
    all_gather x7, blocking collectives, gather_col(): return lax.all_gather(block, 'col', axis=1, tiled=True)  49.2 us
    pallas_call x1, Pallas kernels, on_device(): pl.pallas_call(functools.partial(prefix_kernel, (rows, window, tiles, fir...  27.8 us
    ppermute x6, waiting for transfers between devices, hand_out(): result = result + lax.ppermute(parts[:, piece], 'row', pairs)  10 us
    ppermute x3, starting transfers between devices, on_device(): lax.ppermute(lead, 'row', moves_to([(place, home)]))  9.49 us
    dot_general x10, matrix products, dot(): jnp.dot(left, right, precision=lax.Precision.HIGH, preferred_element_type...  5.84 us
    ppermute x2, starting transfers between devices, on_device(): trail = trail + lax.ppermute(trail, 'row', moves_to(moves))  5.56 us
    ppermute x6, starting transfers between devices, hand_out(): result = result + lax.ppermute(parts[:, piece], 'row', pairs)  5.24 us
    ppermute x5, starting transfers between devices, among(): lax.ppermute(payload, 'row', [(base_row + a, base_row + b) for a, b in pa...  3.64 us
  transfers between devices with their start and end apart: 18, of which 2 were waited for; matrix products, arithmetic and copies ran while one was open for 6% of the time, Pallas kernels for 21%

profile of v4, /device:TPU:0, one launch (start us, length us, event | category | flops | bytes accessed | tf_op | source)
XLA Modules:
  0.0 132.5 jit_solution(308842743395920728)
XLA Ops:
  0.0 3.2 %shard_map.38 = (f32[1024,256]{1,0:T(8,128)S(1)}, f32[1024,256]{1,0:T(8,128)S(1)}, f32[1024,256]{1,0:T(8,128)S(1)}) custom-call(f32[98304,128]{1,0:T(8,128)} %bitcast.87), custom_call_target="tpu_custom_call" | custom-call | tf_op jit(solution)/shard_map/pallas_call | solution.py:142
  3.2 0.7 collective-permute-start
  3.9 0.7 collective-permute-start.1
  4.6 27.8 %shard_map.37 = (f32[1,4,32,256]{3,2,1,0:T(8,128)S(1)}, f32[3,4,32,256]{3,2,1,0:T(8,128)S(1)}, f32[1,4,32,256]{3,2,1,0:T(8,128)S(1)}, f32[3,4,32,256]{3,2,1,0:T(8,128)}) custom-call(f32[12288,256]{1,0:T(8,128)} %bitcast.96, f32[12288,8,1,128]{3,2,1,0:T(1,128)} %bitcast.88, f32[12288,8,1,128]{3,2,1,0:T(1,128)} %bitcast.89, f32[12288,8,1,128]{3,2,1,0:T(1,128)} %bitcast.90, ...), custom_call_target="tpu_custom_call" | custom-call | flops 19327352832 | bytes 62914560 | tf_op jit(solution)/shard_map/pallas_call | solution.py:163
  32.5 0.0 collective-permute-done.1
  32.5 3.0 %collective-permute-start.2 = (f32[1,4,32,256]{3,2,1,0:T(8,128)S(1)}, f32[1,4,32,256]{3,2,1,0:T(8,128)S(1)}, u32[]{:S(2)}, u32[]{:S(2)}) collective-permute-start(f32[1,4,32,256]{3,2,1,0:T(8,128)S(1)} %get-tuple-element.28), channel_id=1, source_target_pairs={{0,4},{4,0},{8,12},{12,8},{16,20},{20,16},{24,28},{28,24},{1,5},{5... | collective-permute-start | bytes 393224 | tf_op jit(solution)/shard_map/reduce0/ppermute | solution.py:193
  35.6 3.5 %collective-permute-done.2 = f32[1,4,32,256]{3,2,1,0:T(8,128)S(1)} collective-permute-done((f32[1,4,32,256]{3,2,1,0:T(8,128)S(1)}, f32[1,4,32,256]{3,2,1,0:T(8,128)S(1)}, u32[]{:S(2)}, u32[]{:S(2)}) %collective-permute-start.2) | collective-permute-done | bytes 131104 | tf_op jit(solution)/shard_map/reduce0/ppermute | solution.py:193
  39.0 1.7 %collective-permute-start.6 = (f32[3,4,32,256]{3,2,1,0:T(8,128)}, f32[3,4,32,256]{3,2,1,0:T(8,128)}, u32[]{:S(2)}, u32[]{:S(2)}) collective-permute-start(f32[3,4,32,256]{3,2,1,0:T(8,128)} %get-tuple-element.30), channel_id=1, source_target_pairs={{0,4},{4,0},{8,12},{12,8},{16,20},{20,16},{24,28},{28,24},{1,5},{5... | collective-permute-start | bytes 1179656 | tf_op jit(solution)/shard_map/reduce1/ppermute | solution.py:198
  40.8 0.7 add.44
  41.5 6.9 %collective-permute-start.3 = (f32[1,4,32,256]{3,2,1,0:T(8,128)}, f32[1,4,32,256]{3,2,1,0:T(8,128)}, u32[]{:S(2)}, u32[]{:S(2)}) collective-permute-start(f32[1,4,32,256]{3,2,1,0:T(8,128)} %add.44), channel_id=1, source_target_pairs={{0,16},{4,20},{1,17},{5,21},{2,18},{6,22},{3,19},{7,23}} | collective-permute-start | bytes 393224 | tf_op jit(solution)/shard_map/reduce0/ppermute | solution.py:196
  48.4 1.3 collective-permute-start.4
  49.7 1.3 collective-permute-start.5
  51.0 0.0 collective-permute-done.6
  51.0 1.1 add.48
  52.1 4.7 %collective-permute-start.7 = (f32[3,4,32,256]{3,2,1,0:T(8,128)S(1)}, f32[3,4,32,256]{3,2,1,0:T(8,128)S(1)}, u32[]{:S(2)}, u32[]{:S(2)}) collective-permute-start(f32[3,4,32,256]{3,2,1,0:T(8,128)S(1)} %add.48), channel_id=1, source_target_pairs={{0,8},{4,12},{24,16},{28,20},{1,9},{5,13},{25,17},{29,21},{2,10},{... | collective-permute-start | bytes 1179656 | tf_op jit(solution)/shard_map/reduce1/ppermute | solution.py:209
  56.9 0.7 collective-permute-start.9
  57.6 0.7 collective-permute-start.14
  58.3 1.1 add_add_fusion
  59.5 7.2 %all_gather.21 = f32[128,1024]{1,0:T(8,128)S(1)} all-gather(f32[128,256]{1,0:T(8,128)S(1)} %bitcast.100), channel_id=1, replica_groups=mesh['row'=8,'col'=4] {'col'}, dimensions={1}, use_global_device_ids=true | all-gather | bytes 655360 | tf_op jit(solution)/shard_map/solve0/all_gather | solution.py:120
  66.7 0.1 add.49
  66.7 0.0 copy-start.2
  66.7 0.8 collective-permute-start.8
  67.6 2.0 %fusion.5 = f32[128,256]{1,0:T(8,128)S(1)} fusion(f32[128,1024]{1,0:T(8,128)S(1)} %all_gather.21, f32[4,1024,256]{2,1,0:T(8,128)} %param.5), kind=kOutput, calls=%fused_computation.6 | convolution fusion | flops 201326592 | bytes 1703936 | tf_op jit(solution)/shard_map/solve0/dot_general | solution.py:93
  69.6 7.3 %all_gather.22 = f32[128,1024]{1,0:T(8,128)S(1)} all-gather(f32[128,256]{1,0:T(8,128)S(1)} %fusion.5), channel_id=1, replica_groups=mesh['row'=8,'col'=4] {'col'}, dimensions={1}, use_global_device_ids=true | all-gather | bytes 655360 | tf_op jit(solution)/shard_map/solve0/all_gather | solution.py:120
  76.9 0.1 add.50
  77.0 0.7 collective-permute-start.13
  77.7 0.4 bitcast_subtract_fusion.2
  78.2 7.3 %all_gather.23 = f32[128,1024]{1,0:T(8,128)S(1)} all-gather(f32[128,256]{1,0:T(8,128)S(1)} %bitcast_subtract_fusion.2), channel_id=1, replica_groups=mesh['row'=8,'col'=4] {'col'}, dimensions={1}, use_global_device_ids=true | all-gather | bytes 655360 | tf_op jit(solution)/shard_map/solve1/all_gather | solution.py:120
  85.5 0.4 fusion.3
  85.9 7.3 %all_gather.24 = f32[128,1024]{1,0:T(8,128)S(1)} all-gather(f32[128,256]{1,0:T(8,128)S(1)} %fusion.3), channel_id=1, replica_groups=mesh['row'=8,'col'=4] {'col'}, dimensions={1}, use_global_device_ids=true | all-gather | bytes 655360 | tf_op jit(solution)/shard_map/solve1/all_gather | solution.py:120
  93.2 0.4 fusion.17
  93.6 0.4 fusion.32
  94.1 7.4 %all_gather.25 = f32[128,1024]{1,0:T(8,128)S(1)} all-gather(f32[128,256]{1,0:T(8,128)S(1)} %fusion.32), channel_id=1, replica_groups=mesh['row'=8,'col'=4] {'col'}, dimensions={1}, use_global_device_ids=true | all-gather | bytes 655360 | tf_op jit(solution)/shard_map/solve2/all_gather | solution.py:120
  101.5 0.4 fusion.1
  102.0 1.3 collective-permute-start.10
  103.3 0.7 collective-permute-start.11
  104.0 0.7 collective-permute-start.12
  104.6 7.3 %all_gather.26 = f32[128,1024]{1,0:T(8,128)S(1)} all-gather(f32[128,256]{1,0:T(8,128)S(1)} %fusion.1), channel_id=1, replica_groups=mesh['row'=8,'col'=4] {'col'}, dimensions={1}, use_global_device_ids=true | all-gather | bytes 655360 | tf_op jit(solution)/shard_map/solve2/all_gather | solution.py:120
  111.9 0.4 fusion.12
  112.4 0.4 fusion.10
  112.8 0.4 fusion.31
  113.3 1.3 collective-permute-start.15
  114.6 0.7 collective-permute-start.16
  115.3 0.7 collective-permute-start.17
  116.0 10.0 %collective-permute-done.15 = f32[1,32,256]{2,1,0:T(8,128)S(1)} collective-permute-done((f32[1,32,256]{2,1,0:T(8,128)S(1)}, f32[1,32,256]{2,1,0:T(8,128)S(1)}, u32[]{:S(2)}, u32[]{:S(2)}) %collective-permute-start.15) | collective-permute-done | bytes 32800 | tf_op jit(solution)/shard_map/out_last/ppermute | solution.py:228
  126.1 5.4 %all-gather = f32[1,32,1024]{2,1,0:T(8,128)S(1)} all-gather(f32[1,32,256]{2,1,0:T(8,128)S(1)} %fusion.40), channel_id=2, replica_groups=mesh['row'=8,'col'=4] {'col'}, dimensions={2}, use_global_device_ids=true | all-gather | bytes 163840 | tf_op jit(solution)/shard_map/out_last/all_gather | solution.py:120
  131.5 0.4 convolution_bitcast_fusion
  131.9 0.7 maximum_bitcast_fusion
  (29 shorter events, 0.2 us)
Async XLA Ops:
  3.2 29.3 %collective-permute-start = (f32[1024,256]{1,0:T(8,128)S(1)}, f32[1024,256]{1,0:T(8,128)S(1)}, u32[]{:S(2)}, u32[]{:S(2)}) collective-permute-start(f32[1024,256]{1,0:T(8,128)S(1)} %get-tuple-element.27), channel_id=1, source_target_pairs={{16,20},{20,16},{24,28},{17,21},{21,17},{25,29},{18,22},{22,18},{2... | collective-permute-start | bytes 3145736 | tf_op jit(solution)/shard_map/near1/ppermute | solution.py:152
  3.9 28.6 %collective-permute-start.1 = (f32[1024,256]{1,0:T(8,128)S(1)}, f32[1024,256]{1,0:T(8,128)S(1)}, u32[]{:S(2)}, u32[]{:S(2)}) collective-permute-start(f32[1024,256]{1,0:T(8,128)S(1)} %get-tuple-element.27), channel_id=1, source_target_pairs={{24,16},{25,17},{26,18},{27,19}} | collective-permute-start | bytes 3145736 | tf_op jit(solution)/shard_map/far/ppermute | solution.py:152
  32.5 9.0 %copy-start = (f32[1024,256]{1,0:T(8,128)}, f32[1024,256]{1,0:T(8,128)S(1)}, u32[]{:S(2)}) copy-start(f32[1024,256]{1,0:T(8,128)S(1)} %collective-permute-done) | copy-start | bytes 3145732
  32.5 15.8 %copy-start.3 = (f32[1024,256]{1,0:T(8,128)}, f32[1024,256]{1,0:T(8,128)S(1)}, u32[]{:S(2)}) copy-start(f32[1024,256]{1,0:T(8,128)S(1)} %collective-permute-done.1) | copy-start | bytes 3145732
  32.5 6.5 %collective-permute-start.2 = (f32[1,4,32,256]{3,2,1,0:T(8,128)S(1)}, f32[1,4,32,256]{3,2,1,0:T(8,128)S(1)}, u32[]{:S(2)}, u32[]{:S(2)}) collective-permute-start(f32[1,4,32,256]{3,2,1,0:T(8,128)S(1)} %get-tuple-element.28), channel_id=1, source_target_pairs={{0,4},{4,0},{8,12},{12,8},{16,20},{20,16},{24,28},{28,24},{1,5},{5... | collective-permute-start | bytes 393224 | tf_op jit(solution)/shard_map/reduce0/ppermute | solution.py:193
  39.0 11.9 %collective-permute-start.6 = (f32[3,4,32,256]{3,2,1,0:T(8,128)}, f32[3,4,32,256]{3,2,1,0:T(8,128)}, u32[]{:S(2)}, u32[]{:S(2)}) collective-permute-start(f32[3,4,32,256]{3,2,1,0:T(8,128)} %get-tuple-element.30), channel_id=1, source_target_pairs={{0,4},{4,0},{8,12},{12,8},{16,20},{20,16},{24,28},{28,24},{1,5},{5... | collective-permute-start | bytes 1179656 | tf_op jit(solution)/shard_map/reduce1/ppermute | solution.py:198
  41.5 9.5 %collective-permute-start.3 = (f32[1,4,32,256]{3,2,1,0:T(8,128)}, f32[1,4,32,256]{3,2,1,0:T(8,128)}, u32[]{:S(2)}, u32[]{:S(2)}) collective-permute-start(f32[1,4,32,256]{3,2,1,0:T(8,128)} %add.44), channel_id=1, source_target_pairs={{0,16},{4,20},{1,17},{5,21},{2,18},{6,22},{3,19},{7,23}} | collective-permute-start | bytes 393224 | tf_op jit(solution)/shard_map/reduce0/ppermute | solution.py:196
  48.4 2.6 %collective-permute-start.4 = (f32[1,4,32,256]{3,2,1,0:T(8,128)}, f32[1,4,32,256]{3,2,1,0:T(8,128)}, u32[]{:S(2)}, u32[]{:S(2)}) collective-permute-start(f32[1,4,32,256]{3,2,1,0:T(8,128)} %add.44), channel_id=1, source_target_pairs={{8,16},{12,20},{9,17},{13,21},{10,18},{14,22},{11,19},{15,23}} | collective-permute-start | bytes 393224 | tf_op jit(solution)/shard_map/reduce0/ppermute | solution.py:196
  49.7 1.3 collective-permute-start.5
  51.0 26.0 %copy-start.1 = (f32[1024,256]{1,0:T(8,128)S(1)}, f32[1024,256]{1,0:T(8,128)}, u32[]{:S(2)}) copy-start(f32[1024,256]{1,0:T(8,128)} %copy-done) | copy-start | bytes 3145732
  52.1 14.5 %collective-permute-start.7 = (f32[3,4,32,256]{3,2,1,0:T(8,128)S(1)}, f32[3,4,32,256]{3,2,1,0:T(8,128)S(1)}, u32[]{:S(2)}, u32[]{:S(2)}) collective-permute-start(f32[3,4,32,256]{3,2,1,0:T(8,128)S(1)} %add.48), channel_id=1, source_target_pairs={{0,8},{4,12},{24,16},{28,20},{1,9},{5,13},{25,17},{29,21},{2,10},{... | collective-permute-start | bytes 1179656 | tf_op jit(solution)/shard_map/reduce1/ppermute | solution.py:209
  56.9 36.3 %collective-permute-start.9 = (f32[1024,256]{1,0:T(8,128)S(1)}, f32[1024,256]{1,0:T(8,128)S(1)}, u32[]{:S(2)}, u32[]{:S(2)}) collective-permute-start(f32[1024,256]{1,0:T(8,128)S(1)} %get-tuple-element.39), channel_id=1, source_target_pairs={{16,20},{20,16},{17,21},{21,17},{18,22},{22,18},{19,23},{23,19}} | collective-permute-start | bytes 3145736 | tf_op jit(solution)/shard_map/near2/ppermute | solution.py:152
  57.6 55.2 %collective-permute-start.14 = (f32[1024,256]{1,0:T(8,128)S(1)}, f32[1024,256]{1,0:T(8,128)S(1)}, u32[]{:S(2)}, u32[]{:S(2)}) collective-permute-start(f32[1024,256]{1,0:T(8,128)S(1)} %get-tuple-element.42), channel_id=1, source_target_pairs={{16,20},{17,21},{18,22},{19,23}} | collective-permute-start | bytes 3145736 | tf_op jit(solution)/shard_map/near3/ppermute | solution.py:152
  66.7 18.8 %copy-start.2 = (f32[4,1024,256]{2,1,0:T(8,128)S(1)}, f32[4,1024,256]{2,1,0:T(8,128)}, u32[]{:S(2)}) copy-start(f32[4,1024,256]{2,1,0:T(8,128)} %param.5) | copy-start | bytes 12582916
  66.7 10.2 %collective-permute-start.8 = (f32[3,4,32,256]{3,2,1,0:T(8,128)S(1)}, f32[3,4,32,256]{3,2,1,0:T(8,128)S(1)}, u32[]{:S(2)}, u32[]{:S(2)}) collective-permute-start(f32[3,4,32,256]{3,2,1,0:T(8,128)S(1)} %add.49), channel_id=1, source_target_pairs={{8,16},{12,20},{9,17},{13,21},{10,18},{14,22},{11,19},{15,23}} | collective-permute-start | bytes 1179656 | tf_op jit(solution)/shard_map/reduce1/ppermute | solution.py:209
  77.0 35.4 %collective-permute-start.13 = (f32[1024,256]{1,0:T(8,128)S(1)}, f32[1024,256]{1,0:T(8,128)S(1)}, u32[]{:S(2)}, u32[]{:S(2)}) collective-permute-start(f32[1024,256]{1,0:T(8,128)S(1)} %copy-done.1), channel_id=1, source_target_pairs={{28,20},{29,21},{30,22},{31,23}} | collective-permute-start | bytes 3145736 | tf_op jit(solution)/shard_map/across/ppermute | solution.py:152
  94.1 18.3 %copy-start.4 = (f32[1024,256]{1,0:T(8,128)S(1)}, f32[1024,256]{1,0:T(8,128)}, u32[]{:S(2)}) copy-start(f32[1024,256]{1,0:T(8,128)} %copy-done.3) | copy-start | bytes 3145732
  102.0 13.3 %collective-permute-start.10 = (f32[3,32,256]{2,1,0:T(8,128)S(1)}, f32[3,32,256]{2,1,0:T(8,128)S(1)}, u32[]{:S(2)}, u32[]{:S(2)}) collective-permute-start(f32[3,32,256]{2,1,0:T(8,128)S(1)} %get-tuple-element.43), channel_id=1, source_target_pairs={{16,0},{20,4},{17,1},{21,5},{18,2},{22,6},{19,3},{23,7}} | collective-permute-start | bytes 294920 | tf_op jit(solution)/shard_map/out/ppermute | solution.py:228
  103.3 12.7 %collective-permute-start.11 = (f32[3,32,256]{2,1,0:T(8,128)S(1)}, f32[3,32,256]{2,1,0:T(8,128)S(1)}, u32[]{:S(2)}, u32[]{:S(2)}) collective-permute-start(f32[3,32,256]{2,1,0:T(8,128)S(1)} %get-tuple-element.45), channel_id=1, source_target_pairs={{16,8},{20,12},{17,9},{21,13},{18,10},{22,14},{19,11},{23,15}} | collective-permute-start | bytes 294920 | tf_op jit(solution)/shard_map/out/ppermute | solution.py:228
  104.0 12.0 %collective-permute-start.12 = (f32[3,32,256]{2,1,0:T(8,128)S(1)}, f32[3,32,256]{2,1,0:T(8,128)S(1)}, u32[]{:S(2)}, u32[]{:S(2)}) collective-permute-start(f32[3,32,256]{2,1,0:T(8,128)S(1)} %get-tuple-element.44), channel_id=1, source_target_pairs={{16,24},{20,28},{17,25},{21,29},{18,26},{22,30},{19,27},{23,31}} | collective-permute-start | bytes 294920 | tf_op jit(solution)/shard_map/out/ppermute | solution.py:228
  113.3 12.7 %collective-permute-start.15 = (f32[1,32,256]{2,1,0:T(8,128)S(1)}, f32[1,32,256]{2,1,0:T(8,128)S(1)}, u32[]{:S(2)}, u32[]{:S(2)}) collective-permute-start(f32[1,32,256]{2,1,0:T(8,128)S(1)} %get-tuple-element.49), channel_id=1, source_target_pairs={{16,0},{20,4},{17,1},{21,5},{18,2},{22,6},{19,3},{23,7}} | collective-permute-start | bytes 98312 | tf_op jit(solution)/shard_map/out_last/ppermute | solution.py:228
  114.6 11.4 %collective-permute-start.16 = (f32[1,32,256]{2,1,0:T(8,128)S(1)}, f32[1,32,256]{2,1,0:T(8,128)S(1)}, u32[]{:S(2)}, u32[]{:S(2)}) collective-permute-start(f32[1,32,256]{2,1,0:T(8,128)S(1)} %get-tuple-element.51), channel_id=1, source_target_pairs={{16,8},{20,12},{17,9},{21,13},{18,10},{22,14},{19,11},{23,15}} | collective-permute-start | bytes 98312 | tf_op jit(solution)/shard_map/out_last/ppermute | solution.py:228
  115.3 10.8 %collective-permute-start.17 = (f32[1,32,256]{2,1,0:T(8,128)S(1)}, f32[1,32,256]{2,1,0:T(8,128)S(1)}, u32[]{:S(2)}, u32[]{:S(2)}) collective-permute-start(f32[1,32,256]{2,1,0:T(8,128)S(1)} %get-tuple-element.50), channel_id=1, source_target_pairs={{16,24},{20,28},{17,25},{21,29},{18,26},{22,30},{19,27},{23,31}} | collective-permute-start | bytes 98312 | tf_op jit(solution)/shard_map/out_last/ppermute | solution.py:228

commit v5 on v4

--- a/solution.py
+++ b/solution.py
@@ -189,28 +189,28 @@
     def moves_to(moves):
         return [(2 * a + k, 2 * b + k) for a, b in moves for k in (0, 1)]
 
+    def bring_home(values, places):
+        return [lax.ppermute(values, "row", moves_to([(place, home)])) for place in places if place != home]
+
     with jax.named_scope("reduce0"):
         arrived = lax.ppermute(sends[0], "row", swap_pairs(rows, 1))
         lead = keeps[0] + arrived
-        places = [place for place in range(pieces) if place != home]
-        straight = [lax.ppermute(lead, "row", moves_to([(place, home)])) for place in places]
+        lead_shares = bring_home(lead, range(pieces))
     with jax.named_scope("reduce1"):
         trail_arrived = lax.ppermute(*wait(arrived, (sends[1],)), "row", swap_pairs(rows, 1))
-    after_trail = wait(trail_arrived, (near[0], *ahead[1:]))
-    with jax.named_scope("near2"):
-        near.append(among([(0, 1), (1, 0)], after_trail[1]))
-    *straight, trail_arrived = lax.optimization_barrier((*straight, trail_arrived))
+    after_lead = wait(lead, ahead[1:])
+    *lead_shares, trail_arrived = lax.optimization_barrier((*lead_shares, trail_arrived))
     with jax.named_scope("reduce0"):
-        for one in straight:
-            lead = lead + one
+        lead = sum(lead_shares, lead)
     with jax.named_scope("reduce1"):
         trail = keeps[1] + trail_arrived
-        for moves in line_steps(pieces, home):
-            trail = trail + lax.ppermute(trail, "row", moves_to(moves))
+        trail = sum(bring_home(trail, range(pieces)[::-1]), trail)
+    with jax.named_scope("near2"):
+        near.append(among([(0, 1), (1, 0)], after_lead[0]))
+    with jax.named_scope("near3"):
+        near.append(among([(0, 1)], after_lead[1]))
     with jax.named_scope("across"):
         across = among([(3, 1)], *wait(trail, (near[0],)))
-    with jax.named_scope("near3"):
-        near.append(among([(0, 1)], after_trail[2]))
     residual = [one.reshape(pieces * part, width) for one in (*lead, *trail)]
 
     def between(i, j):
@@ -222,7 +222,7 @@
     def hand_out(values):
         parts = values.reshape(-1, pieces, part, width)
         result = jnp.where(row // 2 == home, parts[:, home], 0.0)
-        for piece in range(pieces):
+        for piece in sorted(range(pieces), key=lambda place: abs(place - home)):
             if piece != home:
                 pairs = [(base_row + k, 2 * piece + k) for k in (0, 1)]
                 result = result + lax.ppermute(parts[:, piece], "row", pairs)
@@ -246,7 +246,8 @@
         own = hand_out(residual[-1])[0]
         own_solved = dot(gather_col(own), inverse[window - 1])
     with jax.named_scope("out"):
-        result = jnp.concatenate([hand_out(jnp.stack(solved)), own_solved[None]])
+        rest = hand_out(*wait(residual[-1], (jnp.stack(solved),)))
+        result = jnp.concatenate([rest, own_solved[None]])
     return result.transpose(0, 2, 1)
 
 

time: 133 us -> 130 us (0.977)
  waiting for transfers between devices: 13.6 us -> 6.25 us
  starting transfers between devices: 28.7 us -> 32.9 us
    ppermute x6, waiting for transfers between devices: 10 us -> 2.72 us  [hand_out(): result = result + lax.ppermute(parts[:, piece], 'row', pairs)]
    ppermute x5 -> x6, starting transfers between devices: 15.1 us -> 19.1 us  [bring_home(): lax.ppermute(values, 'row', moves_to([(place, home)]))]
  transfers between devices with their start and end apart: 18 -> 19, of which waited for: 2 -> 2; matrix products, arithmetic and copies ran while one was open for 6% -> 6% of each run, Pallas kernels for 21% -> 22%
where the time goes in v5:
time: 130 us; the launch traced here: 129 us
  blocking collectives  49.1 us (38%)
  starting transfers between devices  32.9 us (25%)
  Pallas kernels  31 us (24%)
  waiting for transfers between devices  6.25 us (5%)
  matrix products  5.58 us (4%)
  other arithmetic  3.69 us (3%)
    all_gather x7, blocking collectives, gather_col(): return lax.all_gather(block, 'col', axis=1, tiled=True)  49.1 us
    pallas_call x1, Pallas kernels, on_device(): pl.pallas_call(functools.partial(prefix_kernel, (rows, window, tiles, fir...  27.8 us
    ppermute x6, starting transfers between devices, bring_home(): lax.ppermute(values, 'row', moves_to([(place, home)]))  19.1 us
    dot_general x10, matrix products, dot(): jnp.dot(left, right, precision=lax.Precision.HIGH, preferred_element_type...  5.58 us
    ppermute x6, starting transfers between devices, hand_out(): result = result + lax.ppermute(parts[:, piece], 'row', pairs)  5.24 us
    ppermute x5, starting transfers between devices, among(): lax.ppermute(payload, 'row', [(base_row + a, base_row + b) for a, b in pa...  3.76 us
    ppermute x1, waiting for transfers between devices, on_device(): arrived = lax.ppermute(sends[0], 'row', swap_pairs(rows, 1))  3.5 us
    pallas_call x1, Pallas kernels, on_device(): pl.pallas_call(functools.partial(window_kernel, window, tiles), grid=(cut...  3.16 us
  transfers between devices with their start and end apart: 19, of which 2 were waited for; matrix products, arithmetic and copies ran while one was open for 6% of the time, Pallas kernels for 22%

profile of v5, /device:TPU:0, one launch (start us, length us, event | category | flops | bytes accessed | tf_op | source)
XLA Modules:
  0.0 129.0 jit_solution(17986677873189079580)
XLA Ops:
  0.0 3.2 %shard_map.38 = (f32[1024,256]{1,0:T(8,128)S(1)}, f32[1024,256]{1,0:T(8,128)S(1)}, f32[1024,256]{1,0:T(8,128)S(1)}) custom-call(f32[98304,128]{1,0:T(8,128)} %bitcast.100), custom_call_target="tpu_custom_call" | custom-call | tf_op jit(solution)/shard_map/pallas_call | solution.py:142
  3.2 0.7 collective-permute-start
  3.9 0.7 collective-permute-start.1
  4.6 27.8 %shard_map.37 = (f32[1,4,32,256]{3,2,1,0:T(8,128)S(1)}, f32[3,4,32,256]{3,2,1,0:T(8,128)S(1)}, f32[1,4,32,256]{3,2,1,0:T(8,128)S(1)}, f32[3,4,32,256]{3,2,1,0:T(8,128)}) custom-call(f32[12288,256]{1,0:T(8,128)} %bitcast.109, f32[12288,8,1,128]{3,2,1,0:T(1,128)} %bitcast.101, f32[12288,8,1,128]{3,2,1,0:T(1,128)} %bitcast.102, f32[12288,8,1,128]{3,2,1,0:T(1,128)} %bitcast.103, ...), custom_call_target="tpu_custom_call" | custom-call | flops 19327352832 | bytes 62914560 | tf_op jit(solution)/shard_map/pallas_call | solution.py:163
  32.5 0.0 collective-permute-done
  32.5 3.0 %collective-permute-start.2 = (f32[1,4,32,256]{3,2,1,0:T(8,128)S(1)}, f32[1,4,32,256]{3,2,1,0:T(8,128)S(1)}, u32[]{:S(2)}, u32[]{:S(2)}) collective-permute-start(f32[1,4,32,256]{3,2,1,0:T(8,128)S(1)} %get-tuple-element.30), channel_id=1, source_target_pairs={{0,4},{4,0},{8,12},{12,8},{16,20},{20,16},{24,28},{28,24},{1,5},{5... | collective-permute-start | bytes 393224 | tf_op jit(solution)/shard_map/reduce0/ppermute | solution.py:196
  35.6 3.5 %collective-permute-done.2 = f32[1,4,32,256]{3,2,1,0:T(8,128)S(1)} collective-permute-done((f32[1,4,32,256]{3,2,1,0:T(8,128)S(1)}, f32[1,4,32,256]{3,2,1,0:T(8,128)S(1)}, u32[]{:S(2)}, u32[]{:S(2)}) %collective-permute-start.2) | collective-permute-done | bytes 131104 | tf_op jit(solution)/shard_map/reduce0/ppermute | solution.py:196
  39.0 1.7 %collective-permute-start.6 = (f32[3,4,32,256]{3,2,1,0:T(8,128)}, f32[3,4,32,256]{3,2,1,0:T(8,128)}, u32[]{:S(2)}, u32[]{:S(2)}) collective-permute-start(f32[3,4,32,256]{3,2,1,0:T(8,128)} %get-tuple-element.32), channel_id=1, source_target_pairs={{0,4},{4,0},{8,12},{12,8},{16,20},{20,16},{24,28},{28,24},{1,5},{5... | collective-permute-start | bytes 1179656 | tf_op jit(solution)/shard_map/reduce1/ppermute | solution.py:200
  40.8 0.7 add.47
  41.5 6.9 %collective-permute-start.3 = (f32[1,4,32,256]{3,2,1,0:T(8,128)}, f32[1,4,32,256]{3,2,1,0:T(8,128)}, u32[]{:S(2)}, u32[]{:S(2)}) collective-permute-start(f32[1,4,32,256]{3,2,1,0:T(8,128)} %add.47), channel_id=1, source_target_pairs={{0,16},{4,20},{1,17},{5,21},{2,18},{6,22},{3,19},{7,23}} | collective-permute-start | bytes 393224 | tf_op jit(solution)/shard_map/reduce0/ppermute | solution.py:193
  48.4 1.3 %collective-permute-start.4 = (f32[1,4,32,256]{3,2,1,0:T(8,128)}, f32[1,4,32,256]{3,2,1,0:T(8,128)}, u32[]{:S(2)}, u32[]{:S(2)}) collective-permute-start(f32[1,4,32,256]{3,2,1,0:T(8,128)} %add.47), channel_id=1, source_target_pairs={{8,16},{12,20},{9,17},{13,21},{10,18},{14,22},{11,19},{15,23}} | collective-permute-start | bytes 393224 | tf_op jit(solution)/shard_map/reduce0/ppermute | solution.py:193
  49.7 1.3 %collective-permute-start.5 = (f32[1,4,32,256]{3,2,1,0:T(8,128)}, f32[1,4,32,256]{3,2,1,0:T(8,128)}, u32[]{:S(2)}, u32[]{:S(2)}) collective-permute-start(f32[1,4,32,256]{3,2,1,0:T(8,128)} %add.47), channel_id=1, source_target_pairs={{24,16},{28,20},{25,17},{29,21},{26,18},{30,22},{27,19},{31,23}} | collective-permute-start | bytes 393224 | tf_op jit(solution)/shard_map/reduce0/ppermute | solution.py:193
  51.0 0.8 collective-permute-start.10
  51.8 0.7 collective-permute-start.12
  52.6 0.0 collective-permute-done.6
  52.6 1.0 add.48
  53.7 0.7 collective-permute-start.7
  54.4 0.7 collective-permute-start.8
  55.0 8.3 %collective-permute-start.9 = (f32[3,4,32,256]{3,2,1,0:T(8,128)S(1)}, f32[3,4,32,256]{3,2,1,0:T(8,128)S(1)}, u32[]{:S(2)}, u32[]{:S(2)}) collective-permute-start(f32[3,4,32,256]{3,2,1,0:T(8,128)S(1)} %add.48), channel_id=1, source_target_pairs={{0,16},{4,20},{1,17},{5,21},{2,18},{6,22},{3,19},{7,23}} | collective-permute-start | bytes 1179656 | tf_op jit(solution)/shard_map/reduce1/ppermute | solution.py:193
  63.3 1.1 add_add_fusion.1
  64.4 7.2 %all_gather.21 = f32[128,1024]{1,0:T(8,128)S(1)} all-gather(f32[128,256]{1,0:T(8,128)S(1)} %bitcast.115), channel_id=1, replica_groups=mesh['row'=8,'col'=4] {'col'}, dimensions={1}, use_global_device_ids=true | all-gather | bytes 655360 | tf_op jit(solution)/shard_map/solve0/all_gather | solution.py:120
  71.6 1.8 %fusion.5 = f32[128,256]{1,0:T(8,128)S(1)} fusion(f32[128,1024]{1,0:T(8,128)S(1)} %all_gather.21, f32[4,1024,256]{2,1,0:T(8,128)} %param.5), kind=kOutput, calls=%fused_computation.6 | convolution fusion | flops 201326592 | bytes 1703936 | tf_op jit(solution)/shard_map/solve0/dot_general | solution.py:93
  73.4 7.3 %all_gather.22 = f32[128,1024]{1,0:T(8,128)S(1)} all-gather(f32[128,256]{1,0:T(8,128)S(1)} %fusion.5), channel_id=1, replica_groups=mesh['row'=8,'col'=4] {'col'}, dimensions={1}, use_global_device_ids=true | all-gather | bytes 655360 | tf_op jit(solution)/shard_map/solve0/all_gather | solution.py:120
  80.7 0.0 collective-permute-done.7
  80.7 0.1 add_add_fusion
  80.9 0.7 collective-permute-start.11
  81.6 0.4 bitcast_subtract_fusion.1
  82.0 7.3 %all_gather.23 = f32[128,1024]{1,0:T(8,128)S(1)} all-gather(f32[128,256]{1,0:T(8,128)S(1)} %bitcast_subtract_fusion.1), channel_id=1, replica_groups=mesh['row'=8,'col'=4] {'col'}, dimensions={1}, use_global_device_ids=true | all-gather | bytes 655360 | tf_op jit(solution)/shard_map/solve1/all_gather | solution.py:120
  89.3 0.4 fusion.3
  89.8 7.3 %all_gather.24 = f32[128,1024]{1,0:T(8,128)S(1)} all-gather(f32[128,256]{1,0:T(8,128)S(1)} %fusion.3), channel_id=1, replica_groups=mesh['row'=8,'col'=4] {'col'}, dimensions={1}, use_global_device_ids=true | all-gather | bytes 655360 | tf_op jit(solution)/shard_map/solve1/all_gather | solution.py:120
  97.1 0.4 fusion.15
  97.5 0.4 fusion.30
  97.9 7.3 %all_gather.25 = f32[128,1024]{1,0:T(8,128)S(1)} all-gather(f32[128,256]{1,0:T(8,128)S(1)} %fusion.30), channel_id=1, replica_groups=mesh['row'=8,'col'=4] {'col'}, dimensions={1}, use_global_device_ids=true | all-gather | bytes 655360 | tf_op jit(solution)/shard_map/solve2/all_gather | solution.py:120
  105.2 0.4 fusion.1
  105.7 7.3 %all_gather.26 = f32[128,1024]{1,0:T(8,128)S(1)} all-gather(f32[128,256]{1,0:T(8,128)S(1)} %fusion.1), channel_id=1, replica_groups=mesh['row'=8,'col'=4] {'col'}, dimensions={1}, use_global_device_ids=true | all-gather | bytes 655360 | tf_op jit(solution)/shard_map/solve2/all_gather | solution.py:120
  113.0 0.4 fusion.17
  113.4 0.4 fusion.10
  113.9 0.4 fusion.32
  114.4 0.7 collective-permute-start.16
  115.0 0.7 collective-permute-start.17
  115.7 1.3 %collective-permute-start.18 = (f32[1,32,256]{2,1,0:T(8,128)S(1)}, f32[1,32,256]{2,1,0:T(8,128)S(1)}, u32[]{:S(2)}, u32[]{:S(2)}) collective-permute-start(f32[1,32,256]{2,1,0:T(8,128)S(1)} %get-tuple-element.52), channel_id=1, source_target_pairs={{16,0},{20,4},{17,1},{21,5},{18,2},{22,6},{19,3},{23,7}} | collective-permute-start | bytes 98312 | tf_op jit(solution)/shard_map/out_last/ppermute | solution.py:228
  117.0 0.7 collective-permute-start.13
  117.7 0.7 collective-permute-start.14
  118.4 1.3 %collective-permute-start.15 = (f32[3,32,256]{2,1,0:T(8,128)S(1)}, f32[3,32,256]{2,1,0:T(8,128)S(1)}, u32[]{:S(2)}, u32[]{:S(2)}) collective-permute-start(f32[3,32,256]{2,1,0:T(8,128)S(1)} %get-tuple-element.47), channel_id=1, source_target_pairs={{16,0},{20,4},{17,1},{21,5},{18,2},{22,6},{19,3},{23,7}} | collective-permute-start | bytes 294920 | tf_op jit(solution)/shard_map/out/ppermute | solution.py:228
  119.7 2.7 %collective-permute-done.18 = f32[1,32,256]{2,1,0:T(8,128)S(1)} collective-permute-done((f32[1,32,256]{2,1,0:T(8,128)S(1)}, f32[1,32,256]{2,1,0:T(8,128)S(1)}, u32[]{:S(2)}, u32[]{:S(2)}) %collective-permute-start.18) | collective-permute-done | bytes 32800 | tf_op jit(solution)/shard_map/out_last/ppermute | solution.py:228
  122.4 5.4 %all-gather = f32[1,32,1024]{2,1,0:T(8,128)S(1)} all-gather(f32[1,32,256]{2,1,0:T(8,128)S(1)} %fusion.41), channel_id=2, replica_groups=mesh['row'=8,'col'=4] {'col'}, dimensions={2}, use_global_device_ids=true | all-gather | bytes 163840 | tf_op jit(solution)/shard_map/out_last/all_gather | solution.py:120
  127.8 0.4 convolution_bitcast_fusion
  128.3 0.7 maximum_bitcast_fusion
  (30 shorter events, 0.2 us)
Async XLA Ops:
  3.2 29.3 %collective-permute-start = (f32[1024,256]{1,0:T(8,128)S(1)}, f32[1024,256]{1,0:T(8,128)S(1)}, u32[]{:S(2)}, u32[]{:S(2)}) collective-permute-start(f32[1024,256]{1,0:T(8,128)S(1)} %get-tuple-element.29), channel_id=1, source_target_pairs={{16,20},{20,16},{24,28},{17,21},{21,17},{25,29},{18,22},{22,18},{2... | collective-permute-start | bytes 3145736 | tf_op jit(solution)/shard_map/near1/ppermute | solution.py:152
  3.9 28.6 %collective-permute-start.1 = (f32[1024,256]{1,0:T(8,128)S(1)}, f32[1024,256]{1,0:T(8,128)S(1)}, u32[]{:S(2)}, u32[]{:S(2)}) collective-permute-start(f32[1024,256]{1,0:T(8,128)S(1)} %get-tuple-element.29), channel_id=1, source_target_pairs={{24,16},{25,17},{26,18},{27,19}} | collective-permute-start | bytes 3145736 | tf_op jit(solution)/shard_map/far/ppermute | solution.py:152
  32.5 9.0 %copy-start = (f32[1024,256]{1,0:T(8,128)}, f32[1024,256]{1,0:T(8,128)S(1)}, u32[]{:S(2)}) copy-start(f32[1024,256]{1,0:T(8,128)S(1)} %collective-permute-done) | copy-start | bytes 3145732
  32.5 15.8 %copy-start.3 = (f32[1024,256]{1,0:T(8,128)}, f32[1024,256]{1,0:T(8,128)S(1)}, u32[]{:S(2)}) copy-start(f32[1024,256]{1,0:T(8,128)S(1)} %collective-permute-done.1) | copy-start | bytes 3145732
  32.5 6.5 %collective-permute-start.2 = (f32[1,4,32,256]{3,2,1,0:T(8,128)S(1)}, f32[1,4,32,256]{3,2,1,0:T(8,128)S(1)}, u32[]{:S(2)}, u32[]{:S(2)}) collective-permute-start(f32[1,4,32,256]{3,2,1,0:T(8,128)S(1)} %get-tuple-element.30), channel_id=1, source_target_pairs={{0,4},{4,0},{8,12},{12,8},{16,20},{20,16},{24,28},{28,24},{1,5},{5... | collective-permute-start | bytes 393224 | tf_op jit(solution)/shard_map/reduce0/ppermute | solution.py:196
  39.0 13.5 %collective-permute-start.6 = (f32[3,4,32,256]{3,2,1,0:T(8,128)}, f32[3,4,32,256]{3,2,1,0:T(8,128)}, u32[]{:S(2)}, u32[]{:S(2)}) collective-permute-start(f32[3,4,32,256]{3,2,1,0:T(8,128)} %get-tuple-element.32), channel_id=1, source_target_pairs={{0,4},{4,0},{8,12},{12,8},{16,20},{20,16},{24,28},{28,24},{1,5},{5... | collective-permute-start | bytes 1179656 | tf_op jit(solution)/shard_map/reduce1/ppermute | solution.py:200
  41.5 10.4 %collective-permute-start.3 = (f32[1,4,32,256]{3,2,1,0:T(8,128)}, f32[1,4,32,256]{3,2,1,0:T(8,128)}, u32[]{:S(2)}, u32[]{:S(2)}) collective-permute-start(f32[1,4,32,256]{3,2,1,0:T(8,128)} %add.47), channel_id=1, source_target_pairs={{0,16},{4,20},{1,17},{5,21},{2,18},{6,22},{3,19},{7,23}} | collective-permute-start | bytes 393224 | tf_op jit(solution)/shard_map/reduce0/ppermute | solution.py:193
  48.4 4.2 %collective-permute-start.4 = (f32[1,4,32,256]{3,2,1,0:T(8,128)}, f32[1,4,32,256]{3,2,1,0:T(8,128)}, u32[]{:S(2)}, u32[]{:S(2)}) collective-permute-start(f32[1,4,32,256]{3,2,1,0:T(8,128)} %add.47), channel_id=1, source_target_pairs={{8,16},{12,20},{9,17},{13,21},{10,18},{14,22},{11,19},{15,23}} | collective-permute-start | bytes 393224 | tf_op jit(solution)/shard_map/reduce0/ppermute | solution.py:193
  49.7 2.9 %collective-permute-start.5 = (f32[1,4,32,256]{3,2,1,0:T(8,128)}, f32[1,4,32,256]{3,2,1,0:T(8,128)}, u32[]{:S(2)}, u32[]{:S(2)}) collective-permute-start(f32[1,4,32,256]{3,2,1,0:T(8,128)} %add.47), channel_id=1, source_target_pairs={{24,16},{28,20},{25,17},{29,21},{26,18},{30,22},{27,19},{31,23}} | collective-permute-start | bytes 393224 | tf_op jit(solution)/shard_map/reduce0/ppermute | solution.py:193
  51.0 29.9 %copy-start.1 = (f32[1024,256]{1,0:T(8,128)S(1)}, f32[1024,256]{1,0:T(8,128)}, u32[]{:S(2)}) copy-start(f32[1024,256]{1,0:T(8,128)} %copy-done) | copy-start | bytes 3145732
  51.0 46.1 %collective-permute-start.10 = (f32[1024,256]{1,0:T(8,128)S(1)}, f32[1024,256]{1,0:T(8,128)S(1)}, u32[]{:S(2)}, u32[]{:S(2)}) collective-permute-start(f32[1024,256]{1,0:T(8,128)S(1)} %get-tuple-element.40), channel_id=1, source_target_pairs={{16,20},{20,16},{17,21},{21,17},{18,22},{22,18},{19,23},{23,19}} | collective-permute-start | bytes 3145736 | tf_op jit(solution)/shard_map/near2/ppermute | solution.py:152
  51.8 62.1 %collective-permute-start.12 = (f32[1024,256]{1,0:T(8,128)S(1)}, f32[1024,256]{1,0:T(8,128)S(1)}, u32[]{:S(2)}, u32[]{:S(2)}) collective-permute-start(f32[1024,256]{1,0:T(8,128)S(1)} %get-tuple-element.43), channel_id=1, source_target_pairs={{16,20},{17,21},{18,22},{19,23}} | collective-permute-start | bytes 3145736 | tf_op jit(solution)/shard_map/near3/ppermute | solution.py:152
  53.7 27.0 %collective-permute-start.7 = (f32[3,4,32,256]{3,2,1,0:T(8,128)S(1)}, f32[3,4,32,256]{3,2,1,0:T(8,128)S(1)}, u32[]{:S(2)}, u32[]{:S(2)}) collective-permute-start(f32[3,4,32,256]{3,2,1,0:T(8,128)S(1)} %add.48), channel_id=1, source_target_pairs={{24,16},{28,20},{25,17},{29,21},{26,18},{30,22},{27,19},{31,23}} | collective-permute-start | bytes 1179656 | tf_op jit(solution)/shard_map/reduce1/ppermute | solution.py:193
  54.4 26.4 %collective-permute-start.8 = (f32[3,4,32,256]{3,2,1,0:T(8,128)S(1)}, f32[3,4,32,256]{3,2,1,0:T(8,128)S(1)}, u32[]{:S(2)}, u32[]{:S(2)}) collective-permute-start(f32[3,4,32,256]{3,2,1,0:T(8,128)S(1)} %add.48), channel_id=1, source_target_pairs={{8,16},{12,20},{9,17},{13,21},{10,18},{14,22},{11,19},{15,23}} | collective-permute-start | bytes 1179656 | tf_op jit(solution)/shard_map/reduce1/ppermute | solution.py:193
  55.0 25.7 %collective-permute-start.9 = (f32[3,4,32,256]{3,2,1,0:T(8,128)S(1)}, f32[3,4,32,256]{3,2,1,0:T(8,128)S(1)}, u32[]{:S(2)}, u32[]{:S(2)}) collective-permute-start(f32[3,4,32,256]{3,2,1,0:T(8,128)S(1)} %add.48), channel_id=1, source_target_pairs={{0,16},{4,20},{1,17},{5,21},{2,18},{6,22},{3,19},{7,23}} | collective-permute-start | bytes 1179656 | tf_op jit(solution)/shard_map/reduce1/ppermute | solution.py:193
  71.6 17.7 %copy-start.2 = (f32[4,1024,256]{2,1,0:T(8,128)S(1)}, f32[4,1024,256]{2,1,0:T(8,128)}, u32[]{:S(2)}) copy-start(f32[4,1024,256]{2,1,0:T(8,128)} %param.5) | copy-start | bytes 12582916
  80.9 32.6 %collective-permute-start.11 = (f32[1024,256]{1,0:T(8,128)S(1)}, f32[1024,256]{1,0:T(8,128)S(1)}, u32[]{:S(2)}, u32[]{:S(2)}) collective-permute-start(f32[1024,256]{1,0:T(8,128)S(1)} %copy-done.1), channel_id=1, source_target_pairs={{28,20},{29,21},{30,22},{31,23}} | collective-permute-start | bytes 3145736 | tf_op jit(solution)/shard_map/across/ppermute | solution.py:152
  97.5 15.9 %copy-start.4 = (f32[1024,256]{1,0:T(8,128)S(1)}, f32[1024,256]{1,0:T(8,128)}, u32[]{:S(2)}) copy-start(f32[1024,256]{1,0:T(8,128)} %copy-done.3) | copy-start | bytes 3145732
  114.4 4.0 %collective-permute-start.16 = (f32[1,32,256]{2,1,0:T(8,128)S(1)}, f32[1,32,256]{2,1,0:T(8,128)S(1)}, u32[]{:S(2)}, u32[]{:S(2)}) collective-permute-start(f32[1,32,256]{2,1,0:T(8,128)S(1)} %get-tuple-element.51), channel_id=1, source_target_pairs={{16,8},{20,12},{17,9},{21,13},{18,10},{22,14},{19,11},{23,15}} | collective-permute-start | bytes 98312 | tf_op jit(solution)/shard_map/out_last/ppermute | solution.py:228
  115.0 4.7 %collective-permute-start.17 = (f32[1,32,256]{2,1,0:T(8,128)S(1)}, f32[1,32,256]{2,1,0:T(8,128)S(1)}, u32[]{:S(2)}, u32[]{:S(2)}) collective-permute-start(f32[1,32,256]{2,1,0:T(8,128)S(1)} %get-tuple-element.53), channel_id=1, source_target_pairs={{16,24},{20,28},{17,25},{21,29},{18,26},{22,30},{19,27},{23,31}} | collective-permute-start | bytes 98312 | tf_op jit(solution)/shard_map/out_last/ppermute | solution.py:228
  115.7 6.7 %collective-permute-start.18 = (f32[1,32,256]{2,1,0:T(8,128)S(1)}, f32[1,32,256]{2,1,0:T(8,128)S(1)}, u32[]{:S(2)}, u32[]{:S(2)}) collective-permute-start(f32[1,32,256]{2,1,0:T(8,128)S(1)} %get-tuple-element.52), channel_id=1, source_target_pairs={{16,0},{20,4},{17,1},{21,5},{18,2},{22,6},{19,3},{23,7}} | collective-permute-start | bytes 98312 | tf_op jit(solution)/shard_map/out_last/ppermute | solution.py:228
  117.0 11.2 %collective-permute-start.13 = (f32[3,32,256]{2,1,0:T(8,128)S(1)}, f32[3,32,256]{2,1,0:T(8,128)S(1)}, u32[]{:S(2)}, u32[]{:S(2)}) collective-permute-start(f32[3,32,256]{2,1,0:T(8,128)S(1)} %get-tuple-element.45), channel_id=1, source_target_pairs={{16,8},{20,12},{17,9},{21,13},{18,10},{22,14},{19,11},{23,15}} | collective-permute-start | bytes 294920 | tf_op jit(solution)/shard_map/out/ppermute | solution.py:228
  117.7 10.6 %collective-permute-start.14 = (f32[3,32,256]{2,1,0:T(8,128)S(1)}, f32[3,32,256]{2,1,0:T(8,128)S(1)}, u32[]{:S(2)}, u32[]{:S(2)}) collective-permute-start(f32[3,32,256]{2,1,0:T(8,128)S(1)} %get-tuple-element.46), channel_id=1, source_target_pairs={{16,24},{20,28},{17,25},{21,29},{18,26},{22,30},{19,27},{23,31}} | collective-permute-start | bytes 294920 | tf_op jit(solution)/shard_map/out/ppermute | solution.py:228
  118.4 9.9 %collective-permute-start.15 = (f32[3,32,256]{2,1,0:T(8,128)S(1)}, f32[3,32,256]{2,1,0:T(8,128)S(1)}, u32[]{:S(2)}, u32[]{:S(2)}) collective-permute-start(f32[3,32,256]{2,1,0:T(8,128)S(1)} %get-tuple-element.47), channel_id=1, source_target_pairs={{16,0},{20,4},{17,1},{21,5},{18,2},{22,6},{19,3},{23,7}} | collective-permute-start | bytes 294920 | tf_op jit(solution)/shard_map/out/ppermute | solution.py:228

commit v6 on v5

--- a/solution.py
+++ b/solution.py
@@ -156,7 +156,7 @@
     with jax.named_scope("far"):
         far = among([(2, 0)], ahead[0])
 
-    sizes = (1, window - 1)
+    sizes = (1, 1, window - 2)
     shapes = [(size, pieces, part, width) for size in sizes] * 2
     per_step = 2 if blocks % 2 == 0 else 1
     depth = per_step * order
@@ -189,29 +189,28 @@
     def moves_to(moves):
         return [(2 * a + k, 2 * b + k) for a, b in moves for k in (0, 1)]
 
-    def bring_home(values, places):
-        return [lax.ppermute(values, "row", moves_to([(place, home)])) for place in places if place != home]
-
+    steps = [moves_to(moves) for moves in line_steps(pieces, home)]
     with jax.named_scope("reduce0"):
         arrived = lax.ppermute(sends[0], "row", swap_pairs(rows, 1))
         lead = keeps[0] + arrived
-        lead_shares = bring_home(lead, range(pieces))
+        places = [place for place in range(pieces) if place != home]
+        lead_shares = [lax.ppermute(lead, "row", moves_to([(place, home)])) for place in places]
+    after_arrival = wait(arrived, sends[1:])
+    after_lead = wait(lead, ahead[1:])
     with jax.named_scope("reduce1"):
-        trail_arrived = lax.ppermute(*wait(arrived, (sends[1],)), "row", swap_pairs(rows, 1))
-    after_lead = wait(lead, ahead[1:])
-    *lead_shares, trail_arrived = lax.optimization_barrier((*lead_shares, trail_arrived))
-    with jax.named_scope("reduce0"):
-        lead = sum(lead_shares, lead)
-    with jax.named_scope("reduce1"):
-        trail = keeps[1] + trail_arrived
-        trail = sum(bring_home(trail, range(pieces)[::-1]), trail)
+        second = keeps[1] + lax.ppermute(after_arrival[0], "row", swap_pairs(rows, 1))
+        for pairs in steps:
+            second = second + lax.ppermute(second, "row", pairs)
+    with jax.named_scope("reduce2"):
+        others = keeps[2] + lax.ppermute(after_arrival[1], "row", swap_pairs(rows, 1))
+        others_arrived = lax.ppermute(others, "row", steps[0])
     with jax.named_scope("near2"):
         near.append(among([(0, 1), (1, 0)], after_lead[0]))
     with jax.named_scope("near3"):
         near.append(among([(0, 1)], after_lead[1]))
-    with jax.named_scope("across"):
-        across = among([(3, 1)], *wait(trail, (near[0],)))
-    residual = [one.reshape(pieces * part, width) for one in (*lead, *trail)]
+    with jax.named_scope("reduce0"):
+        lead = sum(lead_shares, lead)
+    residual = [one.reshape(pieces * part, width) for one in (*lead, *second)]
 
     def between(i, j):
         if i < 2:
@@ -222,7 +221,7 @@
     def hand_out(values):
         parts = values.reshape(-1, pieces, part, width)
         result = jnp.where(row // 2 == home, parts[:, home], 0.0)
-        for piece in sorted(range(pieces), key=lambda place: abs(place - home)):
+        for piece in sorted(range(pieces), key=lambda place: -abs(place - home)):
             if piece != home:
                 pairs = [(base_row + k, 2 * piece + k) for k in (0, 1)]
                 result = result + lax.ppermute(parts[:, piece], "row", pairs)
@@ -234,6 +233,15 @@
             solved.append(dot(gather_col(residual[j]), inverse[j]))
             x = gather_col(solved[j])
         if j == 0:
+            with jax.named_scope("reduce2"):
+                x, others_arrived = lax.optimization_barrier((x, others_arrived))
+                others = others + others_arrived
+            with jax.named_scope("across"):
+                across = among([(3, 1)], *wait(others, (near[0],)))
+            with jax.named_scope("reduce2"):
+                for pairs in steps[1:]:
+                    others = others + lax.ppermute(others, "row", pairs)
+            residual += [one.reshape(pieces * part, width) for one in others]
             corner = x
         for k in range(j + 1, window):
             with jax.named_scope(f"term{j}{k}"):

time: 130 us -> 129 us (level); the launches traced: 129 us -> 127 us
  starting transfers between devices: 32.9 us -> 30.4 us
    ppermute x7 -> x9, starting transfers between devices: 20.9 us -> 18.5 us  [the longest x3 9.5 us: on_device(): lax.ppermute(lead, 'row', moves_to([(place, home)]))]
  transfers between devices with their start and end apart: 19 -> 21, of which waited for: 2 -> 3; matrix products, arithmetic and copies ran while one was open for 6% -> 6% of each run, Pallas kernels for 22% -> 22%
where the time goes in v6:
time: 129 us; the launch traced here: 127 us
  blocking collectives  48.9 us (38%)
  Pallas kernels  30.9 us (24%)
  starting transfers between devices  30.4 us (24%)
  waiting for transfers between devices  6.85 us (5%)
  matrix products  5.43 us (4%)
  other arithmetic  3.6 us (3%)
    all_gather x7, blocking collectives, gather_col(): return lax.all_gather(block, 'col', axis=1, tiled=True)  48.9 us
    pallas_call x1, Pallas kernels, on_device(): pl.pallas_call(functools.partial(prefix_kernel, (rows, window, tiles, fir...  27.8 us
    ppermute x3, starting transfers between devices, on_device(): lax.ppermute(lead, 'row', moves_to([(place, home)]))  9.5 us
    dot_general x10, matrix products, dot(): jnp.dot(left, right, precision=lax.Precision.HIGH, preferred_element_type...  5.43 us
    ppermute x6, starting transfers between devices, hand_out(): result = result + lax.ppermute(parts[:, piece], 'row', pairs)  5.23 us
    ppermute x5, starting transfers between devices, among(): lax.ppermute(payload, 'row', [(base_row + a, base_row + b) for a, b in pa...  3.63 us
    ppermute x1, waiting for transfers between devices, on_device(): arrived = lax.ppermute(sends[0], 'row', swap_pairs(rows, 1))  3.5 us
    ppermute x6, waiting for transfers between devices, hand_out(): result = result + lax.ppermute(parts[:, piece], 'row', pairs)  3.32 us
  transfers between devices with their start and end apart: 21, of which 3 were waited for; matrix products, arithmetic and copies ran while one was open for 6% of the time, Pallas kernels for 22%

profile of v6, /device:TPU:0, one launch (start us, length us, event | category | flops | bytes accessed | tf_op | source)
XLA Modules:
  0.0 126.6 jit_solution(15936539676681823844)
XLA Ops:
  0.0 3.2 %shard_map.38 = (f32[1024,256]{1,0:T(8,128)S(1)}, f32[1024,256]{1,0:T(8,128)S(1)}, f32[1024,256]{1,0:T(8,128)S(1)}) custom-call(f32[98304,128]{1,0:T(8,128)} %bitcast.100), custom_call_target="tpu_custom_call" | custom-call | tf_op jit(solution)/shard_map/pallas_call | solution.py:142
  3.2 0.7 collective-permute-start
  3.9 0.7 collective-permute-start.1
  4.6 27.8 %shard_map.37 = (f32[1,4,32,256]{3,2,1,0:T(8,128)S(1)}, f32[1,4,32,256]{3,2,1,0:T(8,128)S(1)}, f32[2,4,32,256]{3,2,1,0:T(8,128)S(1)}, f32[1,4,32,256]{3,2,1,0:T(...) custom-call(f32[12288,256]{1,0:T(8,128)} %bitcast.109, f32[12288,8,1,128]{3,2,1,0:T(1,128)} %bitcast.101, ...), custom_call_target="tpu_custom_call" | custom-call | flops 19327352832 | bytes 62914560 | tf_op jit(solution)/shard_map/pallas_call | solution.py:163
  32.4 0.0 collective-permute-done
  32.4 3.0 %collective-permute-start.2 = (f32[1,4,32,256]{3,2,1,0:T(8,128)S(1)}, f32[1,4,32,256]{3,2,1,0:T(8,128)S(1)}, u32[]{:S(2)}, u32[]{:S(2)}) collective-permute-start(f32[1,4,32,256]{3,2,1,0:T(8,128)S(1)} %get-tuple-element.30), channel_id=1, source_target_pairs={{0,4},{4,0},{8,12},{12,8},{16,20},{20,16},{24,28},{28,24},{1,5},{5... | collective-permute-start | bytes 393224 | tf_op jit(solution)/shard_map/reduce0/ppermute | solution.py:194
  35.5 3.5 %collective-permute-done.2 = f32[1,4,32,256]{3,2,1,0:T(8,128)S(1)} collective-permute-done((f32[1,4,32,256]{3,2,1,0:T(8,128)S(1)}, f32[1,4,32,256]{3,2,1,0:T(8,128)S(1)}, u32[]{:S(2)}, u32[]{:S(2)}) %collective-permute-start.2) | collective-permute-done | bytes 131104 | tf_op jit(solution)/shard_map/reduce0/ppermute | solution.py:194
  39.0 1.7 %collective-permute-start.9 = (f32[1,4,32,256]{3,2,1,0:T(8,128)}, f32[1,4,32,256]{3,2,1,0:T(8,128)}, u32[]{:S(2)}, u32[]{:S(2)}) collective-permute-start(f32[1,4,32,256]{3,2,1,0:T(8,128)} %get-tuple-element.37), channel_id=1, source_target_pairs={{0,4},{4,0},{8,12},{12,8},{16,20},{20,16},{24,28},{28,24},{1,5},{5... | collective-permute-start | bytes 393224 | tf_op jit(solution)/shard_map/reduce1/ppermute | solution.py:201
  40.7 0.7 add.54
  41.4 6.9 %collective-permute-start.4 = (f32[1,4,32,256]{3,2,1,0:T(8,128)}, f32[1,4,32,256]{3,2,1,0:T(8,128)}, u32[]{:S(2)}, u32[]{:S(2)}) collective-permute-start(f32[1,4,32,256]{3,2,1,0:T(8,128)} %add.54), channel_id=1, source_target_pairs={{0,16},{4,20},{1,17},{5,21},{2,18},{6,22},{3,19},{7,23}} | collective-permute-start | bytes 393224 | tf_op jit(solution)/shard_map/reduce0/ppermute | solution.py:197
  48.3 1.3 %collective-permute-start.5 = (f32[1,4,32,256]{3,2,1,0:T(8,128)}, f32[1,4,32,256]{3,2,1,0:T(8,128)}, u32[]{:S(2)}, u32[]{:S(2)}) collective-permute-start(f32[1,4,32,256]{3,2,1,0:T(8,128)} %add.54), channel_id=1, source_target_pairs={{8,16},{12,20},{9,17},{13,21},{10,18},{14,22},{11,19},{15,23}} | collective-permute-start | bytes 393224 | tf_op jit(solution)/shard_map/reduce0/ppermute | solution.py:197
  49.6 1.3 %collective-permute-start.6 = (f32[1,4,32,256]{3,2,1,0:T(8,128)}, f32[1,4,32,256]{3,2,1,0:T(8,128)}, u32[]{:S(2)}, u32[]{:S(2)}) collective-permute-start(f32[1,4,32,256]{3,2,1,0:T(8,128)} %add.54), channel_id=1, source_target_pairs={{24,16},{28,20},{25,17},{29,21},{26,18},{30,22},{27,19},{31,23}} | collective-permute-start | bytes 393224 | tf_op jit(solution)/shard_map/reduce0/ppermute | solution.py:197
  50.9 1.7 %collective-permute-start.3 = (f32[2,4,32,256]{3,2,1,0:T(8,128)}, f32[2,4,32,256]{3,2,1,0:T(8,128)S(1)}, u32[]{:S(2)}, u32[]{:S(2)}) collective-permute-start(f32[2,4,32,256]{3,2,1,0:T(8,128)} %copy-done), channel_id=1, source_target_pairs={{0,4},{4,0},{8,12},{12,8},{16,20},{20,16},{24,28},{28,24},{1,5},{5... | collective-permute-start | bytes 786440 | tf_op jit(solution)/shard_map/reduce2/ppermute | solution.py:205
  52.6 0.7 collective-permute-start.12
  53.4 0.9 add.60
  54.3 0.7 collective-permute-start.14
  55.0 2.5 %collective-permute-start.10 = (f32[1,4,32,256]{3,2,1,0:T(8,128)S(1)}, f32[1,4,32,256]{3,2,1,0:T(8,128)S(1)}, u32[]{:S(2)}, u32[]{:S(2)}) collective-permute-start(f32[1,4,32,256]{3,2,1,0:T(8,128)S(1)} %add.60), channel_id=1, source_target_pairs={{0,8},{4,12},{24,16},{28,20},{1,9},{5,13},{25,17},{29,21},{2,10},{... | collective-permute-start | bytes 393224 | tf_op jit(solution)/shard_map/reduce1/ppermute | solution.py:203
  57.5 1.1 add_add_fusion
  58.7 7.2 %all_gather.21 = f32[128,1024]{1,0:T(8,128)S(1)} all-gather(f32[128,256]{1,0:T(8,128)S(1)} %bitcast.115), channel_id=1, replica_groups=mesh['row'=8,'col'=4] {'col'}, dimensions={1}, use_global_device_ids=true | all-gather | bytes 655360 | tf_op jit(solution)/shard_map/solve0/all_gather | solution.py:120
  65.9 1.7 %collective-permute-start.7 = (f32[2,4,32,256]{3,2,1,0:T(8,128)S(1)}, f32[2,4,32,256]{3,2,1,0:T(8,128)S(1)}, u32[]{:S(2)}, u32[]{:S(2)}) collective-permute-start(f32[2,4,32,256]{3,2,1,0:T(8,128)S(1)} %add.53), channel_id=1, source_target_pairs={{0,8},{4,12},{24,16},{28,20},{1,9},{5,13},{25,17},{29,21},{2,10},{... | collective-permute-start | bytes 786440 | tf_op jit(solution)/shard_map/reduce2/ppermute | solution.py:206
  67.6 1.6 %fusion.5 = f32[128,256]{1,0:T(8,128)S(1)} fusion(f32[128,1024]{1,0:T(8,128)S(1)} %all_gather.21, f32[4,1024,256]{2,1,0:T(8,128)} %param.5), kind=kOutput, calls=%fused_computation.6 | convolution fusion | flops 201326592 | bytes 1703936 | tf_op jit(solution)/shard_map/solve0/dot_general | solution.py:93
  69.3 0.7 collective-permute-start.11
  69.9 7.2 %all_gather.22 = f32[128,1024]{1,0:T(8,128)S(1)} all-gather(f32[128,256]{1,0:T(8,128)S(1)} %fusion.5), channel_id=1, replica_groups=mesh['row'=8,'col'=4] {'col'}, dimensions={1}, use_global_device_ids=true | all-gather | bytes 655360 | tf_op jit(solution)/shard_map/solve0/all_gather | solution.py:120
  77.2 0.7 collective-permute-start.8
  77.9 0.4 bitcast_subtract_fusion.1
  78.3 7.3 %all_gather.23 = f32[128,1024]{1,0:T(8,128)S(1)} all-gather(f32[128,256]{1,0:T(8,128)S(1)} %bitcast_subtract_fusion.1), channel_id=1, replica_groups=mesh['row'=8,'col'=4] {'col'}, dimensions={1}, use_global_device_ids=true | all-gather | bytes 655360 | tf_op jit(solution)/shard_map/solve1/all_gather | solution.py:120
  85.6 0.4 fusion.3
  86.0 0.7 collective-permute-start.13
  86.8 7.3 %all_gather.24 = f32[128,1024]{1,0:T(8,128)S(1)} all-gather(f32[128,256]{1,0:T(8,128)S(1)} %fusion.3), channel_id=1, replica_groups=mesh['row'=8,'col'=4] {'col'}, dimensions={1}, use_global_device_ids=true | all-gather | bytes 655360 | tf_op jit(solution)/shard_map/solve1/all_gather | solution.py:120
  94.1 0.4 fusion.15
  94.6 0.4 fusion.30
  95.0 7.3 %all_gather.25 = f32[128,1024]{1,0:T(8,128)S(1)} all-gather(f32[128,256]{1,0:T(8,128)S(1)} %fusion.30), channel_id=1, replica_groups=mesh['row'=8,'col'=4] {'col'}, dimensions={1}, use_global_device_ids=true | all-gather | bytes 655360 | tf_op jit(solution)/shard_map/solve2/all_gather | solution.py:120
  102.3 0.4 fusion.1
  102.8 7.3 %all_gather.26 = f32[128,1024]{1,0:T(8,128)S(1)} all-gather(f32[128,256]{1,0:T(8,128)S(1)} %fusion.1), channel_id=1, replica_groups=mesh['row'=8,'col'=4] {'col'}, dimensions={1}, use_global_device_ids=true | all-gather | bytes 655360 | tf_op jit(solution)/shard_map/solve2/all_gather | solution.py:120
  110.1 0.4 fusion.17
  110.5 0.4 fusion.10
  111.0 0.4 fusion.32
  111.5 1.3 %collective-permute-start.18 = (f32[1,32,256]{2,1,0:T(8,128)S(1)}, f32[1,32,256]{2,1,0:T(8,128)S(1)}, u32[]{:S(2)}, u32[]{:S(2)}) collective-permute-start(f32[1,32,256]{2,1,0:T(8,128)S(1)} %get-tuple-element.52), channel_id=1, source_target_pairs={{16,0},{20,4},{17,1},{21,5},{18,2},{22,6},{19,3},{23,7}} | collective-permute-start | bytes 98312 | tf_op jit(solution)/shard_map/out_last/ppermute | solution.py:227
  112.8 0.7 collective-permute-start.19
  113.4 0.7 collective-permute-start.20
  114.1 1.3 %collective-permute-start.15 = (f32[3,32,256]{2,1,0:T(8,128)S(1)}, f32[3,32,256]{2,1,0:T(8,128)S(1)}, u32[]{:S(2)}, u32[]{:S(2)}) collective-permute-start(f32[3,32,256]{2,1,0:T(8,128)S(1)} %get-tuple-element.47), channel_id=1, source_target_pairs={{16,0},{20,4},{17,1},{21,5},{18,2},{22,6},{19,3},{23,7}} | collective-permute-start | bytes 294920 | tf_op jit(solution)/shard_map/out/ppermute | solution.py:227
  115.4 0.7 collective-permute-start.16
  116.1 2.1 %collective-permute-done.18 = f32[1,32,256]{2,1,0:T(8,128)S(1)} collective-permute-done((f32[1,32,256]{2,1,0:T(8,128)S(1)}, f32[1,32,256]{2,1,0:T(8,128)S(1)}, u32[]{:S(2)}, u32[]{:S(2)}) %collective-permute-start.18) | collective-permute-done | bytes 32800 | tf_op jit(solution)/shard_map/out_last/ppermute | solution.py:227
  118.2 0.7 collective-permute-start.17
  118.9 5.4 %all-gather = f32[1,32,1024]{2,1,0:T(8,128)S(1)} all-gather(f32[1,32,256]{2,1,0:T(8,128)S(1)} %fusion.41), channel_id=2, replica_groups=mesh['row'=8,'col'=4] {'col'}, dimensions={2}, use_global_device_ids=true | all-gather | bytes 163840 | tf_op jit(solution)/shard_map/out_last/all_gather | solution.py:120
  124.3 0.4 convolution_bitcast_fusion
  124.7 1.2 collective-permute-done.15
  126.0 0.7 maximum_bitcast_fusion
  (40 shorter events, 0.3 us)
Async XLA Ops:
  3.2 29.2 %collective-permute-start = (f32[1024,256]{1,0:T(8,128)S(1)}, f32[1024,256]{1,0:T(8,128)S(1)}, u32[]{:S(2)}, u32[]{:S(2)}) collective-permute-start(f32[1024,256]{1,0:T(8,128)S(1)} %get-tuple-element.29), channel_id=1, source_target_pairs={{16,20},{20,16},{24,28},{17,21},{21,17},{25,29},{18,22},{22,18},{2... | collective-permute-start | bytes 3145736 | tf_op jit(solution)/shard_map/near1/ppermute | solution.py:152
  3.9 28.5 %collective-permute-start.1 = (f32[1024,256]{1,0:T(8,128)S(1)}, f32[1024,256]{1,0:T(8,128)S(1)}, u32[]{:S(2)}, u32[]{:S(2)}) collective-permute-start(f32[1024,256]{1,0:T(8,128)S(1)} %get-tuple-element.29), channel_id=1, source_target_pairs={{24,16},{25,17},{26,18},{27,19}} | collective-permute-start | bytes 3145736 | tf_op jit(solution)/shard_map/far/ppermute | solution.py:152
  32.4 9.0 %copy-start = (f32[2,4,32,256]{3,2,1,0:T(8,128)}, f32[2,4,32,256]{3,2,1,0:T(8,128)S(1)}, u32[]{:S(2)}) copy-start(f32[2,4,32,256]{3,2,1,0:T(8,128)S(1)} %get-tuple-element.33) | copy-start | bytes 786436
  32.4 15.9 %copy-start.1 = (f32[1024,256]{1,0:T(8,128)}, f32[1024,256]{1,0:T(8,128)S(1)}, u32[]{:S(2)}) copy-start(f32[1024,256]{1,0:T(8,128)S(1)} %collective-permute-done) | copy-start | bytes 3145732
  32.4 17.1 %copy-start.4 = (f32[1024,256]{1,0:T(8,128)}, f32[1024,256]{1,0:T(8,128)S(1)}, u32[]{:S(2)}) copy-start(f32[1024,256]{1,0:T(8,128)S(1)} %collective-permute-done.1) | copy-start | bytes 3145732
  32.4 6.5 %collective-permute-start.2 = (f32[1,4,32,256]{3,2,1,0:T(8,128)S(1)}, f32[1,4,32,256]{3,2,1,0:T(8,128)S(1)}, u32[]{:S(2)}, u32[]{:S(2)}) collective-permute-start(f32[1,4,32,256]{3,2,1,0:T(8,128)S(1)} %get-tuple-element.30), channel_id=1, source_target_pairs={{0,4},{4,0},{8,12},{12,8},{16,20},{20,16},{24,28},{28,24},{1,5},{5... | collective-permute-start | bytes 393224 | tf_op jit(solution)/shard_map/reduce0/ppermute | solution.py:194
  39.0 13.7 %collective-permute-start.9 = (f32[1,4,32,256]{3,2,1,0:T(8,128)}, f32[1,4,32,256]{3,2,1,0:T(8,128)}, u32[]{:S(2)}, u32[]{:S(2)}) collective-permute-start(f32[1,4,32,256]{3,2,1,0:T(8,128)} %get-tuple-element.37), channel_id=1, source_target_pairs={{0,4},{4,0},{8,12},{12,8},{16,20},{20,16},{24,28},{28,24},{1,5},{5... | collective-permute-start | bytes 393224 | tf_op jit(solution)/shard_map/reduce1/ppermute | solution.py:201
  41.4 12.9 %collective-permute-start.4 = (f32[1,4,32,256]{3,2,1,0:T(8,128)}, f32[1,4,32,256]{3,2,1,0:T(8,128)}, u32[]{:S(2)}, u32[]{:S(2)}) collective-permute-start(f32[1,4,32,256]{3,2,1,0:T(8,128)} %add.54), channel_id=1, source_target_pairs={{0,16},{4,20},{1,17},{5,21},{2,18},{6,22},{3,19},{7,23}} | collective-permute-start | bytes 393224 | tf_op jit(solution)/shard_map/reduce0/ppermute | solution.py:197
  48.3 6.8 %collective-permute-start.5 = (f32[1,4,32,256]{3,2,1,0:T(8,128)}, f32[1,4,32,256]{3,2,1,0:T(8,128)}, u32[]{:S(2)}, u32[]{:S(2)}) collective-permute-start(f32[1,4,32,256]{3,2,1,0:T(8,128)} %add.54), channel_id=1, source_target_pairs={{8,16},{12,20},{9,17},{13,21},{10,18},{14,22},{11,19},{15,23}} | collective-permute-start | bytes 393224 | tf_op jit(solution)/shard_map/reduce0/ppermute | solution.py:197
  49.6 8.0 %collective-permute-start.6 = (f32[1,4,32,256]{3,2,1,0:T(8,128)}, f32[1,4,32,256]{3,2,1,0:T(8,128)}, u32[]{:S(2)}, u32[]{:S(2)}) collective-permute-start(f32[1,4,32,256]{3,2,1,0:T(8,128)} %add.54), channel_id=1, source_target_pairs={{24,16},{28,20},{25,17},{29,21},{26,18},{30,22},{27,19},{31,23}} | collective-permute-start | bytes 393224 | tf_op jit(solution)/shard_map/reduce0/ppermute | solution.py:197
  50.9 27.0 %copy-start.2 = (f32[1024,256]{1,0:T(8,128)S(1)}, f32[1024,256]{1,0:T(8,128)}, u32[]{:S(2)}) copy-start(f32[1024,256]{1,0:T(8,128)} %copy-done.1) | copy-start | bytes 3145732
  50.9 15.0 %collective-permute-start.3 = (f32[2,4,32,256]{3,2,1,0:T(8,128)}, f32[2,4,32,256]{3,2,1,0:T(8,128)S(1)}, u32[]{:S(2)}, u32[]{:S(2)}) collective-permute-start(f32[2,4,32,256]{3,2,1,0:T(8,128)} %copy-done), channel_id=1, source_target_pairs={{0,4},{4,0},{8,12},{12,8},{16,20},{20,16},{24,28},{28,24},{1,5},{5... | collective-permute-start | bytes 786440 | tf_op jit(solution)/shard_map/reduce2/ppermute | solution.py:205
  52.6 41.5 %collective-permute-start.12 = (f32[1024,256]{1,0:T(8,128)S(1)}, f32[1024,256]{1,0:T(8,128)S(1)}, u32[]{:S(2)}, u32[]{:S(2)}) collective-permute-start(f32[1024,256]{1,0:T(8,128)S(1)} %get-tuple-element.42), channel_id=1, source_target_pairs={{16,20},{20,16},{17,21},{21,17},{18,22},{22,18},{19,23},{23,19}} | collective-permute-start | bytes 3145736 | tf_op jit(solution)/shard_map/near2/ppermute | solution.py:152
  54.3 56.7 %collective-permute-start.14 = (f32[1024,256]{1,0:T(8,128)S(1)}, f32[1024,256]{1,0:T(8,128)S(1)}, u32[]{:S(2)}, u32[]{:S(2)}) collective-permute-start(f32[1024,256]{1,0:T(8,128)S(1)} %get-tuple-element.45), channel_id=1, source_target_pairs={{16,20},{17,21},{18,22},{19,23}} | collective-permute-start | bytes 3145736 | tf_op jit(solution)/shard_map/near3/ppermute | solution.py:152
  55.0 14.2 %collective-permute-start.10 = (f32[1,4,32,256]{3,2,1,0:T(8,128)S(1)}, f32[1,4,32,256]{3,2,1,0:T(8,128)S(1)}, u32[]{:S(2)}, u32[]{:S(2)}) collective-permute-start(f32[1,4,32,256]{3,2,1,0:T(8,128)S(1)} %add.60), channel_id=1, source_target_pairs={{0,8},{4,12},{24,16},{28,20},{1,9},{5,13},{25,17},{29,21},{2,10},{... | collective-permute-start | bytes 393224 | tf_op jit(solution)/shard_map/reduce1/ppermute | solution.py:203
  65.8 19.8 %copy-start.3 = (f32[4,1024,256]{2,1,0:T(8,128)S(1)}, f32[4,1024,256]{2,1,0:T(8,128)}, u32[]{:S(2)}) copy-start(f32[4,1024,256]{2,1,0:T(8,128)} %param.5) | copy-start | bytes 12582916
  65.9 11.3 %collective-permute-start.7 = (f32[2,4,32,256]{3,2,1,0:T(8,128)S(1)}, f32[2,4,32,256]{3,2,1,0:T(8,128)S(1)}, u32[]{:S(2)}, u32[]{:S(2)}) collective-permute-start(f32[2,4,32,256]{3,2,1,0:T(8,128)S(1)} %add.53), channel_id=1, source_target_pairs={{0,8},{4,12},{24,16},{28,20},{1,9},{5,13},{25,17},{29,21},{2,10},{... | collective-permute-start | bytes 786440 | tf_op jit(solution)/shard_map/reduce2/ppermute | solution.py:206
  69.3 7.8 %collective-permute-start.11 = (f32[1,4,32,256]{3,2,1,0:T(8,128)S(1)}, f32[1,4,32,256]{3,2,1,0:T(8,128)S(1)}, u32[]{:S(2)}, u32[]{:S(2)}) collective-permute-start(f32[1,4,32,256]{3,2,1,0:T(8,128)S(1)} %add.61), channel_id=1, source_target_pairs={{8,16},{12,20},{9,17},{13,21},{10,18},{14,22},{11,19},{15,23}} | collective-permute-start | bytes 393224 | tf_op jit(solution)/shard_map/reduce1/ppermute | solution.py:203
  77.2 16.9 %collective-permute-start.8 = (f32[2,4,32,256]{3,2,1,0:T(8,128)S(1)}, f32[2,4,32,256]{3,2,1,0:T(8,128)S(1)}, u32[]{:S(2)}, u32[]{:S(2)}) collective-permute-start(f32[2,4,32,256]{3,2,1,0:T(8,128)S(1)} %add.58), channel_id=1, source_target_pairs={{8,16},{12,20},{9,17},{13,21},{10,18},{14,22},{11,19},{15,23}} | collective-permute-start | bytes 786440 | tf_op jit(solution)/shard_map/reduce2/ppermute | solution.py:243
  86.0 24.5 %collective-permute-start.13 = (f32[1024,256]{1,0:T(8,128)S(1)}, f32[1024,256]{1,0:T(8,128)S(1)}, u32[]{:S(2)}, u32[]{:S(2)}) collective-permute-start(f32[1024,256]{1,0:T(8,128)S(1)} %copy-done.2), channel_id=1, source_target_pairs={{28,20},{29,21},{30,22},{31,23}} | collective-permute-start | bytes 3145736 | tf_op jit(solution)/shard_map/across/ppermute | solution.py:152
  94.6 15.9 %copy-start.5 = (f32[1024,256]{1,0:T(8,128)S(1)}, f32[1024,256]{1,0:T(8,128)}, u32[]{:S(2)}) copy-start(f32[1024,256]{1,0:T(8,128)} %copy-done.4) | copy-start | bytes 3145732
  111.5 6.7 %collective-permute-start.18 = (f32[1,32,256]{2,1,0:T(8,128)S(1)}, f32[1,32,256]{2,1,0:T(8,128)S(1)}, u32[]{:S(2)}, u32[]{:S(2)}) collective-permute-start(f32[1,32,256]{2,1,0:T(8,128)S(1)} %get-tuple-element.52), channel_id=1, source_target_pairs={{16,0},{20,4},{17,1},{21,5},{18,2},{22,6},{19,3},{23,7}} | collective-permute-start | bytes 98312 | tf_op jit(solution)/shard_map/out_last/ppermute | solution.py:227
  112.8 6.1 %collective-permute-start.19 = (f32[1,32,256]{2,1,0:T(8,128)S(1)}, f32[1,32,256]{2,1,0:T(8,128)S(1)}, u32[]{:S(2)}, u32[]{:S(2)}) collective-permute-start(f32[1,32,256]{2,1,0:T(8,128)S(1)} %get-tuple-element.54), channel_id=1, source_target_pairs={{16,8},{20,12},{17,9},{21,13},{18,10},{22,14},{19,11},{23,15}} | collective-permute-start | bytes 98312 | tf_op jit(solution)/shard_map/out_last/ppermute | solution.py:227
  113.4 5.4 %collective-permute-start.20 = (f32[1,32,256]{2,1,0:T(8,128)S(1)}, f32[1,32,256]{2,1,0:T(8,128)S(1)}, u32[]{:S(2)}, u32[]{:S(2)}) collective-permute-start(f32[1,32,256]{2,1,0:T(8,128)S(1)} %get-tuple-element.53), channel_id=1, source_target_pairs={{16,24},{20,28},{17,25},{21,29},{18,26},{22,30},{19,27},{23,31}} | collective-permute-start | bytes 98312 | tf_op jit(solution)/shard_map/out_last/ppermute | solution.py:227
  114.1 11.8 %collective-permute-start.15 = (f32[3,32,256]{2,1,0:T(8,128)S(1)}, f32[3,32,256]{2,1,0:T(8,128)S(1)}, u32[]{:S(2)}, u32[]{:S(2)}) collective-permute-start(f32[3,32,256]{2,1,0:T(8,128)S(1)} %get-tuple-element.47), channel_id=1, source_target_pairs={{16,0},{20,4},{17,1},{21,5},{18,2},{22,6},{19,3},{23,7}} | collective-permute-start | bytes 294920 | tf_op jit(solution)/shard_map/out/ppermute | solution.py:227
  115.4 10.5 %collective-permute-start.16 = (f32[3,32,256]{2,1,0:T(8,128)S(1)}, f32[3,32,256]{2,1,0:T(8,128)S(1)}, u32[]{:S(2)}, u32[]{:S(2)}) collective-permute-start(f32[3,32,256]{2,1,0:T(8,128)S(1)} %get-tuple-element.48), channel_id=1, source_target_pairs={{16,8},{20,12},{17,9},{21,13},{18,10},{22,14},{19,11},{23,15}} | collective-permute-start | bytes 294920 | tf_op jit(solution)/shard_map/out/ppermute | solution.py:227
  118.2 7.8 %collective-permute-start.17 = (f32[3,32,256]{2,1,0:T(8,128)S(1)}, f32[3,32,256]{2,1,0:T(8,128)S(1)}, u32[]{:S(2)}, u32[]{:S(2)}) collective-permute-start(f32[3,32,256]{2,1,0:T(8,128)S(1)} %get-tuple-element.49), channel_id=1, source_target_pairs={{16,24},{20,28},{17,25},{21,29},{18,26},{22,30},{19,27},{23,31}} | collective-permute-start | bytes 294920 | tf_op jit(solution)/shard_map/out/ppermute | solution.py:227

commit v7 on v6

--- a/solution.py
+++ b/solution.py
@@ -218,15 +218,6 @@
             return jnp.where(leader, mine, other) if i == 0 else jnp.where(leader, other, mine)
         return jnp.where(leader, far, across)
 
-    def hand_out(values):
-        parts = values.reshape(-1, pieces, part, width)
-        result = jnp.where(row // 2 == home, parts[:, home], 0.0)
-        for piece in sorted(range(pieces), key=lambda place: -abs(place - home)):
-            if piece != home:
-                pairs = [(base_row + k, 2 * piece + k) for k in (0, 1)]
-                result = result + lax.ppermute(parts[:, piece], "row", pairs)
-        return result
-
     solved = []
     for j in range(window - 1):
         with jax.named_scope(f"solve{j}"):
@@ -250,12 +241,21 @@
         if j == 2:
             with jax.named_scope("corner"):
                 residual[window - 1] = residual[window - 1] - dot(corner, between(0, window - 1))
-    with jax.named_scope("out_last"):
-        own = hand_out(residual[-1])[0]
-        own_solved = dot(gather_col(own), inverse[window - 1])
     with jax.named_scope("out"):
-        rest = hand_out(*wait(residual[-1], (jnp.stack(solved),)))
-        result = jnp.concatenate([rest, own_solved[None]])
+        last = residual[-1].reshape(pieces, part, width)
+        rest = wait(residual[-1], (jnp.stack(solved),))[0].reshape(-1, pieces, part, width)
+        own_last = jnp.where(row // 2 == home, last[home], 0.0)
+        own_rest = jnp.where(row // 2 == home, rest[:, home], 0.0)
+        for place in range(pieces):
+            pairs = [(base_row + k, 2 * place + k) for k in (0, 1)]
+            if place < home:
+                own_last = own_last + lax.ppermute(last[place], "row", pairs)
+                own_rest = own_rest + lax.ppermute(rest[:, place], "row", pairs)
+            elif place > home:
+                moved = lax.ppermute(jnp.concatenate([rest[:, place], last[place][None]]), "row", pairs)
+                own_rest, own_last = own_rest + moved[:-1], own_last + moved[-1]
+        own_solved = dot(gather_col(own_last), inverse[window - 1])
+        result = jnp.concatenate([own_rest, own_solved[None]])
     return result.transpose(0, 2, 1)
 
 

time: 129 us -> 130 us (level); the launches traced: 127 us -> 129 us
  waiting for transfers between devices: 6.85 us -> 8.72 us
    ppermute x6 -> x5, waiting for transfers between devices: 3.32 us -> 5.18 us  [the longest x2 5.17 us: on_device(): own_last = own_last + lax.ppermute(last[place], 'row', pairs)]
    ppermute x6 -> x5, starting transfers between devices: 5.23 us -> 4.58 us  [the longest x2 1.96 us: on_device(): own_rest = own_rest + lax.ppermute(rest[:, place], 'row', pairs)]
  transfers between devices with their start and end apart: 21 -> 20, of which waited for: 3 -> 2; matrix products, arithmetic and copies ran while one was open for 6% -> 7% of each run, Pallas kernels for 22% -> 22%
where the time goes in v7:
time: 130 us; the launch traced here: 129 us
  blocking collectives  48.9 us (38%)
  Pallas kernels  30.9 us (24%)
  starting transfers between devices  29.8 us (23%)
  waiting for transfers between devices  8.72 us (7%)
  matrix products  6.65 us (5%)
  other arithmetic  3.61 us (3%)
    all_gather x7, blocking collectives, gather_col(): return lax.all_gather(block, 'col', axis=1, tiled=True)  48.9 us
    pallas_call x1, Pallas kernels, on_device(): pl.pallas_call(functools.partial(prefix_kernel, (rows, window, tiles, fir...  27.8 us
    ppermute x3, starting transfers between devices, on_device(): lax.ppermute(lead, 'row', moves_to([(place, home)]))  9.52 us
    dot_general x10, matrix products, dot(): jnp.dot(left, right, precision=lax.Precision.HIGH, preferred_element_type...  6.65 us
    ppermute x2, waiting for transfers between devices, on_device(): own_last = own_last + lax.ppermute(last[place], 'row', pairs)  5.17 us
    ppermute x5, starting transfers between devices, among(): lax.ppermute(payload, 'row', [(base_row + a, base_row + b) for a, b in pa...  3.63 us
    ppermute x1, waiting for transfers between devices, on_device(): arrived = lax.ppermute(sends[0], 'row', swap_pairs(rows, 1))  3.5 us
    pallas_call x1, Pallas kernels, on_device(): pl.pallas_call(functools.partial(window_kernel, window, tiles), grid=(cut...  3.16 us
  transfers between devices with their start and end apart: 20, of which 2 were waited for; matrix products, arithmetic and copies ran while one was open for 7% of the time, Pallas kernels for 22%

profile of v7, /device:TPU:0, one launch (start us, length us, event | category | flops | bytes accessed | tf_op | source)
XLA Modules:
  0.0 129.1 jit_solution(2685669563973246281)
XLA Ops:
  0.0 3.2 %shard_map.38 = (f32[1024,256]{1,0:T(8,128)S(1)}, f32[1024,256]{1,0:T(8,128)S(1)}, f32[1024,256]{1,0:T(8,128)S(1)}) custom-call(f32[98304,128]{1,0:T(8,128)} %bitcast.89), custom_call_target="tpu_custom_call" | custom-call | tf_op jit(solution)/shard_map/pallas_call | solution.py:142
  3.2 0.7 collective-permute-start
  3.9 0.7 collective-permute-start.1
  4.6 27.8 %shard_map.37 = (f32[1,4,32,256]{3,2,1,0:T(8,128)S(1)}, f32[1,4,32,256]{3,2,1,0:T(8,128)S(1)}, f32[2,4,32,256]{3,2,1,0:T(8,128)S(1)}, f32[1,4,32,256]{3,2,1,0:T(...) custom-call(f32[12288,256]{1,0:T(8,128)} %bitcast.98, f32[12288,8,1,128]{3,2,1,0:T(1,128)} %bitcast.90, ...), custom_call_target="tpu_custom_call" | custom-call | flops 19327352832 | bytes 62914560 | tf_op jit(solution)/shard_map/pallas_call | solution.py:163
  32.4 0.0 collective-permute-done.1
  32.4 3.0 %collective-permute-start.2 = (f32[1,4,32,256]{3,2,1,0:T(8,128)S(1)}, f32[1,4,32,256]{3,2,1,0:T(8,128)S(1)}, u32[]{:S(2)}, u32[]{:S(2)}) collective-permute-start(f32[1,4,32,256]{3,2,1,0:T(8,128)S(1)} %get-tuple-element.30), channel_id=1, source_target_pairs={{0,4},{4,0},{8,12},{12,8},{16,20},{20,16},{24,28},{28,24},{1,5},{5... | collective-permute-start | bytes 393224 | tf_op jit(solution)/shard_map/reduce0/ppermute | solution.py:194
  35.5 3.5 %collective-permute-done.2 = f32[1,4,32,256]{3,2,1,0:T(8,128)S(1)} collective-permute-done((f32[1,4,32,256]{3,2,1,0:T(8,128)S(1)}, f32[1,4,32,256]{3,2,1,0:T(8,128)S(1)}, u32[]{:S(2)}, u32[]{:S(2)}) %collective-permute-start.2) | collective-permute-done | bytes 131104 | tf_op jit(solution)/shard_map/reduce0/ppermute | solution.py:194
  39.0 1.7 %collective-permute-start.9 = (f32[1,4,32,256]{3,2,1,0:T(8,128)}, f32[1,4,32,256]{3,2,1,0:T(8,128)}, u32[]{:S(2)}, u32[]{:S(2)}) collective-permute-start(f32[1,4,32,256]{3,2,1,0:T(8,128)} %get-tuple-element.37), channel_id=1, source_target_pairs={{0,4},{4,0},{8,12},{12,8},{16,20},{20,16},{24,28},{28,24},{1,5},{5... | collective-permute-start | bytes 393224 | tf_op jit(solution)/shard_map/reduce1/ppermute | solution.py:201
  40.7 0.7 add.54
  41.4 6.9 %collective-permute-start.4 = (f32[1,4,32,256]{3,2,1,0:T(8,128)}, f32[1,4,32,256]{3,2,1,0:T(8,128)}, u32[]{:S(2)}, u32[]{:S(2)}) collective-permute-start(f32[1,4,32,256]{3,2,1,0:T(8,128)} %add.54), channel_id=1, source_target_pairs={{0,16},{4,20},{1,17},{5,21},{2,18},{6,22},{3,19},{7,23}} | collective-permute-start | bytes 393224 | tf_op jit(solution)/shard_map/reduce0/ppermute | solution.py:197
  48.3 1.3 %collective-permute-start.5 = (f32[1,4,32,256]{3,2,1,0:T(8,128)}, f32[1,4,32,256]{3,2,1,0:T(8,128)}, u32[]{:S(2)}, u32[]{:S(2)}) collective-permute-start(f32[1,4,32,256]{3,2,1,0:T(8,128)} %add.54), channel_id=1, source_target_pairs={{8,16},{12,20},{9,17},{13,21},{10,18},{14,22},{11,19},{15,23}} | collective-permute-start | bytes 393224 | tf_op jit(solution)/shard_map/reduce0/ppermute | solution.py:197
  49.6 1.3 %collective-permute-start.6 = (f32[1,4,32,256]{3,2,1,0:T(8,128)}, f32[1,4,32,256]{3,2,1,0:T(8,128)}, u32[]{:S(2)}, u32[]{:S(2)}) collective-permute-start(f32[1,4,32,256]{3,2,1,0:T(8,128)} %add.54), channel_id=1, source_target_pairs={{24,16},{28,20},{25,17},{29,21},{26,18},{30,22},{27,19},{31,23}} | collective-permute-start | bytes 393224 | tf_op jit(solution)/shard_map/reduce0/ppermute | solution.py:197
  50.9 1.7 %collective-permute-start.3 = (f32[2,4,32,256]{3,2,1,0:T(8,128)}, f32[2,4,32,256]{3,2,1,0:T(8,128)S(1)}, u32[]{:S(2)}, u32[]{:S(2)}) collective-permute-start(f32[2,4,32,256]{3,2,1,0:T(8,128)} %copy-done), channel_id=1, source_target_pairs={{0,4},{4,0},{8,12},{12,8},{16,20},{20,16},{24,28},{28,24},{1,5},{5... | collective-permute-start | bytes 786440 | tf_op jit(solution)/shard_map/reduce2/ppermute | solution.py:205
  52.6 0.7 collective-permute-start.12
  53.4 0.9 add.60
  54.3 0.0 collective-permute-done.4
  54.3 0.7 collective-permute-start.14
  55.1 2.5 %collective-permute-start.10 = (f32[1,4,32,256]{3,2,1,0:T(8,128)S(1)}, f32[1,4,32,256]{3,2,1,0:T(8,128)S(1)}, u32[]{:S(2)}, u32[]{:S(2)}) collective-permute-start(f32[1,4,32,256]{3,2,1,0:T(8,128)S(1)} %add.60), channel_id=1, source_target_pairs={{0,8},{4,12},{24,16},{28,20},{1,9},{5,13},{25,17},{29,21},{2,10},{... | collective-permute-start | bytes 393224 | tf_op jit(solution)/shard_map/reduce1/ppermute | solution.py:203
  57.5 0.0 collective-permute-done.6
  57.6 1.1 add_add_fusion
  58.7 7.2 %all_gather.21 = f32[128,1024]{1,0:T(8,128)S(1)} all-gather(f32[128,256]{1,0:T(8,128)S(1)} %bitcast.104), channel_id=1, replica_groups=mesh['row'=8,'col'=4] {'col'}, dimensions={1}, use_global_device_ids=true | all-gather | bytes 655360 | tf_op jit(solution)/shard_map/solve0/all_gather | solution.py:120
  65.9 1.7 %collective-permute-start.7 = (f32[2,4,32,256]{3,2,1,0:T(8,128)S(1)}, f32[2,4,32,256]{3,2,1,0:T(8,128)S(1)}, u32[]{:S(2)}, u32[]{:S(2)}) collective-permute-start(f32[2,4,32,256]{3,2,1,0:T(8,128)S(1)} %add.53), channel_id=1, source_target_pairs={{0,8},{4,12},{24,16},{28,20},{1,9},{5,13},{25,17},{29,21},{2,10},{... | collective-permute-start | bytes 786440 | tf_op jit(solution)/shard_map/reduce2/ppermute | solution.py:206
  67.6 1.6 %fusion.5 = f32[128,256]{1,0:T(8,128)S(1)} fusion(f32[128,1024]{1,0:T(8,128)S(1)} %all_gather.21, f32[4,1024,256]{2,1,0:T(8,128)} %param.5), kind=kOutput, calls=%fused_computation.6 | convolution fusion | flops 201326592 | bytes 1703936 | tf_op jit(solution)/shard_map/solve0/dot_general | solution.py:93
  69.3 0.7 collective-permute-start.11
  70.0 7.2 %all_gather.22 = f32[128,1024]{1,0:T(8,128)S(1)} all-gather(f32[128,256]{1,0:T(8,128)S(1)} %fusion.5), channel_id=1, replica_groups=mesh['row'=8,'col'=4] {'col'}, dimensions={1}, use_global_device_ids=true | all-gather | bytes 655360 | tf_op jit(solution)/shard_map/solve0/all_gather | solution.py:120
  77.2 0.7 collective-permute-start.8
  77.9 0.4 bitcast_subtract_fusion.1
  78.3 7.3 %all_gather.23 = f32[128,1024]{1,0:T(8,128)S(1)} all-gather(f32[128,256]{1,0:T(8,128)S(1)} %bitcast_subtract_fusion.1), channel_id=1, replica_groups=mesh['row'=8,'col'=4] {'col'}, dimensions={1}, use_global_device_ids=true | all-gather | bytes 655360 | tf_op jit(solution)/shard_map/solve1/all_gather | solution.py:120
  85.6 0.4 fusion.3
  86.1 0.7 collective-permute-start.13
  86.8 7.3 %all_gather.24 = f32[128,1024]{1,0:T(8,128)S(1)} all-gather(f32[128,256]{1,0:T(8,128)S(1)} %fusion.3), channel_id=1, replica_groups=mesh['row'=8,'col'=4] {'col'}, dimensions={1}, use_global_device_ids=true | all-gather | bytes 655360 | tf_op jit(solution)/shard_map/solve1/all_gather | solution.py:120
  94.2 0.4 fusion.15
  94.6 0.4 fusion.29
  95.1 7.3 %all_gather.25 = f32[128,1024]{1,0:T(8,128)S(1)} all-gather(f32[128,256]{1,0:T(8,128)S(1)} %fusion.29), channel_id=1, replica_groups=mesh['row'=8,'col'=4] {'col'}, dimensions={1}, use_global_device_ids=true | all-gather | bytes 655360 | tf_op jit(solution)/shard_map/solve2/all_gather | solution.py:120
  102.4 0.4 fusion.1
  102.8 7.3 %all_gather.26 = f32[128,1024]{1,0:T(8,128)S(1)} all-gather(f32[128,256]{1,0:T(8,128)S(1)} %fusion.1), channel_id=1, replica_groups=mesh['row'=8,'col'=4] {'col'}, dimensions={1}, use_global_device_ids=true | all-gather | bytes 655360 | tf_op jit(solution)/shard_map/solve2/all_gather | solution.py:120
  110.1 0.4 fusion.17
  110.6 0.4 fusion.10
  111.0 0.4 fusion.31
  111.5 0.7 collective-permute-start.17
  112.2 1.3 %collective-permute-start.18 = (f32[32,256]{1,0:T(8,128)S(1)}, f32[32,256]{1,0:T(8,128)S(1)}, u32[]{:S(2)}, u32[]{:S(2)}) collective-permute-start(f32[32,256]{1,0:T(8,128)S(1)} %get-tuple-element.52), channel_id=1, source_target_pairs={{16,0},{20,4},{17,1},{21,5},{18,2},{22,6},{19,3},{23,7}} | collective-permute-start | bytes 98312 | tf_op jit(solution)/shard_map/out/ppermute | solution.py:252
  113.5 0.7 collective-permute-start.19
  114.2 1.3 %collective-permute-start.15 = (f32[3,32,256]{2,1,0:T(8,128)S(1)}, f32[3,32,256]{2,1,0:T(8,128)S(1)}, u32[]{:S(2)}, u32[]{:S(2)}) collective-permute-start(f32[3,32,256]{2,1,0:T(8,128)S(1)} %get-tuple-element.47), channel_id=1, source_target_pairs={{16,0},{20,4},{17,1},{21,5},{18,2},{22,6},{19,3},{23,7}} | collective-permute-start | bytes 294920 | tf_op jit(solution)/shard_map/out/ppermute | solution.py:253
  115.5 0.7 collective-permute-start.16
  116.2 5.2 %collective-permute-done.18 = f32[32,256]{1,0:T(8,128)S(1)} collective-permute-done((f32[32,256]{1,0:T(8,128)S(1)}, f32[32,256]{1,0:T(8,128)S(1)}, u32[]{:S(2)}, u32[]{:S(2)}) %collective-permute-start.18) | collective-permute-done | bytes 32800 | tf_op jit(solution)/shard_map/out/ppermute | solution.py:252
  121.3 5.4 %all_gather.27 = f32[32,1024]{1,0:T(8,128)S(1)} all-gather(f32[32,256]{1,0:T(8,128)S(1)} %fusion.36), channel_id=1, replica_groups=mesh['row'=8,'col'=4] {'col'}, dimensions={1}, use_global_device_ids=true | all-gather | bytes 163840 | tf_op jit(solution)/shard_map/out/all_gather | solution.py:120
  126.8 1.6 %convolution_bitcast_fusion = f32[1,32,256]{2,1,0:T(8,128)S(1)} fusion(f32[32,1024]{1,0:T(8,128)S(1)} %all_gather.27, f32[4,1024,256]{2,1,0:T(8,128)} %param.5), kind=kOutput, calls=%fused_computation | convolution fusion | flops 50331648 | bytes 1212416 | tf_op jit(solution)/shard_map/out/dot_general | solution.py:93
  128.4 0.7 maximum_bitcast_fusion
  (39 shorter events, 0.3 us)
Async XLA Ops:
  3.2 29.2 %collective-permute-start = (f32[1024,256]{1,0:T(8,128)S(1)}, f32[1024,256]{1,0:T(8,128)S(1)}, u32[]{:S(2)}, u32[]{:S(2)}) collective-permute-start(f32[1024,256]{1,0:T(8,128)S(1)} %get-tuple-element.29), channel_id=1, source_target_pairs={{16,20},{20,16},{24,28},{17,21},{21,17},{25,29},{18,22},{22,18},{2... | collective-permute-start | bytes 3145736 | tf_op jit(solution)/shard_map/near1/ppermute | solution.py:152
  3.9 28.5 %collective-permute-start.1 = (f32[1024,256]{1,0:T(8,128)S(1)}, f32[1024,256]{1,0:T(8,128)S(1)}, u32[]{:S(2)}, u32[]{:S(2)}) collective-permute-start(f32[1024,256]{1,0:T(8,128)S(1)} %get-tuple-element.29), channel_id=1, source_target_pairs={{24,16},{25,17},{26,18},{27,19}} | collective-permute-start | bytes 3145736 | tf_op jit(solution)/shard_map/far/ppermute | solution.py:152
  32.4 9.0 %copy-start = (f32[2,4,32,256]{3,2,1,0:T(8,128)}, f32[2,4,32,256]{3,2,1,0:T(8,128)S(1)}, u32[]{:S(2)}) copy-start(f32[2,4,32,256]{3,2,1,0:T(8,128)S(1)} %get-tuple-element.33) | copy-start | bytes 786436
  32.4 15.9 %copy-start.1 = (f32[1024,256]{1,0:T(8,128)}, f32[1024,256]{1,0:T(8,128)S(1)}, u32[]{:S(2)}) copy-start(f32[1024,256]{1,0:T(8,128)S(1)} %collective-permute-done) | copy-start | bytes 3145732
  32.4 17.2 %copy-start.4 = (f32[1024,256]{1,0:T(8,128)}, f32[1024,256]{1,0:T(8,128)S(1)}, u32[]{:S(2)}) copy-start(f32[1024,256]{1,0:T(8,128)S(1)} %collective-permute-done.1) | copy-start | bytes 3145732
  32.4 6.5 %collective-permute-start.2 = (f32[1,4,32,256]{3,2,1,0:T(8,128)S(1)}, f32[1,4,32,256]{3,2,1,0:T(8,128)S(1)}, u32[]{:S(2)}, u32[]{:S(2)}) collective-permute-start(f32[1,4,32,256]{3,2,1,0:T(8,128)S(1)} %get-tuple-element.30), channel_id=1, source_target_pairs={{0,4},{4,0},{8,12},{12,8},{16,20},{20,16},{24,28},{28,24},{1,5},{5... | collective-permute-start | bytes 393224 | tf_op jit(solution)/shard_map/reduce0/ppermute | solution.py:194
  39.0 13.7 %collective-permute-start.9 = (f32[1,4,32,256]{3,2,1,0:T(8,128)}, f32[1,4,32,256]{3,2,1,0:T(8,128)}, u32[]{:S(2)}, u32[]{:S(2)}) collective-permute-start(f32[1,4,32,256]{3,2,1,0:T(8,128)} %get-tuple-element.37), channel_id=1, source_target_pairs={{0,4},{4,0},{8,12},{12,8},{16,20},{20,16},{24,28},{28,24},{1,5},{5... | collective-permute-start | bytes 393224 | tf_op jit(solution)/shard_map/reduce1/ppermute | solution.py:201
  41.4 12.9 %collective-permute-start.4 = (f32[1,4,32,256]{3,2,1,0:T(8,128)}, f32[1,4,32,256]{3,2,1,0:T(8,128)}, u32[]{:S(2)}, u32[]{:S(2)}) collective-permute-start(f32[1,4,32,256]{3,2,1,0:T(8,128)} %add.54), channel_id=1, source_target_pairs={{0,16},{4,20},{1,17},{5,21},{2,18},{6,22},{3,19},{7,23}} | collective-permute-start | bytes 393224 | tf_op jit(solution)/shard_map/reduce0/ppermute | solution.py:197
  48.3 6.8 %collective-permute-start.5 = (f32[1,4,32,256]{3,2,1,0:T(8,128)}, f32[1,4,32,256]{3,2,1,0:T(8,128)}, u32[]{:S(2)}, u32[]{:S(2)}) collective-permute-start(f32[1,4,32,256]{3,2,1,0:T(8,128)} %add.54), channel_id=1, source_target_pairs={{8,16},{12,20},{9,17},{13,21},{10,18},{14,22},{11,19},{15,23}} | collective-permute-start | bytes 393224 | tf_op jit(solution)/shard_map/reduce0/ppermute | solution.py:197
  49.6 8.0 %collective-permute-start.6 = (f32[1,4,32,256]{3,2,1,0:T(8,128)}, f32[1,4,32,256]{3,2,1,0:T(8,128)}, u32[]{:S(2)}, u32[]{:S(2)}) collective-permute-start(f32[1,4,32,256]{3,2,1,0:T(8,128)} %add.54), channel_id=1, source_target_pairs={{24,16},{28,20},{25,17},{29,21},{26,18},{30,22},{27,19},{31,23}} | collective-permute-start | bytes 393224 | tf_op jit(solution)/shard_map/reduce0/ppermute | solution.py:197
  50.9 27.0 %copy-start.2 = (f32[1024,256]{1,0:T(8,128)S(1)}, f32[1024,256]{1,0:T(8,128)}, u32[]{:S(2)}) copy-start(f32[1024,256]{1,0:T(8,128)} %copy-done.1) | copy-start | bytes 3145732
  50.9 15.0 %collective-permute-start.3 = (f32[2,4,32,256]{3,2,1,0:T(8,128)}, f32[2,4,32,256]{3,2,1,0:T(8,128)S(1)}, u32[]{:S(2)}, u32[]{:S(2)}) collective-permute-start(f32[2,4,32,256]{3,2,1,0:T(8,128)} %copy-done), channel_id=1, source_target_pairs={{0,4},{4,0},{8,12},{12,8},{16,20},{20,16},{24,28},{28,24},{1,5},{5... | collective-permute-start | bytes 786440 | tf_op jit(solution)/shard_map/reduce2/ppermute | solution.py:205
  52.6 41.5 %collective-permute-start.12 = (f32[1024,256]{1,0:T(8,128)S(1)}, f32[1024,256]{1,0:T(8,128)S(1)}, u32[]{:S(2)}, u32[]{:S(2)}) collective-permute-start(f32[1024,256]{1,0:T(8,128)S(1)} %get-tuple-element.42), channel_id=1, source_target_pairs={{16,20},{20,16},{17,21},{21,17},{18,22},{22,18},{19,23},{23,19}} | collective-permute-start | bytes 3145736 | tf_op jit(solution)/shard_map/near2/ppermute | solution.py:152
  54.3 56.7 %collective-permute-start.14 = (f32[1024,256]{1,0:T(8,128)S(1)}, f32[1024,256]{1,0:T(8,128)S(1)}, u32[]{:S(2)}, u32[]{:S(2)}) collective-permute-start(f32[1024,256]{1,0:T(8,128)S(1)} %get-tuple-element.45), channel_id=1, source_target_pairs={{16,20},{17,21},{18,22},{19,23}} | collective-permute-start | bytes 3145736 | tf_op jit(solution)/shard_map/near3/ppermute | solution.py:152
  55.1 14.2 %collective-permute-start.10 = (f32[1,4,32,256]{3,2,1,0:T(8,128)S(1)}, f32[1,4,32,256]{3,2,1,0:T(8,128)S(1)}, u32[]{:S(2)}, u32[]{:S(2)}) collective-permute-start(f32[1,4,32,256]{3,2,1,0:T(8,128)S(1)} %add.60), channel_id=1, source_target_pairs={{0,8},{4,12},{24,16},{28,20},{1,9},{5,13},{25,17},{29,21},{2,10},{... | collective-permute-start | bytes 393224 | tf_op jit(solution)/shard_map/reduce1/ppermute | solution.py:203
  65.9 19.8 %copy-start.3 = (f32[4,1024,256]{2,1,0:T(8,128)S(1)}, f32[4,1024,256]{2,1,0:T(8,128)}, u32[]{:S(2)}) copy-start(f32[4,1024,256]{2,1,0:T(8,128)} %param.5) | copy-start | bytes 12582916
  65.9 11.3 %collective-permute-start.7 = (f32[2,4,32,256]{3,2,1,0:T(8,128)S(1)}, f32[2,4,32,256]{3,2,1,0:T(8,128)S(1)}, u32[]{:S(2)}, u32[]{:S(2)}) collective-permute-start(f32[2,4,32,256]{3,2,1,0:T(8,128)S(1)} %add.53), channel_id=1, source_target_pairs={{0,8},{4,12},{24,16},{28,20},{1,9},{5,13},{25,17},{29,21},{2,10},{... | collective-permute-start | bytes 786440 | tf_op jit(solution)/shard_map/reduce2/ppermute | solution.py:206
  69.3 7.8 %collective-permute-start.11 = (f32[1,4,32,256]{3,2,1,0:T(8,128)S(1)}, f32[1,4,32,256]{3,2,1,0:T(8,128)S(1)}, u32[]{:S(2)}, u32[]{:S(2)}) collective-permute-start(f32[1,4,32,256]{3,2,1,0:T(8,128)S(1)} %add.61), channel_id=1, source_target_pairs={{8,16},{12,20},{9,17},{13,21},{10,18},{14,22},{11,19},{15,23}} | collective-permute-start | bytes 393224 | tf_op jit(solution)/shard_map/reduce1/ppermute | solution.py:203
  77.2 16.9 %collective-permute-start.8 = (f32[2,4,32,256]{3,2,1,0:T(8,128)S(1)}, f32[2,4,32,256]{3,2,1,0:T(8,128)S(1)}, u32[]{:S(2)}, u32[]{:S(2)}) collective-permute-start(f32[2,4,32,256]{3,2,1,0:T(8,128)S(1)} %add.58), channel_id=1, source_target_pairs={{8,16},{12,20},{9,17},{13,21},{10,18},{14,22},{11,19},{15,23}} | collective-permute-start | bytes 786440 | tf_op jit(solution)/shard_map/reduce2/ppermute | solution.py:234
  86.1 24.5 %collective-permute-start.13 = (f32[1024,256]{1,0:T(8,128)S(1)}, f32[1024,256]{1,0:T(8,128)S(1)}, u32[]{:S(2)}, u32[]{:S(2)}) collective-permute-start(f32[1024,256]{1,0:T(8,128)S(1)} %copy-done.2), channel_id=1, source_target_pairs={{28,20},{29,21},{30,22},{31,23}} | collective-permute-start | bytes 3145736 | tf_op jit(solution)/shard_map/across/ppermute | solution.py:152
  94.6 15.9 %copy-start.5 = (f32[1024,256]{1,0:T(8,128)S(1)}, f32[1024,256]{1,0:T(8,128)}, u32[]{:S(2)}) copy-start(f32[1024,256]{1,0:T(8,128)} %copy-done.4) | copy-start | bytes 3145732
  111.5 9.8 %collective-permute-start.17 = (f32[4,32,256]{2,1,0:T(8,128)S(1)}, f32[4,32,256]{2,1,0:T(8,128)S(1)}, u32[]{:S(2)}, u32[]{:S(2)}) collective-permute-start(f32[4,32,256]{2,1,0:T(8,128)S(1)} %pad_maximum_fusion.1), channel_id=1, source_target_pairs={{16,24},{20,28},{17,25},{21,29},{18,26},{22,30},{19,27},{23,31}} | collective-permute-start | bytes 393224 | tf_op jit(solution)/shard_map/out/ppermute | solution.py:255
  112.2 9.1 %collective-permute-start.18 = (f32[32,256]{1,0:T(8,128)S(1)}, f32[32,256]{1,0:T(8,128)S(1)}, u32[]{:S(2)}, u32[]{:S(2)}) collective-permute-start(f32[32,256]{1,0:T(8,128)S(1)} %get-tuple-element.52), channel_id=1, source_target_pairs={{16,0},{20,4},{17,1},{21,5},{18,2},{22,6},{19,3},{23,7}} | collective-permute-start | bytes 98312 | tf_op jit(solution)/shard_map/out/ppermute | solution.py:252
  113.5 7.8 %collective-permute-start.19 = (f32[32,256]{1,0:T(8,128)S(1)}, f32[32,256]{1,0:T(8,128)S(1)}, u32[]{:S(2)}, u32[]{:S(2)}) collective-permute-start(f32[32,256]{1,0:T(8,128)S(1)} %get-tuple-element.53), channel_id=1, source_target_pairs={{16,8},{20,12},{17,9},{21,13},{18,10},{22,14},{19,11},{23,15}} | collective-permute-start | bytes 98312 | tf_op jit(solution)/shard_map/out/ppermute | solution.py:252
  114.2 14.2 %collective-permute-start.15 = (f32[3,32,256]{2,1,0:T(8,128)S(1)}, f32[3,32,256]{2,1,0:T(8,128)S(1)}, u32[]{:S(2)}, u32[]{:S(2)}) collective-permute-start(f32[3,32,256]{2,1,0:T(8,128)S(1)} %get-tuple-element.47), channel_id=1, source_target_pairs={{16,0},{20,4},{17,1},{21,5},{18,2},{22,6},{19,3},{23,7}} | collective-permute-start | bytes 294920 | tf_op jit(solution)/shard_map/out/ppermute | solution.py:253
  115.5 12.9 %collective-permute-start.16 = (f32[3,32,256]{2,1,0:T(8,128)S(1)}, f32[3,32,256]{2,1,0:T(8,128)S(1)}, u32[]{:S(2)}, u32[]{:S(2)}) collective-permute-start(f32[3,32,256]{2,1,0:T(8,128)S(1)} %get-tuple-element.48), channel_id=1, source_target_pairs={{16,8},{20,12},{17,9},{21,13},{18,10},{22,14},{19,11},{23,15}} | collective-permute-start | bytes 294920 | tf_op jit(solution)/shard_map/out/ppermute | solution.py:253
